TPU v7x, 256 devices: a whole 4x4x8 slice. The times are simulated.
256 devices in a mesh: replica: 4 (over y), fsdp: 64 (over z, x, core).
Axes of the slice: x: 4, y: 4, z: 8, core: 2. Of those that a mesh axis runs over, the one named last changes fastest.
Arguments:
- gradients: bfloat16 [4, 48, 1024, 1024], P('replica', None, 'fsdp'), may hold values from -6 to 6
- stat_left: float32 [128, 1024, 1024], P('fsdp', 'replica'), may hold values from -6 to 6
- stat_right: float32 [128, 1024, 1024], P('fsdp', 'replica'), may hold values from -6 to 6
- root_left: bfloat16 [128, 1024, 1024], P('fsdp', 'replica'), as said below
- root_right: bfloat16 [128, 1024, 1024], P('fsdp', None, 'replica'), as said below
- block_owner: int32 [48], replicated, may hold values from 0 to 63, as said below
- block_slot: int32 [48], replicated, may hold values from 0 to 1, as said below
Outputs:
- left_new: float32 [128, 1024, 1024], P('fsdp', 'replica')
- right_new: float32 [128, 1024, 1024], P('fsdp', 'replica')
- update: bfloat16 [48, 1024, 1024], P(None, 'fsdp', 'replica')
Inputs may be any that keep to these rules, and one draw needn't show every extreme that they name: `block_owner`: some owner holds 2 blocks. `block_slot`: no two blocks share both an owner and a slot. `root_left`: given inverse fourth roots. `root_right`: given inverse fourth roots.
All inputs are finite; a program needn't handle non-finite values.
Results may differ from a plain program's by a relative error of at most 0.017.
Values may be sent and summed in bfloat16 or wider, within the bound.
No kernel may reach another device: no remote copies, remote signals or barrier semaphores. Data moves between devices by JAX's collectives and lax.ppermute only.
A program may use at most 64 MiB of HBM per device.

v0:
```python
import jax
import jax.numpy as jnp
from jax import lax
from jax.sharding import PartitionSpec as P


def per_device(gradients, stat_left, stat_right, root_left, root_right, block_owner, block_slot):
    fsdp_count = lax.axis_size("fsdp")
    capacity = stat_left.shape[0]
    blocksize = stat_left.shape[2]
    rows_here = stat_left.shape[1]
    replica_index = lax.axis_index("replica")
    target = block_owner * capacity + block_slot
    terms = gradients[0].astype(jnp.float32)
    summed = lax.psum(terms.astype(jnp.bfloat16), "replica")
    outgoing = (
        jnp.zeros((fsdp_count * capacity,) + summed.shape[1:], jnp.bfloat16).at[target].set(summed)
    )
    owned = lax.all_to_all(outgoing, "fsdp", split_axis=0, concat_axis=1, tiled=True)
    own_rows = lax.dynamic_slice_in_dim(owned, replica_index * rows_here, rows_here, 1)
    own_cols = lax.dynamic_slice_in_dim(owned, replica_index * rows_here, rows_here, 2)
    outer_left = jnp.einsum("cik,cjk->cij", own_rows, owned, preferred_element_type=jnp.float32)
    outer_right = jnp.einsum("cki,ckj->cij", own_cols, owned, preferred_element_type=jnp.float32)
    left_new = stat_left + outer_left / blocksize
    right_new = stat_right + outer_right / blocksize
    half = jnp.einsum("cik,ckj->cij", owned, root_right, preferred_element_type=jnp.float32).astype(
        jnp.bfloat16
    )
    product = jnp.einsum(
        "cik,ckj->cij",
        lax.all_gather(root_left, "replica", axis=1, tiled=True),
        half,
        preferred_element_type=jnp.float32,
    ).astype(jnp.bfloat16)
    returned = lax.all_to_all(product, "fsdp", split_axis=1, concat_axis=0, tiled=True)
    update = returned[target]
    return (left_new, right_new, update)


def solution(mesh):
    placed = (
        P("replica", None, "fsdp", None),
        P("fsdp", "replica", None),
        P("fsdp", "replica", None),
        P("fsdp", "replica", None),
        P("fsdp", None, "replica"),
        P(),
        P(),
    )
    return jax.shard_map(
        per_device,
        mesh=mesh,
        in_specs=placed,
        out_specs=(
            P("fsdp", "replica", None),
            P("fsdp", "replica", None),
            P(None, "fsdp", "replica"),
        ),
        check_vma=False,
    )
```

profile of v0, /device:TPU:1, one launch (start us, length us, event | category | flops | bytes accessed | tf_op | source)
XLA Modules:
  0.0 240.7 jit_solution(3661952491388168538)
XLA Ops:
  7.2 0.0 copy-start
  7.2 0.0 all-reduce.2.cloned.1.call-start
  7.2 0.7 all-reduce.2.cloned.1.call-update
  7.9 0.7 compare_select_fusion
  8.6 61.1 %all-reduce.2.cloned.1.call-done = bf16[48,16,1024]{2,1,0:T(8,128)(2,1)} async-done(((bf16[48,16,1024]{2,1,0:T(8,128)(2,1)}), bf16[48,16,1024]{2,1,0:T(8,128)(2,1)}) %all-reduce.2.cloned.1.call-update) | async-done | bytes 1572880 | tf_op jit(solution)/shard_map/psum | solution.py:15
  69.7 0.0 copy-start.3
  69.7 2.5 %broadcast_in_dim.7 = bf16[128,16,1024]{2,1,0:T(8,128)(2,1)} broadcast(bf16[]{:T(256)} %constant.9.clone.1), dimensions={} | broadcast | bytes 4194306 | tf_op jit(solution)/shard_map/broadcast_in_dim | solution.py:17
  72.2 0.0 copy-done.3
  72.2 6.6 %scatter_fusion = bf16[128,16,1024]{2,1,0:T(8,128)(2,1)} fusion(bf16[128,16,1024]{2,1,0:T(8,128)(2,1)} %broadcast_in_dim.7, s32[48]{0:T(128)S(1)} %compare_select_fusion, bf16[48,16,1024]{2,1,0:T(8,128)(2,1)S(1)} %copy-done.3), kind=kCustom, calls=%fused_computation.1 | custom fusion | bytes 4718784 | tf_op jit(solution)/shard_map/scatter | solution.py:17
  78.8 11.0 %all-to-all-start = ((bf16[128,16,1024]{2,1,0:T(8,128)(2,1)}), bf16[128,16,1024]{2,1,0:T(8,128)(2,1)}, u32[]{:S(2)}, u32[]{:S(2)}) async-start(bf16[128,16,1024]{2,1,0:T(8,128)(2,1)} %scatter_fusion), calls=%async_computation | async-start | bytes 8388608 | tf_op jit(solution)/shard_map/all_to_all | solution.py:19
  89.8 0.0 all-gather.2.cloned.1.call-start
  89.9 0.7 all-gather.2.cloned.1.call-update
  90.6 93.7 %all-to-all-done = bf16[128,16,1024]{2,1,0:T(8,128)(2,1)} async-done(((bf16[128,16,1024]{2,1,0:T(8,128)(2,1)}), bf16[128,16,1024]{2,1,0:T(8,128)(2,1)}, u32[]{:S(2)}, u32[]{:S(2)}) %all-to-all-start) | async-done | bytes 4194336 | tf_op jit(solution)/shard_map/all_to_all | solution.py:19
  184.2 5.0 %copy.15 = bf16[2,64,16,1024]{3,2,1,0:T(8,128)(2,1)} copy(bf16[2,64,16,1024]{3,2,0,1:T(8,128)(2,1)} %bitcast.2) | data formatting | bytes 8388608 | tf_op jit(solution)/shard_map/all_to_all | solution.py:19
  189.2 0.0 all-gather.2.cloned.1.call-done
  189.2 0.0 copy-done
  189.2 5.9 %fusion = bf16[2,1024,256]{1,2,0:T(8,128)(2,1)S(1)} fusion(bf16[2,1024,1024]{2,1,0:T(8,128)(2,1)} %all-gather.2.cloned.1.call-done, bf16[2,1024,1024]{2,1,0:T(8,128)(2,1)} %bitcast.16, bf16[2,1024,256]{2,1,0:T(8,128)(2,1)S(1)} %copy-done), kind=kOutput, calls=%fused_computation.6 | convolution fusion | flops 2148532224 | bytes 10485760 | tf_op jit(solution)/shard_map/cik,ckj->cij/dot_general | solution.py:29
  195.1 2.0 copy.18
  197.1 7.1 %all-to-all-start.1 = ((bf16[2,1024,256]{2,0,1:T(2,128)(2,1)}), bf16[2,1024,256]{2,0,1:T(2,128)(2,1)S(1)}, u32[]{:S(2)}, u32[]{:S(2)}) async-start(bf16[2,1024,256]{2,0,1:T(2,128)(2,1)} %copy.18), calls=%async_computation.1 | async-start | bytes 2097152 | tf_op jit(solution)/shard_map/all_to_all | solution.py:35
  204.3 0.0 copy-start.1
  204.3 0.0 copy-start.2
  204.3 6.0 %multiply_add_fusion = f32[2,256,1024]{2,1,0:T(8,128)} fusion(f32[2,256,1024]{2,1,0:T(8,128)} %param.9, bf16[2,1024,1024]{2,1,0:T(8,128)(2,1)} %bitcast.17, s32[]{:T(128)S(6)} %select_n.9), kind=kOutput, calls=%fused_computation.2 | convolution fusion | flops 1074790400 | bytes 9437188 | tf_op jit(solution)/shard_map/cki,ckj->cij/dot_general | solution.py:23
  210.3 0.0 copy-done.1
  210.3 0.0 copy-done.2
  210.3 2.6 %multiply_add_fusion.1 = f32[2,256,1024]{2,1,0:T(8,128)} fusion(f32[2,256,1024]{2,1,0:T(8,128)S(1)} %copy-done.2, bf16[2,1024,1024]{2,1,0:T(8,128)(2,1)S(1)} %bitcast.18, s32[]{:T(128)S(6)} %select_n.9), kind=kOutput, calls=%fused_computation.3 | convolution fusion | flops 1074790400 | bytes 9437188 | tf_op jit(solution)/shard_map/cik,cjk->cij/dot_general | solution.py:22
  212.9 19.3 %all-to-all-done.1 = bf16[2,1024,256]{2,0,1:T(2,128)(2,1)S(1)} async-done(((bf16[2,1024,256]{2,0,1:T(2,128)(2,1)}), bf16[2,1024,256]{2,0,1:T(2,128)(2,1)S(1)}, u32[]{:S(2)}, u32[]{:S(2)}) %all-to-all-start.1) | async-done | bytes 1048608 | tf_op jit(solution)/shard_map/all_to_all | solution.py:35
  232.3 0.1 copy.19
  232.4 0.1 copy.20
  232.6 1.3 gather_fusion
  (1 shorter events, 0.0 us)
Async XLA Ops:
  7.2 182.1 %copy-start = (bf16[2,1024,256]{2,1,0:T(8,128)(2,1)S(1)}, bf16[2,1024,256]{2,1,0:T(8,128)(2,1)}, u32[]{:S(2)}) copy-start(bf16[2,1024,256]{2,1,0:T(8,128)(2,1)} %param.11) | copy-start | bytes 3145732
  7.2 62.5 %all-reduce.2.cloned.1.call-start = ((), (), s32[]{:S(2)}) async-start(), calls=%async_computation.2 | async-start | bytes 3145728 | tf_op jit(solution)/shard_map/psum | solution.py:15
  69.7 2.5 %copy-start.3 = (bf16[48,16,1024]{2,1,0:T(8,128)(2,1)S(1)}, bf16[48,16,1024]{2,1,0:T(8,128)(2,1)}, u32[]{:S(2)}) copy-start(bf16[48,16,1024]{2,1,0:T(8,128)(2,1)} %all-reduce.2.cloned.1.call-done) | copy-start | bytes 4718596
  78.8 105.4 %all-to-all-start = ((bf16[128,16,1024]{2,1,0:T(8,128)(2,1)}), bf16[128,16,1024]{2,1,0:T(8,128)(2,1)}, u32[]{:S(2)}, u32[]{:S(2)}) async-start(bf16[128,16,1024]{2,1,0:T(8,128)(2,1)} %scatter_fusion), calls=%async_computation | async-start | bytes 8388608 | tf_op jit(solution)/shard_map/all_to_all | solution.py:19
  89.8 99.4 %all-gather.2.cloned.1.call-start = ((), (), s32[]{:S(2)}) async-start(), calls=%async_computation.3 | async-start | bytes 5242880 | tf_op jit(solution)/shard_map/all_gather | solution.py:31
  197.1 35.1 %all-to-all-start.1 = ((bf16[2,1024,256]{2,0,1:T(2,128)(2,1)}), bf16[2,1024,256]{2,0,1:T(2,128)(2,1)S(1)}, u32[]{:S(2)}, u32[]{:S(2)}) async-start(bf16[2,1024,256]{2,0,1:T(2,128)(2,1)} %copy.18), calls=%async_computation.1 | async-start | bytes 2097152 | tf_op jit(solution)/shard_map/all_to_all | solution.py:35
  204.3 6.0 %copy-start.1 = (bf16[2,64,16,1024]{3,2,1,0:T(8,128)(2,1)S(1)}, bf16[2,64,16,1024]{3,2,1,0:T(8,128)(2,1)}, u32[]{:S(2)}) copy-start(bf16[2,64,16,1024]{3,2,1,0:T(8,128)(2,1)} %copy.15) | copy-start | bytes 12582916
  204.3 6.0 %copy-start.2 = (f32[2,256,1024]{2,1,0:T(8,128)S(1)}, f32[2,256,1024]{2,1,0:T(8,128)}, u32[]{:S(2)}) copy-start(f32[2,256,1024]{2,1,0:T(8,128)} %param.8) | copy-start | bytes 6291460
Sparse Core Ops, SparseCore 0:
  10.4 59.2 all-reduce.1
  92.5 50.5 all-gather.1
where the time goes:
time: 241 us
  waiting for transfers between devices  175 us (73%)
  starting transfers between devices  18.2 us (8%)
  local copies, waits for them, and re-layouts  17.8 us (7%)
  matrix products  14.5 us (6%)
  between operations  14.1 us (6%)
    all_to_all x1, waiting for transfers between devices, per_device(): lax.all_to_all(outgoing, 'fsdp', split_axis=0, concat_axis=1, tiled=True)  93.7 us
    psum x1, waiting for transfers between devices, per_device(): summed = lax.psum(terms.astype(jnp.bfloat16), 'replica')  61.1 us
    all_to_all x1, waiting for transfers between devices, per_device(): lax.all_to_all(product, 'fsdp', split_axis=1, concat_axis=0, tiled=True)  19.3 us
    all_to_all x1, starting transfers between devices, per_device(): lax.all_to_all(outgoing, 'fsdp', split_axis=0, concat_axis=1, tiled=True)  11 us
    all_to_all x1, starting transfers between devices, per_device(): lax.all_to_all(product, 'fsdp', split_axis=1, concat_axis=0, tiled=True)  7.14 us
    scatter x1, local copies, waits for them, and re-layouts, per_device(): jnp.zeros((fsdp_count * capacity,) + summed.shape[1:], jnp.bfloat16)  6.62 us
    dot_general x1, matrix products, per_device(): jnp.einsum('cki,ckj->cij', own_cols, owned, preferred_element_type=jnp.fl...  5.97 us
    dot_general x1, matrix products, per_device(): jnp.einsum('cik,ckj->cij', lax.all_gather(root_left, 'replica', axis=1, t...  5.85 us
  transfers between devices with their start and end apart: 4, of which 3 were waited for; matrix products, arithmetic and copies ran while one was open for 6% of the time, Pallas kernels for 0%

commit v1 on v0

v1 whole, which is shorter than its diff:
```python
import functools

import jax
import jax.numpy as jnp
from jax import lax
from jax.experimental import pallas as pl
from jax.experimental.pallas import tpu as pltpu
from jax.sharding import PartitionSpec as P

PLANES = 4
CORES = 2
SLOTS = 2
VMEM_LIMIT = 12 * 1024 * 1024
VMEM_WHOLE = 60 * 1024 * 1024
F32 = jnp.float32
BF16 = jnp.bfloat16
ANY = pl.BlockSpec(memory_space=pl.ANY)
VMEM = pl.BlockSpec(memory_space=pltpu.VMEM)
SMEM = pl.BlockSpec(memory_space=pltpu.SMEM)


def call(body, name, out_shape, in_specs, out_specs, scratch, flops=0, nbytes=0, vmem=VMEM_LIMIT):
    return pl.pallas_call(
        body,
        name=name,
        out_shape=out_shape,
        in_specs=in_specs,
        out_specs=out_specs,
        scratch_shapes=scratch,
        compiler_params=pltpu.CompilerParams(vmem_limit_bytes=vmem),
        cost_estimate=pl.CostEstimate(flops=flops, bytes_accessed=nbytes, transcendentals=0),
    )


def like(shape, dtype=BF16):
    return jax.ShapeDtypeStruct(shape, dtype)


def my_place():
    f = lax.axis_index("fsdp")
    return lax.axis_index("replica"), f // CORES, f % CORES


def by_plane(rank, target, g, sorted_target, order, *outs):
    count = g.shape[0]
    r, _, _ = my_place()

    @pl.loop(0, count, unroll=8)
    def _(b):
        order[rank[b]] = b
        sorted_target[rank[b]] = target[b]

    for k in range(PLANES):
        plane = (r + k) % PLANES
        for j in range(count // PLANES):
            outs[k][j] = g[order[PLANES * j + plane]]


def sum_and_place(sorted_target, _, own, one, two, three, out):
    r, _, _ = my_place()
    half = out.shape[2]
    out[...] = jnp.zeros_like(out)
    for j in range(own.shape[0]):
        chip = sorted_target[PLANES * j + r] // (CORES * SLOTS)
        total = own[j].astype(F32) + one[j].astype(F32) + two[j].astype(F32) + three[j].astype(F32)
        total = total.astype(BF16)
        for h in range(CORES):
            out[CORES * chip + h] = total[:, h * half : (h + 1) * half]


def root_halves(_, left, right, *outs):
    _, _, c = my_place()
    for i, which in enumerate((c, 1 - c)):
        for s in range(SLOTS):
            out = outs[SLOTS * i + s]
            for m in range(4):
                first = pl.multiple_of(which * 512 + 128 * m, 128)
                out[m] = left[s, :, pl.ds(first, 128)]
                first = pl.multiple_of(which * 128, 128)
                out[4 + m] = right[s, 256 * m : 256 * (m + 1), pl.ds(first, 128)]


def roots_by_plane(sorted_target, *rest):
    ins, outs, (table, sems) = rest[:4], rest[4:8], rest[8:]
    r, q, c = my_place()
    for plane in range(PLANES):
        table[plane] = 0

    @pl.loop(0, sorted_target.shape[0], unroll=8)
    def _(i):
        t = sorted_target[i]

        @pl.when(t // (CORES * SLOTS) == q)
        def _():
            table[i % PLANES] = t % (CORES * SLOTS)

    for k in range(PLANES):
        local = table[(r + k) % PLANES]
        place = jnp.where(local // SLOTS == c, 0, SLOTS) + local % SLOTS
        for i in range(2 * SLOTS):
            pl.when(place == i)(pltpu.make_async_copy(ins[i], outs[k], sems.at[k]).start)
    for k in range(PLANES):
        pltpu.make_async_copy(outs[k], outs[k], sems.at[k]).wait()


def collect(*refs):
    roots, (left, right) = refs[:PLANES], refs[PLANES:]
    for k in range(PLANES):
        for m in range(4):
            left[256 * k : 256 * (k + 1), 128 * m : 128 * (m + 1)] = roots[k][m]
            right[256 * m : 256 * (m + 1), 128 * k : 128 * (k + 1)] = roots[k][4 + m]


def together(x, y):
    return pl.pallas_call(
        lambda *_: None,
        name="together",
        out_shape=[like(x.shape), like(y.shape)],
        in_specs=[VMEM] * 2,
        out_specs=[VMEM] * 2,
        input_output_aliases={0: 0, 1: 1},
        compiler_params=pltpu.CompilerParams(vmem_limit_bytes=VMEM_LIMIT),
    )(x, y)


def block_products(s_own, s_far, l_own, l_far, r_cols, out, *rest):
    grams, half = rest[:PLANES], rest[PLANES]
    r, _, c = my_place()
    near = pl.ds(pl.multiple_of(c * 512, 512), 512)
    far = pl.ds(pl.multiple_of((1 - c) * 512, 512), 512)
    for m in range(4):
        rows = slice(256 * m, 256 * (m + 1))
        total = jnp.dot(s_own[rows, :], r_cols[near, :], preferred_element_type=F32)
        total += jnp.dot(s_far[rows, :], r_cols[far, :], preferred_element_type=F32)
        half[rows, :] = total.astype(BF16)
    for k in range(PLANES):
        rows = slice(256 * k, 256 * (k + 1))
        source = (r - k + PLANES) % PLANES
        total = jnp.dot(l_own[rows, :], half[near, :], preferred_element_type=F32)
        total += jnp.dot(l_far[rows, :], half[far, :], preferred_element_type=F32)
        total = total.astype(BF16)
        if len(out.shape) == 3:
            out[pl.ds(16 * source, 16)] = total.reshape(16, 16, 512)
        else:
            for kk in range(PLANES):
                plane = (r - kk + PLANES) % PLANES
                part = total[:, 128 * kk : 128 * (kk + 1)].reshape(16, 16, 128)
                out[plane, pl.ds(16 * source, 16)] = part

    across_rows = (((1,), (1,)), ((), ()))
    across_columns = (((0,), (0,)), ((), ()))
    for k in range(PLANES):
        plane = (r + k) % PLANES
        rows = pl.ds(pl.multiple_of(plane * 256, 256), 256)
        left = lax.dot_general(s_own[rows, :], s_own[near, :], across_rows, preferred_element_type=F32)
        left += lax.dot_general(s_far[rows, :], s_far[near, :], across_rows, preferred_element_type=F32)
        grams[k][0] = (left / 1024).astype(BF16)
        columns = pl.ds(pl.multiple_of((plane % 2) * 256, 256), 256)
        strip = jnp.where(plane // 2 == c, s_own[:, columns], s_far[:, columns])
        right = lax.dot_general(strip, s_own[...], across_columns, preferred_element_type=F32)
        grams[k][1] = (right / 1024).astype(BF16)


def statistics(sorted_target, stat_left, stat_right, *rest):
    own, other, (left_new, right_new), scratch = rest[:4], rest[4:8], rest[8:10], rest[10:]
    table, added, left, right, g_sems, in_sems, out_sems = scratch
    r, q, c = my_place()
    pairs = ((stat_left, left, left_new), (stat_right, right, right_new))
    for s in range(SLOTS):
        for i, (source, here, _) in enumerate(pairs):
            pltpu.make_async_copy(source.at[s], here.at[s], in_sems.at[2 * s + i]).start()
    for s in range(SLOTS):
        table[s] = 0
        table[SLOTS + s] = 0

    @pl.loop(0, sorted_target.shape[0], unroll=8)
    def _(i):
        t = sorted_target[i]

        @pl.when(t // SLOTS == CORES * q + c)
        def _():
            table[t % SLOTS] = i % PLANES
            table[SLOTS + t % SLOTS] = 1

    near = pl.ds(pl.multiple_of(c * 512, 512), 512)
    far = pl.ds(pl.multiple_of((1 - c) * 512, 512), 512)
    for s in range(SLOTS):
        step = (r - table[s] + PLANES) % PLANES
        for k in range(PLANES):

            @pl.when(step == k)
            def _():
                pltpu.make_async_copy(own[k], added.at[s, :, :, near], g_sems.at[s]).start()
                pltpu.make_async_copy(other[k], added.at[s, :, :, far], g_sems.at[s]).start()

    stores = []
    for s in range(SLOTS):
        pltpu.make_async_copy(added.at[s], added.at[s], g_sems.at[s]).wait()
        used = table[SLOTS + s] > 0
        for i, (source, here, out) in enumerate(pairs):
            pltpu.make_async_copy(source.at[s], here.at[s], in_sems.at[2 * s + i]).wait()

            @pl.when(used)
            def _():
                here[s] = here[s] + added[s, i].astype(F32)

            store = pltpu.make_async_copy(here.at[s], out.at[s], out_sems.at[2 * s + i])
            store.start()
            stores.append(store)
    for store in stores:
        store.wait()


def pick(order, sorted_target, received, out):
    for i in range(out.shape[0]):
        chip = sorted_target[i] // (CORES * SLOTS)
        for h in range(CORES):
            out[order[i], :, 128 * h : 128 * (h + 1)] = received[i % PLANES, chip, h]


def per_device(gradients, stat_left, stat_right, root_left, root_right, block_owner, block_slot):
    blocks, rows, width = gradients.shape[1:]
    each = blocks // PLANES
    fsdp_count = lax.axis_size("fsdp")
    target = block_owner * SLOTS + block_slot
    rank = jnp.sum((target[None, :] < target[:, None]).astype(jnp.int32), axis=1)

    def along(x, step):
        return lax.ppermute(x, "replica", [(i, (i + step) % PLANES) for i in range(PLANES)])

    def across(x):
        return lax.ppermute(x, "fsdp", [(i, i ^ 1) for i in range(fsdp_count)])

    sorted_target, order, *terms = call(
        by_plane,
        "by_plane",
        [like((blocks,), jnp.int32)] * 2 + [like((each, rows, width))] * PLANES,
        [SMEM, SMEM, VMEM],
        [SMEM] * 2 + [VMEM] * PLANES,
        [],
        nbytes=3 << 20,
    )(rank, target, gradients[0])
    summands = [terms[0]] + [along(terms[k], k) for k in range(1, PLANES)]
    part = like((8, 256, 128))
    halves = call(
        root_halves,
        "root_halves",
        [part] * 4,
        [SMEM, VMEM, VMEM],
        [VMEM] * 4,
        [],
    )(sorted_target, root_left, root_right)
    halves = [*halves[:2], *(across(x) for x in halves[2:])]
    roots = call(
        roots_by_plane,
        "roots_by_plane",
        [part] * PLANES,
        [SMEM] + [VMEM] * 4,
        [VMEM] * PLANES,
        [pltpu.SMEM((PLANES,), jnp.int32), pltpu.SemaphoreType.DMA((PLANES,))],
    )(sorted_target, *halves)

    outgoing = call(
        sum_and_place,
        "sum_and_place",
        like((fsdp_count, rows, width // CORES)),
        [SMEM, ANY] + [VMEM] * PLANES,
        VMEM,
        [],
        nbytes=3 << 20,
    )(sorted_target, roots[0], *summands)
    roots, _ = lax.optimization_barrier((roots, outgoing))
    arrived = lax.all_to_all(outgoing, "fsdp", split_axis=0, concat_axis=0, tiled=True)

    roots = [roots[0]] + [along(roots[k], k) for k in range(1, PLANES)]
    l_own, r_cols = call(
        collect,
        "collect",
        [like((width, 512))] * 2,
        [VMEM] * PLANES,
        [VMEM] * 2,
        [],
    )(*roots)

    arrived, l_far = together(arrived, across(l_own))
    s_own = arrived.reshape(width, width // CORES)
    update, *grams = call(
        block_products,
        "block_products",
        [like((PLANES, fsdp_count, rows, 128))] + [like((2, 256, 512))] * PLANES,
        [VMEM] * 5,
        [VMEM] * (1 + PLANES),
        [pltpu.VMEM((width, 512), BF16)],
        flops=8 * 1024 * 1024 * 512,
        nbytes=8 << 20,
    )(s_own, across(s_own), l_own, l_far, r_cols)
    update = update.reshape(PLANES * fsdp_count, rows, 128)
    returned = lax.all_to_all(update, ("replica", "fsdp"), split_axis=0, concat_axis=0, tiled=True)
    new = call(
        pick,
        "pick",
        like((blocks, rows, width // PLANES)),
        [SMEM, SMEM, VMEM],
        VMEM,
        [],
        nbytes=2 << 20,
    )(order, sorted_target, returned.reshape(PLANES, fsdp_count // CORES, CORES, rows, 128))

    grams = [grams[0]] + [along(grams[k], k) for k in range(1, PLANES)]
    grams_far = [across(x) for x in grams]
    left_new, right_new = call(
        statistics,
        "statistics",
        [like(stat_left.shape, F32)] * 2,
        [SMEM] + [ANY] * (2 + 2 * PLANES),
        [ANY] * 2,
        [
            pltpu.SMEM((2 * SLOTS,), jnp.int32),
            pltpu.VMEM((SLOTS, 2, 256, width), BF16),
            pltpu.VMEM(stat_left.shape, F32),
            pltpu.VMEM(stat_right.shape, F32),
            pltpu.SemaphoreType.DMA((SLOTS,)),
            pltpu.SemaphoreType.DMA((2 * SLOTS,)),
            pltpu.SemaphoreType.DMA((2 * SLOTS,)),
        ],
        flops=15 * 1000**3,
        nbytes=8 << 20,
        vmem=VMEM_WHOLE,
    )(sorted_target, stat_left, stat_right, *grams, *grams_far)

    return (left_new, right_new, new)


def solution(mesh):
    placed = (
        P("replica", None, "fsdp", None),
        P("fsdp", "replica", None),
        P("fsdp", "replica", None),
        P("fsdp", "replica", None),
        P("fsdp", None, "replica"),
        P(),
        P(),
    )
    return jax.shard_map(
        per_device,
        mesh=mesh,
        in_specs=placed,
        out_specs=(
            P("fsdp", "replica", None),
            P("fsdp", "replica", None),
            P(None, "fsdp", "replica"),
        ),
        check_vma=False,
    )
```

time: 241 us -> 133 us (0.55)
  waiting for transfers between devices: 175 us -> 60.6 us
  starting transfers between devices: 18.2 us -> 46.6 us
  Pallas kernels: 0 us -> 18.5 us
  matrix products: 14.5 us -> 0 us
  between operations: 14.1 us -> 0.78 us
  local copies, waits for them, and re-layouts: 17.8 us -> 5.57 us
    all_to_all x2, waiting for transfers between devices: 113 us -> 5.28 us  [the longest x1 5.27 us: per_device(): lax.all_to_all(update, ('replica', 'fsdp'), split_axis=0, concat_axis=0,...]
    psum x1 -> x0, waiting for transfers between devices: 61.1 us -> none  [per_device(): summed = lax.psum(terms.astype(jnp.bfloat16), 'replica')]
    ppermute x0 -> x17, waiting for transfers between devices: none -> 55.3 us  [the longest x9 50.2 us: along(): lax.ppermute(x, 'replica', [(i, (i + step) % PLANES) for i in range(PLANE...]
    ppermute x0 -> x17, starting transfers between devices: none -> 23.1 us  [the longest x9 12.1 us: along(): lax.ppermute(x, 'replica', [(i, (i + step) % PLANES) for i in range(PLANE...]
    pallas_call x0 -> x9, Pallas kernels: none -> 18.5 us  [the longest x1 5.85 us: per_device(): call(block_products, 'block_products', [like((PLANES, fsdp_count, rows, 1...]
    dot_general x3 -> x0, matrix products: 14.5 us -> none  [the longest x1 5.97 us: per_device(): jnp.einsum('cki,ckj->cij', own_cols, owned, preferred_element_type=jnp.fl...]
    scatter x1 -> x0, local copies, waits for them, and re-layouts: 6.62 us -> none  [per_device(): jnp.zeros((fsdp_count * capacity,) + summed.shape[1:], jnp.bfloat16)]
    unnamed x8 -> x30, local copies, waits for them, and re-layouts: 0.02 us -> 5.57 us
  transfers between devices with their start and end apart: 4 -> 19, of which waited for: 3 -> 11; matrix products, arithmetic and copies ran while one was open for 6% -> 0% of each run, Pallas kernels for 0% -> 5%
where the time goes in v1:
time: 133 us
  waiting for transfers between devices  60.6 us (46%)
  starting transfers between devices  46.6 us (35%)
  Pallas kernels  18.5 us (14%)
  local copies, waits for them, and re-layouts  5.57 us (4%)
    ppermute x9, waiting for transfers between devices, along(): lax.ppermute(x, 'replica', [(i, (i + step) % PLANES) for i in range(PLANE...  50.2 us
    ppermute x9, starting transfers between devices, along(): lax.ppermute(x, 'replica', [(i, (i + step) % PLANES) for i in range(PLANE...  12.1 us
    all_to_all x1, starting transfers between devices, per_device(): lax.all_to_all(outgoing, 'fsdp', split_axis=0, concat_axis=0, tiled=True)  11.9 us
    all_to_all x1, starting transfers between devices, per_device(): lax.all_to_all(update, ('replica', 'fsdp'), split_axis=0, concat_axis=0,...  11.6 us
    ppermute x8, starting transfers between devices, across(): return lax.ppermute(x, 'fsdp', [(i, i ^ 1) for i in range(fsdp_count)])  11 us
    pallas_call x1, Pallas kernels, per_device(): call(block_products, 'block_products', [like((PLANES, fsdp_count, rows, 1...  5.85 us
    unnamed x30, local copies, waits for them, and re-layouts  5.57 us
    pallas_call x1, Pallas kernels, per_device(): call(statistics, 'statistics', [like(stat_left.shape, F32)] * 2, [SMEM] +...  5.34 us
  transfers between devices with their start and end apart: 19, of which 11 were waited for; matrix products, arithmetic and copies ran while one was open for 0% of the time, Pallas kernels for 5%

profile of v1, /device:TPU:1, one launch (start us, length us, event | category | flops | bytes accessed | tf_op | source)
XLA Modules:
  0.0 132.9 jit_solution(18247572645446757818)
XLA Ops:
  1.5 1.4 %copy-done = bf16[1,48,16,1024]{3,2,1,0:T(8,128)(2,1)S(1)} copy-done((bf16[1,48,16,1024]{3,2,1,0:T(8,128)(2,1)S(1)}, bf16[1,48,16,1024]{3,2,1,0:T(8,128)(2,1)}, u32[]{:S(2)}) %copy-start) | copy-done | bytes 1572888
  2.9 1.4 %by_plane.1 = (s32[48]{0:T(128)S(1)}, s32[48]{0:T(128)S(1)}, bf16[12,16,1024]{2,1,0:T(8,128)(2,1)S(1)}, bf16[12,16,1024]{2,1,0:T(8,128)(2,1)S(1)}, bf16[12,16,10...) custom-call(s32[48]{0:T(128)S(1)} %convert_reduce_fusion.rank, s32[48]{0:T(128)S(1)} %multiply_add_fusion.target, ...), custom_call_target="tpu_custom_call" | custom-call | bytes 3145728 | tf_op jit(solution)/shard_map/by_plane/pallas_call | solution.py:234
  4.3 1.2 copy-done.2
  5.5 0.9 root_halves.1
  6.5 3.3 %collective-permute-start = (bf16[8,256,128]{2,1,0:T(8,128)(2,1)S(1)}, bf16[8,256,128]{2,1,0:T(8,128)(2,1)S(1)}, u32[]{:S(2)}, u32[]{:S(2)}) collective-permute-start(bf16[8,256,128]{2,1,0:T(8,128)(2,1)S(1)} %get-tuple-element.35), channel_id=1, source_target_pairs={{0,1},{1,0},{2,3},{3,2},{4,5},{5,4},{6,7},{7,6},{8,9},{9,8},{10,11... | collective-permute-start | bytes 1572872 | tf_op jit(solution)/shard_map/ppermute | solution.py:232
  9.9 2.2 %collective-permute-start.3 = (bf16[12,16,1024]{2,1,0:T(8,128)(2,1)S(1)}, bf16[12,16,1024]{2,1,0:T(8,128)(2,1)S(1)}, u32[]{:S(2)}, u32[]{:S(2)}) collective-permute-start(bf16[12,16,1024]{2,1,0:T(8,128)(2,1)S(1)} %get-tuple-element.40), channel_id=1, source_target_pairs={{0,128},{64,192},{128,0},{192,64},{1,129},{65,193},{129,1},{193,65... | collective-permute-start | bytes 1179656 | tf_op jit(solution)/shard_map/ppermute | solution.py:229
  12.1 1.1 collective-permute-start.4
  13.2 1.3 roots_by_plane.1
  14.5 7.4 %collective-permute-done.2.one = bf16[12,16,1024]{2,1,0:T(8,128)(2,1)S(1)} collective-permute-done((bf16[12,16,1024]{2,1,0:T(8,128)(2,1)S(1)}, bf16[12,16,1024]{2,1,0:T(8,128)(2,1)S(1)}, u32[]{:S(2)}, u32[]{:S(2)}) %collective-permute-start.2) | collective-permute-done | bytes 393248 | tf_op jit(solution)/shard_map/ppermute | solution.py:229
  21.9 7.5 %collective-permute-done.3.two = bf16[12,16,1024]{2,1,0:T(8,128)(2,1)S(1)} collective-permute-done((bf16[12,16,1024]{2,1,0:T(8,128)(2,1)S(1)}, bf16[12,16,1024]{2,1,0:T(8,128)(2,1)S(1)}, u32[]{:S(2)}, u32[]{:S(2)}) %collective-permute-start.3) | collective-permute-done | bytes 393248 | tf_op jit(solution)/shard_map/ppermute | solution.py:229
  30.1 1.8 %sum_and_place.1 = bf16[64,16,512]{2,1,0:T(8,128)(2,1)} custom-call(s32[48]{0:T(128)S(1)} %get-tuple-element.32._.sorted_target, bf16[8,256,128]{2,1,0:T(8,128)(2,1)S(1)} %get-tuple-element.45._.refs_0_, bf16[12,16,1024]{2,1,0:T(8,128)(2,1)S(1)} %get-tuple-element.38.own, bf16[12,16,1024]{2,1,0:T(8,128)(2,1)S(1)} %collective-permute-done.2.one, ...), custom_call_target="tpu_custom_call" | custom-call | bytes 3145728 | tf_op jit(solution)/shard_map/sum_and_place/pallas_call | solution.py:263
  31.9 11.9 %all-to-all-start = ((bf16[64,16,512]{2,1,0:T(8,128)(2,1)}), bf16[64,16,512]{2,1,0:T(8,128)(2,1)S(1)}, u32[]{:S(2)}, u32[]{:S(2)}) async-start(bf16[64,16,512]{2,1,0:T(8,128)(2,1)} %sum_and_place.1), calls=%async_computation | async-start | bytes 2097152 | tf_op jit(solution)/shard_map/all_to_all | solution.py:273
  43.8 0.9 collective-permute-start.5
  44.8 2.1 %collective-permute-start.6 = (bf16[8,256,128]{2,1,0:T(8,128)(2,1)S(1)}, bf16[8,256,128]{2,1,0:T(8,128)(2,1)S(1)}, u32[]{:S(2)}, u32[]{:S(2)}) collective-permute-start(bf16[8,256,128]{2,1,0:T(8,128)(2,1)S(1)} %get-tuple-element.47), channel_id=1, source_target_pairs={{0,128},{64,192},{128,0},{192,64},{1,129},{65,193},{129,1},{193,65... | collective-permute-start | bytes 1572872 | tf_op jit(solution)/shard_map/ppermute | solution.py:229
  46.9 1.4 %collective-permute-start.7 = (bf16[8,256,128]{2,1,0:T(8,128)(2,1)S(1)}, bf16[8,256,128]{2,1,0:T(8,128)(2,1)S(1)}, u32[]{:S(2)}, u32[]{:S(2)}) collective-permute-start(bf16[8,256,128]{2,1,0:T(8,128)(2,1)S(1)} %get-tuple-element.48), channel_id=1, source_target_pairs={{0,192},{64,0},{128,64},{192,128},{1,193},{65,1},{129,65},{193,129... | collective-permute-start | bytes 1572872 | tf_op jit(solution)/shard_map/ppermute | solution.py:229
  48.3 9.9 %collective-permute-done.5.refs_1_ = bf16[8,256,128]{2,1,0:T(8,128)(2,1)S(1)} collective-permute-done((bf16[8,256,128]{2,1,0:T(8,128)(2,1)S(1)}, bf16[8,256,128]{2,1,0:T(8,128)(2,1)S(1)}, u32[]{:S(2)}, u32[]{:S(2)}) %collective-permute-start.5) | collective-permute-done | bytes 524320 | tf_op jit(solution)/shard_map/ppermute | solution.py:229
  58.2 11.5 %collective-permute-done.6.refs_2_ = bf16[8,256,128]{2,1,0:T(8,128)(2,1)S(1)} collective-permute-done((bf16[8,256,128]{2,1,0:T(8,128)(2,1)S(1)}, bf16[8,256,128]{2,1,0:T(8,128)(2,1)S(1)}, u32[]{:S(2)}, u32[]{:S(2)}) %collective-permute-start.6) | collective-permute-done | bytes 524320 | tf_op jit(solution)/shard_map/ppermute | solution.py:229
  70.1 1.0 copy-done.5
  71.1 1.6 %collective-permute-start.8 = (bf16[1024,512]{1,0:T(8,128)(2,1)S(1)}, bf16[1024,512]{1,0:T(8,128)(2,1)S(1)}, u32[]{:S(2)}, u32[]{:S(2)}) collective-permute-start(bf16[1024,512]{1,0:T(8,128)(2,1)S(1)} %get-tuple-element.49.l_own), channel_id=1, source_target_pairs={{0,1},{1,0},{2,3},{3,2},{4,5},{5,4},{6,7},{7,6},{8,9},{9,8},{10,11... | collective-permute-start | bytes 3145736 | tf_op jit(solution)/shard_map/ppermute | solution.py:232
  72.7 2.3 %collective-permute-done.8.__1_ = bf16[1024,512]{1,0:T(8,128)(2,1)S(1)} collective-permute-done((bf16[1024,512]{1,0:T(8,128)(2,1)S(1)}, bf16[1024,512]{1,0:T(8,128)(2,1)S(1)}, u32[]{:S(2)}, u32[]{:S(2)}) %collective-permute-start.8) | collective-permute-done | bytes 1048608 | tf_op jit(solution)/shard_map/ppermute | solution.py:232
  75.3 2.3 %collective-permute-done.9.s_far = bf16[1024,512]{1,0:T(8,128)(2,1)S(1)} collective-permute-done((bf16[1024,512]{1,0:T(8,128)(2,1)S(1)}, bf16[1024,512]{1,0:T(8,128)(2,1)S(1)}, u32[]{:S(2)}, u32[]{:S(2)}) %collective-permute-start.9) | collective-permute-done | bytes 1048608 | tf_op jit(solution)/shard_map/ppermute | solution.py:232
  77.6 5.9 %block_products.1 = (bf16[4,64,16,128]{3,2,1,0:T(8,128)(2,1)}, bf16[2,256,512]{2,1,0:T(8,128)(2,1)S(1)}, bf16[2,256,512]{2,1,0:T(8,128)(2,1)}, bf16[2,256,512]{2,1,0:T(8,128)(2,1)}, bf16[2,256,512]{2,1,0:T(8,128)(2,1)}) custom-call(bf16[1024,512]{1,0:T(8,128)(2,1)S(1)} %bitcast.6, bf16[1024,512]{1,0:T(8,128)(2,1)S(1)} %collective-permute-done.9.s_far, ...), custom_call_target="tpu_custom_call" | custom-call | flops 4294967296 | bytes 8388608 | tf_op jit(solution)/shard_map/block_products/pallas_call | solution.py:287
  84.3 1.4 %collective-permute-start.10 = (bf16[2,256,512]{2,1,0:T(8,128)(2,1)}, bf16[2,256,512]{2,1,0:T(8,128)(2,1)S(1)}, u32[]{:S(2)}, u32[]{:S(2)}) collective-permute-start(bf16[2,256,512]{2,1,0:T(8,128)(2,1)} %get-tuple-element.54), channel_id=1, source_target_pairs={{0,64},{64,128},{128,192},{192,0},{1,65},{65,129},{129,193},{193,1... | collective-permute-start | bytes 1572872 | tf_op jit(solution)/shard_map/ppermute | solution.py:229
  85.7 2.1 %collective-permute-start.11 = (bf16[2,256,512]{2,1,0:T(8,128)(2,1)}, bf16[2,256,512]{2,1,0:T(8,128)(2,1)S(1)}, u32[]{:S(2)}, u32[]{:S(2)}) collective-permute-start(bf16[2,256,512]{2,1,0:T(8,128)(2,1)} %get-tuple-element.55), channel_id=1, source_target_pairs={{0,128},{64,192},{128,0},{192,64},{1,129},{65,193},{129,1},{193,65... | collective-permute-start | bytes 1572872 | tf_op jit(solution)/shard_map/ppermute | solution.py:229
  88.6 11.6 %all-to-all-start.1 = ((bf16[256,16,128]{2,1,0:T(8,128)(2,1)}), bf16[256,16,128]{2,1,0:T(8,128)(2,1)S(1)}, u32[]{:S(2)}, u32[]{:S(2)}) async-start(bf16[256,16,128]{2,1,0:T(8,128)(2,1)} %bitcast.2), calls=%async_computation.1 | async-start | bytes 2097152 | tf_op jit(solution)/shard_map/all_to_all | solution.py:298
  100.3 2.2 %collective-permute-start.13 = (bf16[2,256,512]{2,1,0:T(8,128)(2,1)S(1)}, bf16[2,256,512]{2,1,0:T(8,128)(2,1)S(1)}, u32[]{:S(2)}, u32[]{:S(2)}) collective-permute-start(bf16[2,256,512]{2,1,0:T(8,128)(2,1)S(1)} %copy-done.8), channel_id=1, source_target_pairs={{0,1},{1,0},{2,3},{3,2},{4,5},{5,4},{6,7},{7,6},{8,9},{9,8},{10,11... | collective-permute-start | bytes 1572872 | tf_op jit(solution)/shard_map/ppermute | solution.py:232
  102.6 13.1 %collective-permute-done.11.rest_2_ = bf16[2,256,512]{2,1,0:T(8,128)(2,1)S(1)} collective-permute-done((bf16[2,256,512]{2,1,0:T(8,128)(2,1)}, bf16[2,256,512]{2,1,0:T(8,128)(2,1)S(1)}, u32[]{:S(2)}, u32[]{:S(2)}) %collective-permute-start.11) | collective-permute-done | bytes 524320 | tf_op jit(solution)/shard_map/ppermute | solution.py:229
  115.7 2.3 %collective-permute-start.15 = (bf16[2,256,512]{2,1,0:T(8,128)(2,1)S(1)}, bf16[2,256,512]{2,1,0:T(8,128)(2,1)S(1)}, u32[]{:S(2)}, u32[]{:S(2)}) collective-permute-start(bf16[2,256,512]{2,1,0:T(8,128)(2,1)S(1)} %collective-permute-done.11.rest_2_), channel_id=1, source_target_pairs={{0,1},{1,0},{2,3},{3,2},{4,5},{5,4},{6,7},{7,6},{8,9},{9,8},{10,11... | collective-permute-start | bytes 1572872 | tf_op jit(solution)/shard_map/ppermute | solution.py:232
  118.0 1.0 collective-permute-start.16
  120.7 5.3 %statistics.1 = (f32[2,256,1024]{2,1,0:T(8,128)}, f32[2,256,1024]{2,1,0:T(8,128)}) custom-call(s32[48]{0:T(128)} %copy-done.3, f32[2,256,1024]{2,1,0:T(8,128)} %stat_left.1, f32[2,256,1024]{2,1,0:T(8,128)} %stat_right.1, bf16[2,256,512]{2,1,0:T(8,128)(2,1)} %copy-done.7, bf16[2,256,512]{2,1,0:T(8,128)(2,1)} %copy-done.9, bf16[2,256,512]{2,1,0:T(8,128)(2,1)} %copy-done.10, ...), custom_call_target="tpu_custom_call" | custom-call | flops 15000000512 | bytes 8388608 | tf_op jit(solution)/shard_map/statistics/pallas_call | solution.py:311
  126.1 5.3 %all-to-all-done.1 = bf16[256,16,128]{2,1,0:T(8,128)(2,1)S(1)} async-done(((bf16[256,16,128]{2,1,0:T(8,128)(2,1)}), bf16[256,16,128]{2,1,0:T(8,128)(2,1)S(1)}, u32[]{:S(2)}, u32[]{:S(2)}) %all-to-all-start.1) | async-done | bytes 1048608 | tf_op jit(solution)/shard_map/all_to_all | solution.py:298
  131.3 1.6 %pick.1 = bf16[48,16,256]{2,1,0:T(8,128)(2,1)} custom-call(s32[48]{0:T(128)S(1)} %get-tuple-element.59.order, s32[48]{0:T(128)S(1)} %copy-done.4, bf16[4,32,2,16,128]{4,3,2,1,0:T(8,128)(2,1)S(1)} %bitcast.4), custom_call_target="tpu_custom_call" | custom-call | bytes 2097152 | tf_op jit(solution)/shard_map/pick/pallas_call | solution.py:299
  (47 shorter events, 6.0 us)
Async XLA Ops:
  1.5 1.4 %copy-start = (bf16[1,48,16,1024]{3,2,1,0:T(8,128)(2,1)S(1)}, bf16[1,48,16,1024]{3,2,1,0:T(8,128)(2,1)}, u32[]{:S(2)}) copy-start(bf16[1,48,16,1024]{3,2,1,0:T(8,128)(2,1)} %param.7) | copy-start | bytes 4718596
  2.9 1.4 %copy-start.1 = (bf16[2,256,1024]{2,1,0:T(8,128)(2,1)S(1)}, bf16[2,256,1024]{2,1,0:T(8,128)(2,1)}, u32[]{:S(2)}) copy-start(bf16[2,256,1024]{2,1,0:T(8,128)(2,1)} %left.1) | copy-start | bytes 3145732
  4.3 25.9 %copy-start.3 = (s32[48]{0:T(128)}, s32[48]{0:T(128)S(1)}, u32[]{:S(2)}) copy-start(s32[48]{0:T(128)S(1)} %get-tuple-element.32._.sorted_target) | copy-start | bytes 580
  4.3 1.2 copy-start.2
  6.5 6.7 %collective-permute-start = (bf16[8,256,128]{2,1,0:T(8,128)(2,1)S(1)}, bf16[8,256,128]{2,1,0:T(8,128)(2,1)S(1)}, u32[]{:S(2)}, u32[]{:S(2)}) collective-permute-start(bf16[8,256,128]{2,1,0:T(8,128)(2,1)S(1)} %get-tuple-element.35), channel_id=1, source_target_pairs={{0,1},{1,0},{2,3},{3,2},{4,5},{5,4},{6,7},{7,6},{8,9},{9,8},{10,11... | collective-permute-start | bytes 1572872 | tf_op jit(solution)/shard_map/ppermute | solution.py:232
  9.8 3.4 %collective-permute-start.1 = (bf16[8,256,128]{2,1,0:T(8,128)(2,1)S(1)}, bf16[8,256,128]{2,1,0:T(8,128)(2,1)S(1)}, u32[]{:S(2)}, u32[]{:S(2)}) collective-permute-start(bf16[8,256,128]{2,1,0:T(8,128)(2,1)S(1)} %get-tuple-element.36), channel_id=1, source_target_pairs={{0,1},{1,0},{2,3},{3,2},{4,5},{5,4},{6,7},{7,6},{8,9},{9,8},{10,11... | collective-permute-start | bytes 1572872 | tf_op jit(solution)/shard_map/ppermute | solution.py:232
  9.9 12.0 %collective-permute-start.2 = (bf16[12,16,1024]{2,1,0:T(8,128)(2,1)S(1)}, bf16[12,16,1024]{2,1,0:T(8,128)(2,1)S(1)}, u32[]{:S(2)}, u32[]{:S(2)}) collective-permute-start(bf16[12,16,1024]{2,1,0:T(8,128)(2,1)S(1)} %get-tuple-element.39), channel_id=1, source_target_pairs={{0,64},{64,128},{128,192},{192,0},{1,65},{65,129},{129,193},{193,1... | collective-permute-start | bytes 1179656 | tf_op jit(solution)/shard_map/ppermute | solution.py:229
  9.9 19.5 %collective-permute-start.3 = (bf16[12,16,1024]{2,1,0:T(8,128)(2,1)S(1)}, bf16[12,16,1024]{2,1,0:T(8,128)(2,1)S(1)}, u32[]{:S(2)}, u32[]{:S(2)}) collective-permute-start(bf16[12,16,1024]{2,1,0:T(8,128)(2,1)S(1)} %get-tuple-element.40), channel_id=1, source_target_pairs={{0,128},{64,192},{128,0},{192,64},{1,129},{65,193},{129,1},{193,65... | collective-permute-start | bytes 1179656 | tf_op jit(solution)/shard_map/ppermute | solution.py:229
  12.1 18.1 %collective-permute-start.4 = (bf16[12,16,1024]{2,1,0:T(8,128)(2,1)S(1)}, bf16[12,16,1024]{2,1,0:T(8,128)(2,1)S(1)}, u32[]{:S(2)}, u32[]{:S(2)}) collective-permute-start(bf16[12,16,1024]{2,1,0:T(8,128)(2,1)S(1)} %get-tuple-element.41), channel_id=1, source_target_pairs={{0,192},{64,0},{128,64},{192,128},{1,193},{65,1},{129,65},{193,129... | collective-permute-start | bytes 1179656 | tf_op jit(solution)/shard_map/ppermute | solution.py:229
  31.9 43.0 %all-to-all-start = ((bf16[64,16,512]{2,1,0:T(8,128)(2,1)}), bf16[64,16,512]{2,1,0:T(8,128)(2,1)S(1)}, u32[]{:S(2)}, u32[]{:S(2)}) async-start(bf16[64,16,512]{2,1,0:T(8,128)(2,1)} %sum_and_place.1), calls=%async_computation | async-start | bytes 2097152 | tf_op jit(solution)/shard_map/all_to_all | solution.py:273
  43.8 14.3 %collective-permute-start.5 = (bf16[8,256,128]{2,1,0:T(8,128)(2,1)S(1)}, bf16[8,256,128]{2,1,0:T(8,128)(2,1)S(1)}, u32[]{:S(2)}, u32[]{:S(2)}) collective-permute-start(bf16[8,256,128]{2,1,0:T(8,128)(2,1)S(1)} %get-tuple-element.46), channel_id=1, source_target_pairs={{0,64},{64,128},{128,192},{192,0},{1,65},{65,129},{129,193},{193,1... | collective-permute-start | bytes 1572872 | tf_op jit(solution)/shard_map/ppermute | solution.py:229
  44.8 24.9 %collective-permute-start.6 = (bf16[8,256,128]{2,1,0:T(8,128)(2,1)S(1)}, bf16[8,256,128]{2,1,0:T(8,128)(2,1)S(1)}, u32[]{:S(2)}, u32[]{:S(2)}) collective-permute-start(bf16[8,256,128]{2,1,0:T(8,128)(2,1)S(1)} %get-tuple-element.47), channel_id=1, source_target_pairs={{0,128},{64,192},{128,0},{192,64},{1,129},{65,193},{129,1},{193,65... | collective-permute-start | bytes 1572872 | tf_op jit(solution)/shard_map/ppermute | solution.py:229
  46.9 22.9 %collective-permute-start.7 = (bf16[8,256,128]{2,1,0:T(8,128)(2,1)S(1)}, bf16[8,256,128]{2,1,0:T(8,128)(2,1)S(1)}, u32[]{:S(2)}, u32[]{:S(2)}) collective-permute-start(bf16[8,256,128]{2,1,0:T(8,128)(2,1)S(1)} %get-tuple-element.48), channel_id=1, source_target_pairs={{0,192},{64,0},{128,64},{192,128},{1,193},{65,1},{129,65},{193,129... | collective-permute-start | bytes 1572872 | tf_op jit(solution)/shard_map/ppermute | solution.py:229
  70.1 1.0 copy-start.5
  71.1 3.8 %collective-permute-start.8 = (bf16[1024,512]{1,0:T(8,128)(2,1)S(1)}, bf16[1024,512]{1,0:T(8,128)(2,1)S(1)}, u32[]{:S(2)}, u32[]{:S(2)}) collective-permute-start(bf16[1024,512]{1,0:T(8,128)(2,1)S(1)} %get-tuple-element.49.l_own), channel_id=1, source_target_pairs={{0,1},{1,0},{2,3},{3,2},{4,5},{5,4},{6,7},{7,6},{8,9},{9,8},{10,11... | collective-permute-start | bytes 3145736 | tf_op jit(solution)/shard_map/ppermute | solution.py:232
  74.9 2.7 %copy-start.6 = (bf16[1024,512]{1,0:T(8,128)(2,1)S(1)}, bf16[1024,512]{1,0:T(8,128)(2,1)}, u32[]{:S(2)}) copy-start(bf16[1024,512]{1,0:T(8,128)(2,1)} %copy-done.5) | copy-start | bytes 3145732
  74.9 2.7 %collective-permute-start.9 = (bf16[1024,512]{1,0:T(8,128)(2,1)S(1)}, bf16[1024,512]{1,0:T(8,128)(2,1)S(1)}, u32[]{:S(2)}, u32[]{:S(2)}) collective-permute-start(bf16[1024,512]{1,0:T(8,128)(2,1)S(1)} %bitcast.5), channel_id=1, source_target_pairs={{0,1},{1,0},{2,3},{3,2},{4,5},{5,4},{6,7},{7,6},{8,9},{9,8},{10,11... | collective-permute-start | bytes 3145736 | tf_op jit(solution)/shard_map/ppermute | solution.py:232
  84.3 16.0 %copy-start.8 = (bf16[2,256,512]{2,1,0:T(8,128)(2,1)S(1)}, bf16[2,256,512]{2,1,0:T(8,128)(2,1)}, u32[]{:S(2)}) copy-start(bf16[2,256,512]{2,1,0:T(8,128)(2,1)} %copy-done.7) | copy-start | bytes 1572868
  84.3 18.2 %collective-permute-start.10 = (bf16[2,256,512]{2,1,0:T(8,128)(2,1)}, bf16[2,256,512]{2,1,0:T(8,128)(2,1)S(1)}, u32[]{:S(2)}, u32[]{:S(2)}) collective-permute-start(bf16[2,256,512]{2,1,0:T(8,128)(2,1)} %get-tuple-element.54), channel_id=1, source_target_pairs={{0,64},{64,128},{128,192},{192,0},{1,65},{65,129},{129,193},{193,1... | collective-permute-start | bytes 1572872 | tf_op jit(solution)/shard_map/ppermute | solution.py:229
  85.7 30.0 %collective-permute-start.11 = (bf16[2,256,512]{2,1,0:T(8,128)(2,1)}, bf16[2,256,512]{2,1,0:T(8,128)(2,1)S(1)}, u32[]{:S(2)}, u32[]{:S(2)}) collective-permute-start(bf16[2,256,512]{2,1,0:T(8,128)(2,1)} %get-tuple-element.55), channel_id=1, source_target_pairs={{0,128},{64,192},{128,0},{192,64},{1,129},{65,193},{129,1},{193,65... | collective-permute-start | bytes 1572872 | tf_op jit(solution)/shard_map/ppermute | solution.py:229
  87.8 30.2 %collective-permute-start.12 = (bf16[2,256,512]{2,1,0:T(8,128)(2,1)}, bf16[2,256,512]{2,1,0:T(8,128)(2,1)S(1)}, u32[]{:S(2)}, u32[]{:S(2)}) collective-permute-start(bf16[2,256,512]{2,1,0:T(8,128)(2,1)} %get-tuple-element.56), channel_id=1, source_target_pairs={{0,192},{64,0},{128,64},{192,128},{1,193},{65,1},{129,65},{193,129... | collective-permute-start | bytes 1572872 | tf_op jit(solution)/shard_map/ppermute | solution.py:229
  88.6 42.7 %all-to-all-start.1 = ((bf16[256,16,128]{2,1,0:T(8,128)(2,1)}), bf16[256,16,128]{2,1,0:T(8,128)(2,1)S(1)}, u32[]{:S(2)}, u32[]{:S(2)}) async-start(bf16[256,16,128]{2,1,0:T(8,128)(2,1)} %bitcast.2), calls=%async_computation.1 | async-start | bytes 2097152 | tf_op jit(solution)/shard_map/all_to_all | solution.py:298
  100.2 31.1 %copy-start.4 = (s32[48]{0:T(128)S(1)}, s32[48]{0:T(128)}, u32[]{:S(2)}) copy-start(s32[48]{0:T(128)} %copy-done.3) | copy-start | bytes 580
  100.3 18.8 %collective-permute-start.13 = (bf16[2,256,512]{2,1,0:T(8,128)(2,1)S(1)}, bf16[2,256,512]{2,1,0:T(8,128)(2,1)S(1)}, u32[]{:S(2)}, u32[]{:S(2)}) collective-permute-start(bf16[2,256,512]{2,1,0:T(8,128)(2,1)S(1)} %copy-done.8), channel_id=1, source_target_pairs={{0,1},{1,0},{2,3},{3,2},{4,5},{5,4},{6,7},{7,6},{8,9},{9,8},{10,11... | collective-permute-start | bytes 1572872 | tf_op jit(solution)/shard_map/ppermute | solution.py:232
  102.5 18.2 %copy-start.9 = (bf16[2,256,512]{2,1,0:T(8,128)(2,1)}, bf16[2,256,512]{2,1,0:T(8,128)(2,1)S(1)}, u32[]{:S(2)}) copy-start(bf16[2,256,512]{2,1,0:T(8,128)(2,1)S(1)} %collective-permute-done.10.rest_1_) | copy-start | bytes 1572868
  102.5 16.5 %collective-permute-start.14 = (bf16[2,256,512]{2,1,0:T(8,128)(2,1)S(1)}, bf16[2,256,512]{2,1,0:T(8,128)(2,1)S(1)}, u32[]{:S(2)}, u32[]{:S(2)}) collective-permute-start(bf16[2,256,512]{2,1,0:T(8,128)(2,1)S(1)} %collective-permute-done.10.rest_1_), channel_id=1, source_target_pairs={{0,1},{1,0},{2,3},{3,2},{4,5},{5,4},{6,7},{7,6},{8,9},{9,8},{10,11... | collective-permute-start | bytes 1572872 | tf_op jit(solution)/shard_map/ppermute | solution.py:232
  115.7 5.0 %copy-start.10 = (bf16[2,256,512]{2,1,0:T(8,128)(2,1)}, bf16[2,256,512]{2,1,0:T(8,128)(2,1)S(1)}, u32[]{:S(2)}) copy-start(bf16[2,256,512]{2,1,0:T(8,128)(2,1)S(1)} %collective-permute-done.11.rest_2_) | copy-start | bytes 1572868
  115.7 3.8 %collective-permute-start.15 = (bf16[2,256,512]{2,1,0:T(8,128)(2,1)S(1)}, bf16[2,256,512]{2,1,0:T(8,128)(2,1)S(1)}, u32[]{:S(2)}, u32[]{:S(2)}) collective-permute-start(bf16[2,256,512]{2,1,0:T(8,128)(2,1)S(1)} %collective-permute-done.11.rest_2_), channel_id=1, source_target_pairs={{0,1},{1,0},{2,3},{3,2},{4,5},{5,4},{6,7},{7,6},{8,9},{9,8},{10,11... | collective-permute-start | bytes 1572872 | tf_op jit(solution)/shard_map/ppermute | solution.py:232
  118.0 2.7 %copy-start.11 = (bf16[2,256,512]{2,1,0:T(8,128)(2,1)}, bf16[2,256,512]{2,1,0:T(8,128)(2,1)S(1)}, u32[]{:S(2)}) copy-start(bf16[2,256,512]{2,1,0:T(8,128)(2,1)S(1)} %collective-permute-done.12.rest_3_) | copy-start | bytes 1572868
  118.0 2.7 %collective-permute-start.16 = (bf16[2,256,512]{2,1,0:T(8,128)(2,1)S(1)}, bf16[2,256,512]{2,1,0:T(8,128)(2,1)}, u32[]{:S(2)}, u32[]{:S(2)}) collective-permute-start(bf16[2,256,512]{2,1,0:T(8,128)(2,1)S(1)} %collective-permute-done.12.rest_3_), channel_id=1, source_target_pairs={{0,1},{1,0},{2,3},{3,2},{4,5},{5,4},{6,7},{7,6},{8,9},{9,8},{10,11... | collective-permute-start | bytes 1572872 | tf_op jit(solution)/shard_map/ppermute | solution.py:232
  119.0 1.7 %copy-start.12 = (bf16[2,256,512]{2,1,0:T(8,128)(2,1)}, bf16[2,256,512]{2,1,0:T(8,128)(2,1)S(1)}, u32[]{:S(2)}) copy-start(bf16[2,256,512]{2,1,0:T(8,128)(2,1)S(1)} %collective-permute-done.13.rest_4_) | copy-start | bytes 1572868
  119.0 0.8 copy-start.13
  (2 other events, 1.6 us)

commit v2 on v1

--- a/solution.py
+++ b/solution.py
@@ -12,6 +12,9 @@
 SLOTS = 2
 VMEM_LIMIT = 12 * 1024 * 1024
 VMEM_WHOLE = 60 * 1024 * 1024
+SUM_HINT = 20 * 1000**3
+ROOT_HINT = 20 * 1000**3
+GRAM_HINT = 20 * 1000**3
 F32 = jnp.float32
 BF16 = jnp.bfloat16
 ANY = pl.BlockSpec(memory_space=pl.ANY)
@@ -68,8 +71,30 @@
             out[CORES * chip + h] = total[:, h * half : (h + 1) * half]
 
 
-def root_halves(_, left, right, *outs):
-    _, _, c = my_place()
+def root_halves(sorted_target, left, right, *outs):
+    *outs, table, slots = outs
+    r, q, c = my_place()
+    for i in range(8):
+        table[i] = 0
+    for plane in range(PLANES):
+        slots[plane] = SLOTS * c
+
+    @pl.loop(0, sorted_target.shape[0], unroll=8)
+    def _(i):
+        t = sorted_target[i]
+
+        @pl.when(t // (CORES * SLOTS) == q)
+        def _():
+            slots[i % PLANES] = t % (CORES * SLOTS)
+
+        @pl.when(t // SLOTS == CORES * q + c)
+        def _():
+            table[4 + t % SLOTS] = i % PLANES
+            table[6 + t % SLOTS] = 1
+
+    for k in range(PLANES):
+        local = slots[(r + k) % PLANES]
+        table[k] = jnp.where(local // SLOTS == c, 0, SLOTS) + local % SLOTS
     for i, which in enumerate((c, 1 - c)):
         for s in range(SLOTS):
             out = outs[SLOTS * i + s]
@@ -80,27 +105,14 @@
                 out[4 + m] = right[s, 256 * m : 256 * (m + 1), pl.ds(first, 128)]
 
 
-def roots_by_plane(sorted_target, *rest):
-    ins, outs, (table, sems) = rest[:4], rest[4:8], rest[8:]
-    r, q, c = my_place()
-    for plane in range(PLANES):
-        table[plane] = 0
-
-    @pl.loop(0, sorted_target.shape[0], unroll=8)
-    def _(i):
-        t = sorted_target[i]
-
-        @pl.when(t // (CORES * SLOTS) == q)
-        def _():
-            table[i % PLANES] = t % (CORES * SLOTS)
-
-    for k in range(PLANES):
-        local = table[(r + k) % PLANES]
-        place = jnp.where(local // SLOTS == c, 0, SLOTS) + local % SLOTS
+def roots_by_plane(table, *refs):
+    ins, outs = refs[:4], refs[4:]
+    for k in (2, 1, 3, 0):
         for i in range(2 * SLOTS):
-            pl.when(place == i)(pltpu.make_async_copy(ins[i], outs[k], sems.at[k]).start)
-    for k in range(PLANES):
-        pltpu.make_async_copy(outs[k], outs[k], sems.at[k]).wait()
+
+            @pl.when(table[k] == i)
+            def _():
+                outs[k][...] = ins[i][...]
 
 
 def collect(*refs):
@@ -109,6 +121,19 @@
         for m in range(4):
             left[256 * k : 256 * (k + 1), 128 * m : 128 * (m + 1)] = roots[k][m]
             right[256 * m : 256 * (m + 1), 128 * k : 128 * (k + 1)] = roots[k][4 + m]
+
+
+def settle(x, flops):
+    return pl.pallas_call(
+        lambda *_: None,
+        name="settle",
+        out_shape=like(x.shape),
+        in_specs=[VMEM],
+        out_specs=VMEM,
+        input_output_aliases={0: 0},
+        compiler_params=pltpu.CompilerParams(vmem_limit_bytes=VMEM_LIMIT),
+        cost_estimate=pl.CostEstimate(flops=flops, bytes_accessed=0, transcendentals=0),
+    )(x)
 
 
 def together(x, y):
@@ -123,8 +148,7 @@
     )(x, y)
 
 
-def block_products(s_own, s_far, l_own, l_far, r_cols, out, *rest):
-    grams, half = rest[:PLANES], rest[PLANES]
+def update_block(s_own, s_far, l_own, l_far, r_cols, out, half):
     r, _, c = my_place()
     near = pl.ds(pl.multiple_of(c * 512, 512), 512)
     far = pl.ds(pl.multiple_of((1 - c) * 512, 512), 512)
@@ -147,6 +171,10 @@
                 part = total[:, 128 * kk : 128 * (kk + 1)].reshape(16, 16, 128)
                 out[plane, pl.ds(16 * source, 16)] = part
 
+
+def gram(s_own, s_far, *grams):
+    r, _, c = my_place()
+    near = pl.ds(pl.multiple_of(c * 512, 512), 512)
     across_rows = (((1,), (1,)), ((), ()))
     across_columns = (((0,), (0,)), ((), ()))
     for k in range(PLANES):
@@ -161,31 +189,17 @@
         grams[k][1] = (right / 1024).astype(BF16)
 
 
-def statistics(sorted_target, stat_left, stat_right, *rest):
+def statistics(table, stat_left, stat_right, *rest):
     own, other, (left_new, right_new), scratch = rest[:4], rest[4:8], rest[8:10], rest[10:]
-    table, added, left, right, g_sems, in_sems, out_sems = scratch
-    r, q, c = my_place()
+    added, left, right, g_sems, in_sems, out_sems = scratch
+    r, _, c = my_place()
     pairs = ((stat_left, left, left_new), (stat_right, right, right_new))
+    near = pl.ds(pl.multiple_of(c * 512, 512), 512)
+    far = pl.ds(pl.multiple_of((1 - c) * 512, 512), 512)
     for s in range(SLOTS):
         for i, (source, here, _) in enumerate(pairs):
             pltpu.make_async_copy(source.at[s], here.at[s], in_sems.at[2 * s + i]).start()
-    for s in range(SLOTS):
-        table[s] = 0
-        table[SLOTS + s] = 0
-
-    @pl.loop(0, sorted_target.shape[0], unroll=8)
-    def _(i):
-        t = sorted_target[i]
-
-        @pl.when(t // SLOTS == CORES * q + c)
-        def _():
-            table[t % SLOTS] = i % PLANES
-            table[SLOTS + t % SLOTS] = 1
-
-    near = pl.ds(pl.multiple_of(c * 512, 512), 512)
-    far = pl.ds(pl.multiple_of((1 - c) * 512, 512), 512)
-    for s in range(SLOTS):
-        step = (r - table[s] + PLANES) % PLANES
+        step = (r - table[4 + s] + PLANES) % PLANES
         for k in range(PLANES):
 
             @pl.when(step == k)
@@ -196,7 +210,7 @@
     stores = []
     for s in range(SLOTS):
         pltpu.make_async_copy(added.at[s], added.at[s], g_sems.at[s]).wait()
-        used = table[SLOTS + s] > 0
+        used = table[6 + s] > 0
         for i, (source, here, out) in enumerate(pairs):
             pltpu.make_async_copy(source.at[s], here.at[s], in_sems.at[2 * s + i]).wait()
 
@@ -240,15 +254,15 @@
         [],
         nbytes=3 << 20,
     )(rank, target, gradients[0])
-    summands = [terms[0]] + [along(terms[k], k) for k in range(1, PLANES)]
+    summands = [terms[0]] + [settle(along(terms[k], k), SUM_HINT) for k in (1, 3, 2)]
     part = like((8, 256, 128))
-    halves = call(
+    *halves, table = call(
         root_halves,
         "root_halves",
-        [part] * 4,
+        [part] * 4 + [like((8,), jnp.int32)],
         [SMEM, VMEM, VMEM],
-        [VMEM] * 4,
-        [],
+        [VMEM] * 4 + [SMEM],
+        [pltpu.SMEM((PLANES,), jnp.int32)],
     )(sorted_target, root_left, root_right)
     halves = [*halves[:2], *(across(x) for x in halves[2:])]
     roots = call(
@@ -257,8 +271,8 @@
         [part] * PLANES,
         [SMEM] + [VMEM] * 4,
         [VMEM] * PLANES,
-        [pltpu.SMEM((PLANES,), jnp.int32), pltpu.SemaphoreType.DMA((PLANES,))],
-    )(sorted_target, *halves)
+        [],
+    )(table, *halves)
 
     outgoing = call(
         sum_and_place,
@@ -270,9 +284,10 @@
         nbytes=3 << 20,
     )(sorted_target, roots[0], *summands)
     roots, _ = lax.optimization_barrier((roots, outgoing))
+    first = settle(along(roots[2], 2), ROOT_HINT)
     arrived = lax.all_to_all(outgoing, "fsdp", split_axis=0, concat_axis=0, tiled=True)
 
-    roots = [roots[0]] + [along(roots[k], k) for k in range(1, PLANES)]
+    roots = [roots[0], along(roots[1], 1), first, along(roots[3], 3)]
     l_own, r_cols = call(
         collect,
         "collect",
@@ -284,16 +299,27 @@
 
     arrived, l_far = together(arrived, across(l_own))
     s_own = arrived.reshape(width, width // CORES)
-    update, *grams = call(
-        block_products,
-        "block_products",
-        [like((PLANES, fsdp_count, rows, 128))] + [like((2, 256, 512))] * PLANES,
+    s_far = across(s_own)
+    grams = call(
+        gram,
+        "gram",
+        [like((2, 256, 512))] * PLANES,
+        [VMEM] * 2,
+        [VMEM] * PLANES,
+        [],
+        flops=4 * 1024 * 1024 * 512,
+        nbytes=4 << 20,
+    )(s_own, s_far)
+    update = call(
+        update_block,
+        "update_block",
+        like((PLANES, fsdp_count, rows, 128)),
         [VMEM] * 5,
-        [VMEM] * (1 + PLANES),
+        VMEM,
         [pltpu.VMEM((width, 512), BF16)],
-        flops=8 * 1024 * 1024 * 512,
-        nbytes=8 << 20,
-    )(s_own, across(s_own), l_own, l_far, r_cols)
+        flops=4 * 1024 * 1024 * 512,
+        nbytes=6 << 20,
+    )(s_own, s_far, l_own, l_far, r_cols)
     update = update.reshape(PLANES * fsdp_count, rows, 128)
     returned = lax.all_to_all(update, ("replica", "fsdp"), split_axis=0, concat_axis=0, tiled=True)
     new = call(
@@ -315,7 +341,6 @@
         [SMEM] + [ANY] * (2 + 2 * PLANES),
         [ANY] * 2,
         [
-            pltpu.SMEM((2 * SLOTS,), jnp.int32),
             pltpu.VMEM((SLOTS, 2, 256, width), BF16),
             pltpu.VMEM(stat_left.shape, F32),
             pltpu.VMEM(stat_right.shape, F32),
@@ -326,7 +351,7 @@
         flops=15 * 1000**3,
         nbytes=8 << 20,
         vmem=VMEM_WHOLE,
-    )(sorted_target, stat_left, stat_right, *grams, *grams_far)
+    )(table, stat_left, stat_right, *grams, *grams_far)
 
     return (left_new, right_new, new)
 

time: 133 us -> 126 us (0.947)
  waiting for transfers between devices: 60.6 us -> 55.3 us
  starting transfers between devices: 46.6 us -> 43.1 us
  Pallas kernels: 18.5 us -> 21.3 us
    ppermute x9, waiting for transfers between devices: 50.2 us -> 38.5 us  [along(): lax.ppermute(x, 'replica', [(i, (i + step) % PLANES) for i in range(PLANE...]
    all_to_all x1, waiting for transfers between devices: 0.01 us -> 8.27 us  [per_device(): lax.all_to_all(outgoing, 'fsdp', split_axis=0, concat_axis=0, tiled=True)]
    all_to_all x1, starting transfers between devices: 11.6 us -> 6.96 us  [per_device(): lax.all_to_all(update, ('replica', 'fsdp'), split_axis=0, concat_axis=0,...]
    all_to_all x1, waiting for transfers between devices: 5.27 us -> 1.57 us  [per_device(): lax.all_to_all(update, ('replica', 'fsdp'), split_axis=0, concat_axis=0,...]
    pallas_call x2 -> x7, Pallas kernels: 6.78 us -> 8.92 us  [the longest x1 3.45 us: per_device(): call(update_block, 'update_block', like((PLANES, fsdp_count, rows, 128)),...]
    ppermute x8, waiting for transfers between devices: 5.09 us -> 6.96 us  [across(): return lax.ppermute(x, 'fsdp', [(i, i ^ 1) for i in range(fsdp_count)])]
    all_to_all x1, starting transfers between devices: 11.9 us -> 13.6 us  [per_device(): lax.all_to_all(outgoing, 'fsdp', split_axis=0, concat_axis=0, tiled=True)]
    ppermute x8, starting transfers between devices: 11 us -> 9.57 us  [across(): return lax.ppermute(x, 'fsdp', [(i, i ^ 1) for i in range(fsdp_count)])]
  transfers between devices with their start and end apart: 19 -> 19, of which waited for: 11 -> 10; matrix products, arithmetic and copies ran while one was open for 0% -> 0% of each run, Pallas kernels for 5% -> 9%
where the time goes in v2:
time: 126 us
  waiting for transfers between devices  55.3 us (44%)
  starting transfers between devices  43.1 us (34%)
  Pallas kernels  21.3 us (17%)
  local copies, waits for them, and re-layouts  4.49 us (4%)
    ppermute x9, waiting for transfers between devices, along(): lax.ppermute(x, 'replica', [(i, (i + step) % PLANES) for i in range(PLANE...  38.5 us
    all_to_all x1, starting transfers between devices, per_device(): lax.all_to_all(outgoing, 'fsdp', split_axis=0, concat_axis=0, tiled=True)  13.6 us
    ppermute x9, starting transfers between devices, along(): lax.ppermute(x, 'replica', [(i, (i + step) % PLANES) for i in range(PLANE...  13 us
    ppermute x8, starting transfers between devices, across(): return lax.ppermute(x, 'fsdp', [(i, i ^ 1) for i in range(fsdp_count)])  9.57 us
    all_to_all x1, waiting for transfers between devices, per_device(): lax.all_to_all(outgoing, 'fsdp', split_axis=0, concat_axis=0, tiled=True)  8.27 us
    ppermute x8, waiting for transfers between devices, across(): return lax.ppermute(x, 'fsdp', [(i, i ^ 1) for i in range(fsdp_count)])  6.96 us
    all_to_all x1, starting transfers between devices, per_device(): lax.all_to_all(update, ('replica', 'fsdp'), split_axis=0, concat_axis=0,...  6.96 us
    pallas_call x1, Pallas kernels, per_device(): call(statistics, 'statistics', [like(stat_left.shape, F32)] * 2, [SMEM] +...  5.7 us
  transfers between devices with their start and end apart: 19, of which 10 were waited for; matrix products, arithmetic and copies ran while one was open for 0% of the time, Pallas kernels for 9%

profile of v2, /device:TPU:1, one launch (start us, length us, event | category | flops | bytes accessed | tf_op | source)
XLA Modules:
  0.0 125.7 jit_solution(16508003868732052887)
XLA Ops:
  1.5 1.4 %copy-done = bf16[1,48,16,1024]{3,2,1,0:T(8,128)(2,1)S(1)} copy-done((bf16[1,48,16,1024]{3,2,1,0:T(8,128)(2,1)S(1)}, bf16[1,48,16,1024]{3,2,1,0:T(8,128)(2,1)}, u32[]{:S(2)}) %copy-start) | copy-done | bytes 1572888
  2.9 1.4 %by_plane.1 = (s32[48]{0:T(128)S(1)}, s32[48]{0:T(128)S(1)}, bf16[12,16,1024]{2,1,0:T(8,128)(2,1)S(1)}, bf16[12,16,1024]{2,1,0:T(8,128)(2,1)S(1)}, bf16[12,16,10...) custom-call(s32[48]{0:T(128)S(1)} %convert_reduce_fusion.rank, s32[48]{0:T(128)S(1)} %multiply_add_fusion.target, ...), custom_call_target="tpu_custom_call" | custom-call | bytes 3145728 | tf_op jit(solution)/shard_map/by_plane/pallas_call | solution.py:248
  4.3 2.2 %collective-permute-start.2 = (bf16[12,16,1024]{2,1,0:T(8,128)(2,1)S(1)}, bf16[12,16,1024]{2,1,0:T(8,128)(2,1)S(1)}, u32[]{:S(2)}, u32[]{:S(2)}) collective-permute-start(bf16[12,16,1024]{2,1,0:T(8,128)(2,1)S(1)} %get-tuple-element.40), channel_id=1, source_target_pairs={{0,64},{64,128},{128,192},{192,0},{1,65},{65,129},{129,193},{193,1... | collective-permute-start | bytes 1179656 | tf_op jit(solution)/shard_map/ppermute | solution.py:243
  6.5 1.5 %collective-permute-start.3 = (bf16[12,16,1024]{2,1,0:T(8,128)(2,1)S(1)}, bf16[12,16,1024]{2,1,0:T(8,128)(2,1)S(1)}, u32[]{:S(2)}, u32[]{:S(2)}) collective-permute-start(bf16[12,16,1024]{2,1,0:T(8,128)(2,1)S(1)} %get-tuple-element.41), channel_id=1, source_target_pairs={{0,192},{64,0},{128,64},{192,128},{1,193},{65,1},{129,65},{193,129... | collective-permute-start | bytes 1179656 | tf_op jit(solution)/shard_map/ppermute | solution.py:243
  8.0 1.6 %collective-permute-start.4 = (bf16[12,16,1024]{2,1,0:T(8,128)(2,1)S(1)}, bf16[12,16,1024]{2,1,0:T(8,128)(2,1)S(1)}, u32[]{:S(2)}, u32[]{:S(2)}) collective-permute-start(bf16[12,16,1024]{2,1,0:T(8,128)(2,1)S(1)} %get-tuple-element.42), channel_id=1, source_target_pairs={{0,128},{64,192},{128,0},{192,64},{1,129},{65,193},{129,1},{193,65... | collective-permute-start | bytes 1179656 | tf_op jit(solution)/shard_map/ppermute | solution.py:243
  9.6 1.2 copy-done.2
  10.8 2.3 %root_halves.1 = (bf16[8,256,128]{2,1,0:T(8,128)(2,1)S(1)}, bf16[8,256,128]{2,1,0:T(8,128)(2,1)S(1)}, bf16[8,256,128]{2,1,0:T(8,128)(2,1)S(1)}, bf16[8,256,128]{2,1,0:T(8,128)(2,1)S(1)}, s32[8]{0:T(128)S(1)}) custom-call(s32[48]{0:T(128)S(1)} %get-tuple-element.32.sorted_target, bf16[2,256,1024]{2,1,0:T(8,128)(2,1)S(1)} %copy-done.1, ...), custom_call_target="tpu_custom_call" | custom-call | tf_op jit(solution)/shard_map/root_halves/pallas_call | solution.py:259
  13.1 1.6 %collective-permute-start = (bf16[8,256,128]{2,1,0:T(8,128)(2,1)S(1)}, bf16[8,256,128]{2,1,0:T(8,128)(2,1)S(1)}, u32[]{:S(2)}, u32[]{:S(2)}) collective-permute-start(bf16[8,256,128]{2,1,0:T(8,128)(2,1)S(1)} %get-tuple-element.36), channel_id=1, source_target_pairs={{0,1},{1,0},{2,3},{3,2},{4,5},{5,4},{6,7},{7,6},{8,9},{9,8},{10,11... | collective-permute-start | bytes 1572872 | tf_op jit(solution)/shard_map/ppermute | solution.py:246
  15.9 10.2 %collective-permute-done.4.__0_ = bf16[12,16,1024]{2,1,0:T(8,128)(2,1)S(1)} collective-permute-done((bf16[12,16,1024]{2,1,0:T(8,128)(2,1)S(1)}, bf16[12,16,1024]{2,1,0:T(8,128)(2,1)S(1)}, u32[]{:S(2)}, u32[]{:S(2)}) %collective-permute-start.4) | collective-permute-done | bytes 393248 | tf_op jit(solution)/shard_map/ppermute | solution.py:243
  26.1 1.6 %roots_by_plane.1 = (bf16[8,256,128]{2,1,0:T(8,128)(2,1)S(1)}, bf16[8,256,128]{2,1,0:T(8,128)(2,1)S(1)}, bf16[8,256,128]{2,1,0:T(8,128)(2,1)}, bf16[8,256,128]{2,1,0:T(8,128)(2,1)S(1)}) custom-call(s32[8]{0:T(128)S(1)} %get-tuple-element.33.table, bf16[8,256,128]{2,1,0:T(8,128)(2,1)S(1)} %get-tuple-element.34.refs_0_, ...), custom_call_target="tpu_custom_call" | custom-call | tf_op jit(solution)/shard_map/roots_by_plane/pallas_call | solution.py:268
  27.7 1.8 %sum_and_place.1 = bf16[64,16,512]{2,1,0:T(8,128)(2,1)} custom-call(s32[48]{0:T(128)S(1)} %get-tuple-element.32.sorted_target, bf16[8,256,128]{2,1,0:T(8,128)(2,1)S(1)} %get-tuple-element.46._.refs_0_, bf16[12,16,1024]{2,1,0:T(8,128)(2,1)S(1)} %get-tuple-element.39.own, bf16[12,16,1024]{2,1,0:T(8,128)(2,1)S(1)} %settle.4.one, ...), custom_call_target="tpu_custom_call" | custom-call | bytes 3145728 | tf_op jit(solution)/shard_map/sum_and_place/pallas_call | solution.py:277
  29.6 13.6 %all-to-all-start = ((bf16[64,16,512]{2,1,0:T(8,128)(2,1)}), bf16[64,16,512]{2,1,0:T(8,128)(2,1)S(1)}, u32[]{:S(2)}, u32[]{:S(2)}) async-start(bf16[64,16,512]{2,1,0:T(8,128)(2,1)} %sum_and_place.1), calls=%async_computation | async-start | bytes 2097152 | tf_op jit(solution)/shard_map/all_to_all | solution.py:288
  43.2 1.8 %collective-permute-start.5 = (bf16[8,256,128]{2,1,0:T(8,128)(2,1)S(1)}, bf16[8,256,128]{2,1,0:T(8,128)(2,1)S(1)}, u32[]{:S(2)}, u32[]{:S(2)}) collective-permute-start(bf16[8,256,128]{2,1,0:T(8,128)(2,1)S(1)} %get-tuple-element.47), channel_id=1, source_target_pairs={{0,64},{64,128},{128,192},{192,0},{1,65},{65,129},{129,193},{193,1... | collective-permute-start | bytes 1572872 | tf_op jit(solution)/shard_map/ppermute | solution.py:243
  45.0 1.2 collective-permute-start.7
  46.2 11.6 %collective-permute-done.5.refs_1_ = bf16[8,256,128]{2,1,0:T(8,128)(2,1)S(1)} collective-permute-done((bf16[8,256,128]{2,1,0:T(8,128)(2,1)S(1)}, bf16[8,256,128]{2,1,0:T(8,128)(2,1)S(1)}, u32[]{:S(2)}, u32[]{:S(2)}) %collective-permute-start.5) | collective-permute-done | bytes 524320 | tf_op jit(solution)/shard_map/ppermute | solution.py:243
  59.1 1.6 %collective-permute-start.8 = (bf16[1024,512]{1,0:T(8,128)(2,1)S(1)}, bf16[1024,512]{1,0:T(8,128)(2,1)S(1)}, u32[]{:S(2)}, u32[]{:S(2)}) collective-permute-start(bf16[1024,512]{1,0:T(8,128)(2,1)S(1)} %get-tuple-element.50.l_own), channel_id=1, source_target_pairs={{0,1},{1,0},{2,3},{3,2},{4,5},{5,4},{6,7},{7,6},{8,9},{9,8},{10,11... | collective-permute-start | bytes 3145736 | tf_op jit(solution)/shard_map/ppermute | solution.py:246
  60.7 2.3 %collective-permute-done.8.__1_ = bf16[1024,512]{1,0:T(8,128)(2,1)S(1)} collective-permute-done((bf16[1024,512]{1,0:T(8,128)(2,1)S(1)}, bf16[1024,512]{1,0:T(8,128)(2,1)S(1)}, u32[]{:S(2)}, u32[]{:S(2)}) %collective-permute-start.8) | collective-permute-done | bytes 1048608 | tf_op jit(solution)/shard_map/ppermute | solution.py:246
  63.0 8.3 %all-to-all-done.__0_ = bf16[64,16,512]{2,1,0:T(8,128)(2,1)S(1)} async-done(((bf16[64,16,512]{2,1,0:T(8,128)(2,1)}), bf16[64,16,512]{2,1,0:T(8,128)(2,1)S(1)}, u32[]{:S(2)}, u32[]{:S(2)}) %all-to-all-start) | async-done | bytes 1048608 | tf_op jit(solution)/shard_map/all_to_all | solution.py:288
  71.2 1.4 %collective-permute-start.9 = (bf16[1024,512]{1,0:T(8,128)(2,1)S(1)}, bf16[1024,512]{1,0:T(8,128)(2,1)S(1)}, u32[]{:S(2)}, u32[]{:S(2)}) collective-permute-start(bf16[1024,512]{1,0:T(8,128)(2,1)S(1)} %bitcast.5), channel_id=1, source_target_pairs={{0,1},{1,0},{2,3},{3,2},{4,5},{5,4},{6,7},{7,6},{8,9},{9,8},{10,11... | collective-permute-start | bytes 3145736 | tf_op jit(solution)/shard_map/ppermute | solution.py:246
  72.6 2.3 %collective-permute-done.9.s_far = bf16[1024,512]{1,0:T(8,128)(2,1)S(1)} collective-permute-done((bf16[1024,512]{1,0:T(8,128)(2,1)S(1)}, bf16[1024,512]{1,0:T(8,128)(2,1)S(1)}, u32[]{:S(2)}, u32[]{:S(2)}) %collective-permute-start.9) | collective-permute-done | bytes 1048608 | tf_op jit(solution)/shard_map/ppermute | solution.py:246
  74.9 3.2 %gram.1 = (bf16[2,256,512]{2,1,0:T(8,128)(2,1)S(1)}, bf16[2,256,512]{2,1,0:T(8,128)(2,1)}, bf16[2,256,512]{2,1,0:T(8,128)(2,1)}, bf16[2,256,512]{2,1,0:T(8,128)(2,1)}) custom-call(bf16[1024,512]{1,0:T(8,128)(2,1)S(1)} %bitcast.6, bf16[1024,512]{1,0:T(8,128)(2,1)S(1)} %collective-permute-done.9.s_far), custom_call_target="tpu_custom_call" | custom-call | flops 2147483648 | bytes 4194304 | tf_op jit(solution)/shard_map/gram/pallas_call | solution.py:303
  78.1 1.7 %collective-permute-start.10 = (bf16[2,256,512]{2,1,0:T(8,128)(2,1)}, bf16[2,256,512]{2,1,0:T(8,128)(2,1)}, u32[]{:S(2)}, u32[]{:S(2)}) collective-permute-start(bf16[2,256,512]{2,1,0:T(8,128)(2,1)} %get-tuple-element.53), channel_id=1, source_target_pairs={{0,64},{64,128},{128,192},{192,0},{1,65},{65,129},{129,193},{193,1... | collective-permute-start | bytes 1572872 | tf_op jit(solution)/shard_map/ppermute | solution.py:243
  79.8 2.3 %collective-permute-start.11 = (bf16[2,256,512]{2,1,0:T(8,128)(2,1)}, bf16[2,256,512]{2,1,0:T(8,128)(2,1)}, u32[]{:S(2)}, u32[]{:S(2)}) collective-permute-start(bf16[2,256,512]{2,1,0:T(8,128)(2,1)} %get-tuple-element.54), channel_id=1, source_target_pairs={{0,128},{64,192},{128,0},{192,64},{1,129},{65,193},{129,1},{193,65... | collective-permute-start | bytes 1572872 | tf_op jit(solution)/shard_map/ppermute | solution.py:243
  82.6 3.4 %update_block.1 = bf16[4,64,16,128]{3,2,1,0:T(8,128)(2,1)} custom-call(bf16[1024,512]{1,0:T(8,128)(2,1)S(1)} %bitcast.7, bf16[1024,512]{1,0:T(8,128)(2,1)S(1)} %collective-permute-done.9.s_far, bf16[1024,512]{1,0:T(8,128)(2,1)S(1)} %get-tuple-element.50.l_own, bf16[1024,512]{1,0:T(8,128)(2,1)S(1)} %get-tuple-element.59.l_far, bf16[1024,512]{1,0:T(8,128)(2,1)S(1)} %copy-done.5), custom_call_target="tpu_custom_call" | custom-call | flops 2147483648 | bytes 6291456 | tf_op jit(solution)/shard_map/update_block/pallas_call | solution.py:313
  86.1 7.0 %all-to-all-start.1 = ((bf16[256,16,128]{2,1,0:T(8,128)(2,1)}), bf16[256,16,128]{2,1,0:T(8,128)(2,1)S(1)}, u32[]{:S(2)}, u32[]{:S(2)}) async-start(bf16[256,16,128]{2,1,0:T(8,128)(2,1)} %bitcast.2), calls=%async_computation.1 | async-start | bytes 2097152 | tf_op jit(solution)/shard_map/all_to_all | solution.py:324
  93.1 2.2 %collective-permute-start.13 = (bf16[2,256,512]{2,1,0:T(8,128)(2,1)S(1)}, bf16[2,256,512]{2,1,0:T(8,128)(2,1)S(1)}, u32[]{:S(2)}, u32[]{:S(2)}) collective-permute-start(bf16[2,256,512]{2,1,0:T(8,128)(2,1)S(1)} %copy-done.7), channel_id=1, source_target_pairs={{0,1},{1,0},{2,3},{3,2},{4,5},{5,4},{6,7},{7,6},{8,9},{9,8},{10,11... | collective-permute-start | bytes 1572872 | tf_op jit(solution)/shard_map/ppermute | solution.py:246
  95.4 15.6 %collective-permute-done.11.rest_2_ = bf16[2,256,512]{2,1,0:T(8,128)(2,1)} collective-permute-done((bf16[2,256,512]{2,1,0:T(8,128)(2,1)}, bf16[2,256,512]{2,1,0:T(8,128)(2,1)}, u32[]{:S(2)}, u32[]{:S(2)}) %collective-permute-start.11) | collective-permute-done | bytes 524320 | tf_op jit(solution)/shard_map/ppermute | solution.py:243
  111.0 2.5 %collective-permute-start.15 = (bf16[2,256,512]{2,1,0:T(8,128)(2,1)}, bf16[2,256,512]{2,1,0:T(8,128)(2,1)S(1)}, u32[]{:S(2)}, u32[]{:S(2)}) collective-permute-start(bf16[2,256,512]{2,1,0:T(8,128)(2,1)} %collective-permute-done.11.rest_2_), channel_id=1, source_target_pairs={{0,1},{1,0},{2,3},{3,2},{4,5},{5,4},{6,7},{7,6},{8,9},{9,8},{10,11... | collective-permute-start | bytes 1572872 | tf_op jit(solution)/shard_map/ppermute | solution.py:246
  113.6 1.6 %collective-permute-done.15.rest_6_ = bf16[2,256,512]{2,1,0:T(8,128)(2,1)S(1)} collective-permute-done((bf16[2,256,512]{2,1,0:T(8,128)(2,1)}, bf16[2,256,512]{2,1,0:T(8,128)(2,1)S(1)}, u32[]{:S(2)}, u32[]{:S(2)}) %collective-permute-start.15) | collective-permute-done | bytes 524320 | tf_op jit(solution)/shard_map/ppermute | solution.py:246
  116.9 5.7 %statistics.1 = (f32[2,256,1024]{2,1,0:T(8,128)}, f32[2,256,1024]{2,1,0:T(8,128)}) custom-call(s32[8]{0:T(128)} %copy-done.3, f32[2,256,1024]{2,1,0:T(8,128)} %stat_left.1, f32[2,256,1024]{2,1,0:T(8,128)} %stat_right.1, bf16[2,256,512]{2,1,0:T(8,128)(2,1)} %copy-done.6, bf16[2,256,512]{2,1,0:T(8,128)(2,1)} %collective-permute-done.10.rest_1_, ...), custom_call_target="tpu_custom_call" | custom-call | flops 15000000512 | bytes 8388608 | tf_op jit(solution)/shard_map/statistics/pallas_call | solution.py:337
  122.6 1.6 %all-to-all-done.1 = bf16[256,16,128]{2,1,0:T(8,128)(2,1)S(1)} async-done(((bf16[256,16,128]{2,1,0:T(8,128)(2,1)}), bf16[256,16,128]{2,1,0:T(8,128)(2,1)S(1)}, u32[]{:S(2)}, u32[]{:S(2)}) %all-to-all-start.1) | async-done | bytes 1048608 | tf_op jit(solution)/shard_map/all_to_all | solution.py:324
  124.1 1.6 %pick.1 = bf16[48,16,256]{2,1,0:T(8,128)(2,1)} custom-call(s32[48]{0:T(128)S(1)} %get-tuple-element.58.order, s32[48]{0:T(128)S(1)} %get-tuple-element.32.sorted_target, bf16[4,32,2,16,128]{4,3,2,1,0:T(8,128)(2,1)S(1)} %bitcast.4), custom_call_target="tpu_custom_call" | custom-call | bytes 2097152 | tf_op jit(solution)/shard_map/pick/pallas_call | solution.py:325
  (46 shorter events, 6.1 us)
Async XLA Ops:
  1.5 1.4 %copy-start = (bf16[1,48,16,1024]{3,2,1,0:T(8,128)(2,1)S(1)}, bf16[1,48,16,1024]{3,2,1,0:T(8,128)(2,1)}, u32[]{:S(2)}) copy-start(bf16[1,48,16,1024]{3,2,1,0:T(8,128)(2,1)} %param.7) | copy-start | bytes 4718596
  2.9 6.7 %copy-start.1 = (bf16[2,256,1024]{2,1,0:T(8,128)(2,1)S(1)}, bf16[2,256,1024]{2,1,0:T(8,128)(2,1)}, u32[]{:S(2)}) copy-start(bf16[2,256,1024]{2,1,0:T(8,128)(2,1)} %left.1) | copy-start | bytes 3145732
  4.3 10.5 %collective-permute-start.2 = (bf16[12,16,1024]{2,1,0:T(8,128)(2,1)S(1)}, bf16[12,16,1024]{2,1,0:T(8,128)(2,1)S(1)}, u32[]{:S(2)}, u32[]{:S(2)}) collective-permute-start(bf16[12,16,1024]{2,1,0:T(8,128)(2,1)S(1)} %get-tuple-element.40), channel_id=1, source_target_pairs={{0,64},{64,128},{128,192},{192,0},{1,65},{65,129},{129,193},{193,1... | collective-permute-start | bytes 1179656 | tf_op jit(solution)/shard_map/ppermute | solution.py:243
  6.5 9.4 %collective-permute-start.3 = (bf16[12,16,1024]{2,1,0:T(8,128)(2,1)S(1)}, bf16[12,16,1024]{2,1,0:T(8,128)(2,1)S(1)}, u32[]{:S(2)}, u32[]{:S(2)}) collective-permute-start(bf16[12,16,1024]{2,1,0:T(8,128)(2,1)S(1)} %get-tuple-element.41), channel_id=1, source_target_pairs={{0,192},{64,0},{128,64},{192,128},{1,193},{65,1},{129,65},{193,129... | collective-permute-start | bytes 1179656 | tf_op jit(solution)/shard_map/ppermute | solution.py:243
  8.0 18.0 %collective-permute-start.4 = (bf16[12,16,1024]{2,1,0:T(8,128)(2,1)S(1)}, bf16[12,16,1024]{2,1,0:T(8,128)(2,1)S(1)}, u32[]{:S(2)}, u32[]{:S(2)}) collective-permute-start(bf16[12,16,1024]{2,1,0:T(8,128)(2,1)S(1)} %get-tuple-element.42), channel_id=1, source_target_pairs={{0,128},{64,192},{128,0},{192,64},{1,129},{65,193},{129,1},{193,65... | collective-permute-start | bytes 1179656 | tf_op jit(solution)/shard_map/ppermute | solution.py:243
  9.6 1.2 copy-start.2
  13.1 13.0 %copy-start.3 = (s32[8]{0:T(128)}, s32[8]{0:T(128)S(1)}, u32[]{:S(2)}) copy-start(s32[8]{0:T(128)S(1)} %get-tuple-element.33.table) | copy-start | bytes 100
  13.1 13.0 %collective-permute-start = (bf16[8,256,128]{2,1,0:T(8,128)(2,1)S(1)}, bf16[8,256,128]{2,1,0:T(8,128)(2,1)S(1)}, u32[]{:S(2)}, u32[]{:S(2)}) collective-permute-start(bf16[8,256,128]{2,1,0:T(8,128)(2,1)S(1)} %get-tuple-element.36), channel_id=1, source_target_pairs={{0,1},{1,0},{2,3},{3,2},{4,5},{5,4},{6,7},{7,6},{8,9},{9,8},{10,11... | collective-permute-start | bytes 1572872 | tf_op jit(solution)/shard_map/ppermute | solution.py:246
  14.7 11.4 %collective-permute-start.1 = (bf16[8,256,128]{2,1,0:T(8,128)(2,1)S(1)}, bf16[8,256,128]{2,1,0:T(8,128)(2,1)S(1)}, u32[]{:S(2)}, u32[]{:S(2)}) collective-permute-start(bf16[8,256,128]{2,1,0:T(8,128)(2,1)S(1)} %get-tuple-element.37), channel_id=1, source_target_pairs={{0,1},{1,0},{2,3},{3,2},{4,5},{5,4},{6,7},{7,6},{8,9},{9,8},{10,11... | collective-permute-start | bytes 1572872 | tf_op jit(solution)/shard_map/ppermute | solution.py:246
  29.4 16.7 %collective-permute-start.6 = (bf16[8,256,128]{2,1,0:T(8,128)(2,1)}, bf16[8,256,128]{2,1,0:T(8,128)(2,1)S(1)}, u32[]{:S(2)}, u32[]{:S(2)}) collective-permute-start(bf16[8,256,128]{2,1,0:T(8,128)(2,1)} %get-tuple-element.48), channel_id=1, source_target_pairs={{0,128},{64,192},{128,0},{192,64},{1,129},{65,193},{129,1},{193,65... | collective-permute-start | bytes 1572872 | tf_op jit(solution)/shard_map/ppermute | solution.py:243
  29.6 41.6 %all-to-all-start = ((bf16[64,16,512]{2,1,0:T(8,128)(2,1)}), bf16[64,16,512]{2,1,0:T(8,128)(2,1)S(1)}, u32[]{:S(2)}, u32[]{:S(2)}) async-start(bf16[64,16,512]{2,1,0:T(8,128)(2,1)} %sum_and_place.1), calls=%async_computation | async-start | bytes 2097152 | tf_op jit(solution)/shard_map/all_to_all | solution.py:288
  43.2 14.5 %collective-permute-start.5 = (bf16[8,256,128]{2,1,0:T(8,128)(2,1)S(1)}, bf16[8,256,128]{2,1,0:T(8,128)(2,1)S(1)}, u32[]{:S(2)}, u32[]{:S(2)}) collective-permute-start(bf16[8,256,128]{2,1,0:T(8,128)(2,1)S(1)} %get-tuple-element.47), channel_id=1, source_target_pairs={{0,64},{64,128},{128,192},{192,0},{1,65},{65,129},{129,193},{193,1... | collective-permute-start | bytes 1572872 | tf_op jit(solution)/shard_map/ppermute | solution.py:243
  45.0 12.7 %collective-permute-start.7 = (bf16[8,256,128]{2,1,0:T(8,128)(2,1)S(1)}, bf16[8,256,128]{2,1,0:T(8,128)(2,1)S(1)}, u32[]{:S(2)}, u32[]{:S(2)}) collective-permute-start(bf16[8,256,128]{2,1,0:T(8,128)(2,1)S(1)} %get-tuple-element.49), channel_id=1, source_target_pairs={{0,192},{64,0},{128,64},{192,128},{1,193},{65,1},{129,65},{193,129... | collective-permute-start | bytes 1572872 | tf_op jit(solution)/shard_map/ppermute | solution.py:243
  58.1 1.0 copy-start.4
  59.1 3.9 %collective-permute-start.8 = (bf16[1024,512]{1,0:T(8,128)(2,1)S(1)}, bf16[1024,512]{1,0:T(8,128)(2,1)S(1)}, u32[]{:S(2)}, u32[]{:S(2)}) collective-permute-start(bf16[1024,512]{1,0:T(8,128)(2,1)S(1)} %get-tuple-element.50.l_own), channel_id=1, source_target_pairs={{0,1},{1,0},{2,3},{3,2},{4,5},{5,4},{6,7},{7,6},{8,9},{9,8},{10,11... | collective-permute-start | bytes 3145736 | tf_op jit(solution)/shard_map/ppermute | solution.py:246
  71.2 11.4 %copy-start.5 = (bf16[1024,512]{1,0:T(8,128)(2,1)S(1)}, bf16[1024,512]{1,0:T(8,128)(2,1)}, u32[]{:S(2)}) copy-start(bf16[1024,512]{1,0:T(8,128)(2,1)} %copy-done.4) | copy-start | bytes 3145732
  71.2 3.6 %collective-permute-start.9 = (bf16[1024,512]{1,0:T(8,128)(2,1)S(1)}, bf16[1024,512]{1,0:T(8,128)(2,1)S(1)}, u32[]{:S(2)}, u32[]{:S(2)}) collective-permute-start(bf16[1024,512]{1,0:T(8,128)(2,1)S(1)} %bitcast.5), channel_id=1, source_target_pairs={{0,1},{1,0},{2,3},{3,2},{4,5},{5,4},{6,7},{7,6},{8,9},{9,8},{10,11... | collective-permute-start | bytes 3145736 | tf_op jit(solution)/shard_map/ppermute | solution.py:246
  78.1 8.0 %copy-start.6 = (bf16[2,256,512]{2,1,0:T(8,128)(2,1)}, bf16[2,256,512]{2,1,0:T(8,128)(2,1)S(1)}, u32[]{:S(2)}) copy-start(bf16[2,256,512]{2,1,0:T(8,128)(2,1)S(1)} %get-tuple-element.52.rest_0_) | copy-start | bytes 1572868
  78.1 17.2 %collective-permute-start.10 = (bf16[2,256,512]{2,1,0:T(8,128)(2,1)}, bf16[2,256,512]{2,1,0:T(8,128)(2,1)}, u32[]{:S(2)}, u32[]{:S(2)}) collective-permute-start(bf16[2,256,512]{2,1,0:T(8,128)(2,1)} %get-tuple-element.53), channel_id=1, source_target_pairs={{0,64},{64,128},{128,192},{192,0},{1,65},{65,129},{129,193},{193,1... | collective-permute-start | bytes 1572872 | tf_op jit(solution)/shard_map/ppermute | solution.py:243
  79.8 31.2 %collective-permute-start.11 = (bf16[2,256,512]{2,1,0:T(8,128)(2,1)}, bf16[2,256,512]{2,1,0:T(8,128)(2,1)}, u32[]{:S(2)}, u32[]{:S(2)}) collective-permute-start(bf16[2,256,512]{2,1,0:T(8,128)(2,1)} %get-tuple-element.54), channel_id=1, source_target_pairs={{0,128},{64,192},{128,0},{192,64},{1,129},{65,193},{129,1},{193,65... | collective-permute-start | bytes 1572872 | tf_op jit(solution)/shard_map/ppermute | solution.py:243
  82.0 31.5 %collective-permute-start.12 = (bf16[2,256,512]{2,1,0:T(8,128)(2,1)}, bf16[2,256,512]{2,1,0:T(8,128)(2,1)}, u32[]{:S(2)}, u32[]{:S(2)}) collective-permute-start(bf16[2,256,512]{2,1,0:T(8,128)(2,1)} %get-tuple-element.55), channel_id=1, source_target_pairs={{0,192},{64,0},{128,64},{192,128},{1,193},{65,1},{129,65},{193,129... | collective-permute-start | bytes 1572872 | tf_op jit(solution)/shard_map/ppermute | solution.py:243
  86.1 7.0 %copy-start.7 = (bf16[2,256,512]{2,1,0:T(8,128)(2,1)S(1)}, bf16[2,256,512]{2,1,0:T(8,128)(2,1)}, u32[]{:S(2)}) copy-start(bf16[2,256,512]{2,1,0:T(8,128)(2,1)} %copy-done.6) | copy-start | bytes 1572868
  86.1 38.1 %all-to-all-start.1 = ((bf16[256,16,128]{2,1,0:T(8,128)(2,1)}), bf16[256,16,128]{2,1,0:T(8,128)(2,1)S(1)}, u32[]{:S(2)}, u32[]{:S(2)}) async-start(bf16[256,16,128]{2,1,0:T(8,128)(2,1)} %bitcast.2), calls=%async_computation.1 | async-start | bytes 2097152 | tf_op jit(solution)/shard_map/all_to_all | solution.py:324
  93.1 20.5 %collective-permute-start.13 = (bf16[2,256,512]{2,1,0:T(8,128)(2,1)S(1)}, bf16[2,256,512]{2,1,0:T(8,128)(2,1)S(1)}, u32[]{:S(2)}, u32[]{:S(2)}) collective-permute-start(bf16[2,256,512]{2,1,0:T(8,128)(2,1)S(1)} %copy-done.7), channel_id=1, source_target_pairs={{0,1},{1,0},{2,3},{3,2},{4,5},{5,4},{6,7},{7,6},{8,9},{9,8},{10,11... | collective-permute-start | bytes 1572872 | tf_op jit(solution)/shard_map/ppermute | solution.py:246
  95.3 18.3 %collective-permute-start.14 = (bf16[2,256,512]{2,1,0:T(8,128)(2,1)}, bf16[2,256,512]{2,1,0:T(8,128)(2,1)S(1)}, u32[]{:S(2)}, u32[]{:S(2)}) collective-permute-start(bf16[2,256,512]{2,1,0:T(8,128)(2,1)} %collective-permute-done.10.rest_1_), channel_id=1, source_target_pairs={{0,1},{1,0},{2,3},{3,2},{4,5},{5,4},{6,7},{7,6},{8,9},{9,8},{10,11... | collective-permute-start | bytes 1572872 | tf_op jit(solution)/shard_map/ppermute | solution.py:246
  111.0 4.2 %collective-permute-start.15 = (bf16[2,256,512]{2,1,0:T(8,128)(2,1)}, bf16[2,256,512]{2,1,0:T(8,128)(2,1)S(1)}, u32[]{:S(2)}, u32[]{:S(2)}) collective-permute-start(bf16[2,256,512]{2,1,0:T(8,128)(2,1)} %collective-permute-done.11.rest_2_), channel_id=1, source_target_pairs={{0,1},{1,0},{2,3},{3,2},{4,5},{5,4},{6,7},{7,6},{8,9},{9,8},{10,11... | collective-permute-start | bytes 1572872 | tf_op jit(solution)/shard_map/ppermute | solution.py:246
  113.5 2.5 %collective-permute-start.16 = (bf16[2,256,512]{2,1,0:T(8,128)(2,1)}, bf16[2,256,512]{2,1,0:T(8,128)(2,1)S(1)}, u32[]{:S(2)}, u32[]{:S(2)}) collective-permute-start(bf16[2,256,512]{2,1,0:T(8,128)(2,1)} %collective-permute-done.12.rest_3_), channel_id=1, source_target_pairs={{0,1},{1,0},{2,3},{3,2},{4,5},{5,4},{6,7},{7,6},{8,9},{9,8},{10,11... | collective-permute-start | bytes 1572872 | tf_op jit(solution)/shard_map/ppermute | solution.py:246
  113.6 2.4 %copy-start.8 = (bf16[2,256,512]{2,1,0:T(8,128)(2,1)}, bf16[2,256,512]{2,1,0:T(8,128)(2,1)S(1)}, u32[]{:S(2)}) copy-start(bf16[2,256,512]{2,1,0:T(8,128)(2,1)S(1)} %collective-permute-done.13.rest_4_) | copy-start | bytes 1572868
  113.6 2.4 %copy-start.9 = (bf16[2,256,512]{2,1,0:T(8,128)(2,1)}, bf16[2,256,512]{2,1,0:T(8,128)(2,1)S(1)}, u32[]{:S(2)}) copy-start(bf16[2,256,512]{2,1,0:T(8,128)(2,1)S(1)} %collective-permute-done.14.rest_5_) | copy-start | bytes 1572868
  115.3 0.8 copy-start.10
  116.1 0.8 copy-start.11

commit v3 on v2

--- a/solution.py
+++ b/solution.py
@@ -189,16 +189,23 @@
         grams[k][1] = (right / 1024).astype(BF16)
 
 
-def statistics(table, stat_left, stat_right, *rest):
+def preload(_, stat_left, stat_right, left, right, sems):
+    copies = [pltpu.make_async_copy(stat_left, left, sems.at[0])]
+    copies.append(pltpu.make_async_copy(stat_right, right, sems.at[1]))
+    for copy in copies:
+        copy.start()
+    for copy in copies:
+        copy.wait()
+
+
+def statistics(table, left, right, *rest):
     own, other, (left_new, right_new), scratch = rest[:4], rest[4:8], rest[8:10], rest[10:]
-    added, left, right, g_sems, in_sems, out_sems = scratch
+    added, sums, g_sems, out_sems = scratch
     r, _, c = my_place()
-    pairs = ((stat_left, left, left_new), (stat_right, right, right_new))
+    pairs = ((left, left_new), (right, right_new))
     near = pl.ds(pl.multiple_of(c * 512, 512), 512)
     far = pl.ds(pl.multiple_of((1 - c) * 512, 512), 512)
     for s in range(SLOTS):
-        for i, (source, here, _) in enumerate(pairs):
-            pltpu.make_async_copy(source.at[s], here.at[s], in_sems.at[2 * s + i]).start()
         step = (r - table[4 + s] + PLANES) % PLANES
         for k in range(PLANES):
 
@@ -211,14 +218,9 @@
     for s in range(SLOTS):
         pltpu.make_async_copy(added.at[s], added.at[s], g_sems.at[s]).wait()
         used = table[6 + s] > 0
-        for i, (source, here, out) in enumerate(pairs):
-            pltpu.make_async_copy(source.at[s], here.at[s], in_sems.at[2 * s + i]).wait()
-
-            @pl.when(used)
-            def _():
-                here[s] = here[s] + added[s, i].astype(F32)
-
-            store = pltpu.make_async_copy(here.at[s], out.at[s], out_sems.at[2 * s + i])
+        for i, (here, out) in enumerate(pairs):
+            sums[s, i] = jnp.where(used, here[s] + added[s, i].astype(F32), here[s])
+            store = pltpu.make_async_copy(sums.at[s, i], out.at[s], out_sems.at[2 * s + i])
             store.start()
             stores.append(store)
     for store in stores:
@@ -332,25 +334,30 @@
         nbytes=2 << 20,
     )(order, sorted_target, returned.reshape(PLANES, fsdp_count // CORES, CORES, rows, 128))
 
-    grams = [grams[0]] + [along(grams[k], k) for k in range(1, PLANES)]
+    first = settle(along(grams[2], 2), GRAM_HINT)
+    grams = [grams[0], along(grams[1], 1), first, along(grams[3], 3)]
     grams_far = [across(x) for x in grams]
+    stat_left, stat_right = call(
+        preload,
+        "preload",
+        [like(stat_left.shape, F32), like(stat_right.shape, F32)],
+        [ANY] * 3,
+        [VMEM] * 2,
+        [pltpu.SemaphoreType.DMA((2,))],
+    )(first, stat_left, stat_right)
     left_new, right_new = call(
         statistics,
         "statistics",
         [like(stat_left.shape, F32)] * 2,
-        [SMEM] + [ANY] * (2 + 2 * PLANES),
+        [SMEM, VMEM, VMEM] + [ANY] * (2 * PLANES),
         [ANY] * 2,
         [
             pltpu.VMEM((SLOTS, 2, 256, width), BF16),
-            pltpu.VMEM(stat_left.shape, F32),
-            pltpu.VMEM(stat_right.shape, F32),
+            pltpu.VMEM((SLOTS, 2, 256, width), F32),
             pltpu.SemaphoreType.DMA((SLOTS,)),
             pltpu.SemaphoreType.DMA((2 * SLOTS,)),
-            pltpu.SemaphoreType.DMA((2 * SLOTS,)),
         ],
-        flops=15 * 1000**3,
         nbytes=8 << 20,
-        vmem=VMEM_WHOLE,
     )(table, stat_left, stat_right, *grams, *grams_far)
 
     return (left_new, right_new, new)

time: 126 us -> 125 us (level)
  Pallas kernels: 21.3 us -> 18.7 us
  local copies, waits for them, and re-layouts: 4.49 us -> 6.19 us
  starting transfers between devices: 43.1 us -> 44.8 us
  waiting for transfers between devices: 55.3 us -> 53.9 us
    pallas_call x1 -> x2, Pallas kernels: 5.7 us -> 3.38 us  [the longest x1 3.08 us: per_device(): call(statistics, 'statistics', [like(stat_left.shape, F32)] * 2, [SMEM, V...]
    unnamed x24 -> x26, local copies, waits for them, and re-layouts: 4.49 us -> 6.19 us
    ppermute x8, waiting for transfers between devices: 6.96 us -> 5.27 us  [across(): return lax.ppermute(x, 'fsdp', [(i, i ^ 1) for i in range(fsdp_count)])]
  transfers between devices with their start and end apart: 19 -> 19, of which waited for: 10 -> 10; matrix products, arithmetic and copies ran while one was open for 0% -> 0% of each run, Pallas kernels for 9% -> 8%
where the time goes in v3:
time: 125 us
  waiting for transfers between devices  53.9 us (43%)
  starting transfers between devices  44.8 us (36%)
  Pallas kernels  18.7 us (15%)
  local copies, waits for them, and re-layouts  6.19 us (5%)
    ppermute x9, waiting for transfers between devices, along(): lax.ppermute(x, 'replica', [(i, (i + step) % PLANES) for i in range(PLANE...  38.8 us
    ppermute x9, starting transfers between devices, along(): lax.ppermute(x, 'replica', [(i, (i + step) % PLANES) for i in range(PLANE...  13.7 us
    all_to_all x1, starting transfers between devices, per_device(): lax.all_to_all(outgoing, 'fsdp', split_axis=0, concat_axis=0, tiled=True)  13.6 us
    ppermute x8, starting transfers between devices, across(): return lax.ppermute(x, 'fsdp', [(i, i ^ 1) for i in range(fsdp_count)])  10.4 us
    all_to_all x1, waiting for transfers between devices, per_device(): lax.all_to_all(outgoing, 'fsdp', split_axis=0, concat_axis=0, tiled=True)  8.26 us
    all_to_all x1, starting transfers between devices, per_device(): lax.all_to_all(update, ('replica', 'fsdp'), split_axis=0, concat_axis=0,...  7.14 us
    unnamed x26, local copies, waits for them, and re-layouts  6.19 us
    ppermute x8, waiting for transfers between devices, across(): return lax.ppermute(x, 'fsdp', [(i, i ^ 1) for i in range(fsdp_count)])  5.27 us
  transfers between devices with their start and end apart: 19, of which 10 were waited for; matrix products, arithmetic and copies ran while one was open for 0% of the time, Pallas kernels for 8%

profile of v3, /device:TPU:1, one launch (start us, length us, event | category | flops | bytes accessed | tf_op | source)
XLA Modules:
  0.0 125.2 jit_solution(14941836102347256615)
XLA Ops:
  1.5 1.4 %copy-done.2 = bf16[1,48,16,1024]{3,2,1,0:T(8,128)(2,1)S(1)} copy-done((bf16[1,48,16,1024]{3,2,1,0:T(8,128)(2,1)S(1)}, bf16[1,48,16,1024]{3,2,1,0:T(8,128)(2,1)}, u32[]{:S(2)}) %copy-start.2) | copy-done | bytes 1572888
  2.9 1.4 %by_plane.1 = (s32[48]{0:T(128)S(1)}, s32[48]{0:T(128)S(1)}, bf16[12,16,1024]{2,1,0:T(8,128)(2,1)S(1)}, bf16[12,16,1024]{2,1,0:T(8,128)(2,1)S(1)}, bf16[12,16,10...) custom-call(s32[48]{0:T(128)S(1)} %convert_reduce_fusion.rank, s32[48]{0:T(128)S(1)} %multiply_add_fusion.target, ...), custom_call_target="tpu_custom_call" | custom-call | bytes 3145728 | tf_op jit(solution)/shard_map/by_plane/pallas_call | solution.py:250
  4.3 2.2 %collective-permute-start.2 = (bf16[12,16,1024]{2,1,0:T(8,128)(2,1)S(1)}, bf16[12,16,1024]{2,1,0:T(8,128)(2,1)S(1)}, u32[]{:S(2)}, u32[]{:S(2)}) collective-permute-start(bf16[12,16,1024]{2,1,0:T(8,128)(2,1)S(1)} %get-tuple-element.42), channel_id=1, source_target_pairs={{0,64},{64,128},{128,192},{192,0},{1,65},{65,129},{129,193},{193,1... | collective-permute-start | bytes 1179656 | tf_op jit(solution)/shard_map/ppermute | solution.py:245
  6.5 1.5 %collective-permute-start.3 = (bf16[12,16,1024]{2,1,0:T(8,128)(2,1)S(1)}, bf16[12,16,1024]{2,1,0:T(8,128)(2,1)S(1)}, u32[]{:S(2)}, u32[]{:S(2)}) collective-permute-start(bf16[12,16,1024]{2,1,0:T(8,128)(2,1)S(1)} %get-tuple-element.43), channel_id=1, source_target_pairs={{0,192},{64,0},{128,64},{192,128},{1,193},{65,1},{129,65},{193,129... | collective-permute-start | bytes 1179656 | tf_op jit(solution)/shard_map/ppermute | solution.py:245
  8.0 1.6 %collective-permute-start.4 = (bf16[12,16,1024]{2,1,0:T(8,128)(2,1)S(1)}, bf16[12,16,1024]{2,1,0:T(8,128)(2,1)S(1)}, u32[]{:S(2)}, u32[]{:S(2)}) collective-permute-start(bf16[12,16,1024]{2,1,0:T(8,128)(2,1)S(1)} %get-tuple-element.44), channel_id=1, source_target_pairs={{0,128},{64,192},{128,0},{192,64},{1,129},{65,193},{129,1},{193,65... | collective-permute-start | bytes 1179656 | tf_op jit(solution)/shard_map/ppermute | solution.py:245
  9.6 1.2 copy-done.4
  10.8 2.2 %root_halves.1 = (bf16[8,256,128]{2,1,0:T(8,128)(2,1)S(1)}, bf16[8,256,128]{2,1,0:T(8,128)(2,1)S(1)}, bf16[8,256,128]{2,1,0:T(8,128)(2,1)S(1)}, bf16[8,256,128]{2,1,0:T(8,128)(2,1)S(1)}, s32[8]{0:T(128)S(1)}) custom-call(s32[48]{0:T(128)S(1)} %get-tuple-element.34.sorted_target, bf16[2,256,1024]{2,1,0:T(8,128)(2,1)S(1)} %copy-done.3, ...), custom_call_target="tpu_custom_call" | custom-call | tf_op jit(solution)/shard_map/root_halves/pallas_call | solution.py:261
  13.1 1.6 %collective-permute-start = (bf16[8,256,128]{2,1,0:T(8,128)(2,1)S(1)}, bf16[8,256,128]{2,1,0:T(8,128)(2,1)S(1)}, u32[]{:S(2)}, u32[]{:S(2)}) collective-permute-start(bf16[8,256,128]{2,1,0:T(8,128)(2,1)S(1)} %get-tuple-element.38), channel_id=1, source_target_pairs={{0,1},{1,0},{2,3},{3,2},{4,5},{5,4},{6,7},{7,6},{8,9},{9,8},{10,11... | collective-permute-start | bytes 1572872 | tf_op jit(solution)/shard_map/ppermute | solution.py:248
  15.9 10.2 %collective-permute-done.4.__0_ = bf16[12,16,1024]{2,1,0:T(8,128)(2,1)S(1)} collective-permute-done((bf16[12,16,1024]{2,1,0:T(8,128)(2,1)S(1)}, bf16[12,16,1024]{2,1,0:T(8,128)(2,1)S(1)}, u32[]{:S(2)}, u32[]{:S(2)}) %collective-permute-start.4) | collective-permute-done | bytes 393248 | tf_op jit(solution)/shard_map/ppermute | solution.py:245
  26.1 1.6 %roots_by_plane.1 = (bf16[8,256,128]{2,1,0:T(8,128)(2,1)S(1)}, bf16[8,256,128]{2,1,0:T(8,128)(2,1)S(1)}, bf16[8,256,128]{2,1,0:T(8,128)(2,1)}, bf16[8,256,128]{2,1,0:T(8,128)(2,1)S(1)}) custom-call(s32[8]{0:T(128)S(1)} %get-tuple-element.35.table, bf16[8,256,128]{2,1,0:T(8,128)(2,1)S(1)} %get-tuple-element.36.refs_0_, ...), custom_call_target="tpu_custom_call" | custom-call | tf_op jit(solution)/shard_map/roots_by_plane/pallas_call | solution.py:270
  27.6 1.8 %sum_and_place.1 = bf16[64,16,512]{2,1,0:T(8,128)(2,1)} custom-call(s32[48]{0:T(128)S(1)} %get-tuple-element.34.sorted_target, bf16[8,256,128]{2,1,0:T(8,128)(2,1)S(1)} %get-tuple-element.48._.refs_0_, bf16[12,16,1024]{2,1,0:T(8,128)(2,1)S(1)} %get-tuple-element.41.own, bf16[12,16,1024]{2,1,0:T(8,128)(2,1)S(1)} %settle.5.one, ...), custom_call_target="tpu_custom_call" | custom-call | bytes 3145728 | tf_op jit(solution)/shard_map/sum_and_place/pallas_call | solution.py:279
  29.6 13.6 %all-to-all-start = ((bf16[64,16,512]{2,1,0:T(8,128)(2,1)}), bf16[64,16,512]{2,1,0:T(8,128)(2,1)S(1)}, u32[]{:S(2)}, u32[]{:S(2)}) async-start(bf16[64,16,512]{2,1,0:T(8,128)(2,1)} %sum_and_place.1), calls=%async_computation | async-start | bytes 2097152 | tf_op jit(solution)/shard_map/all_to_all | solution.py:290
  43.2 1.8 %collective-permute-start.5 = (bf16[8,256,128]{2,1,0:T(8,128)(2,1)S(1)}, bf16[8,256,128]{2,1,0:T(8,128)(2,1)S(1)}, u32[]{:S(2)}, u32[]{:S(2)}) collective-permute-start(bf16[8,256,128]{2,1,0:T(8,128)(2,1)S(1)} %get-tuple-element.49), channel_id=1, source_target_pairs={{0,64},{64,128},{128,192},{192,0},{1,65},{65,129},{129,193},{193,1... | collective-permute-start | bytes 1572872 | tf_op jit(solution)/shard_map/ppermute | solution.py:245
  45.0 1.2 collective-permute-start.7
  46.1 11.6 %collective-permute-done.5.refs_1_ = bf16[8,256,128]{2,1,0:T(8,128)(2,1)S(1)} collective-permute-done((bf16[8,256,128]{2,1,0:T(8,128)(2,1)S(1)}, bf16[8,256,128]{2,1,0:T(8,128)(2,1)S(1)}, u32[]{:S(2)}, u32[]{:S(2)}) %collective-permute-start.5) | collective-permute-done | bytes 524320 | tf_op jit(solution)/shard_map/ppermute | solution.py:245
  59.1 1.6 %collective-permute-start.8 = (bf16[1024,512]{1,0:T(8,128)(2,1)S(1)}, bf16[1024,512]{1,0:T(8,128)(2,1)S(1)}, u32[]{:S(2)}, u32[]{:S(2)}) collective-permute-start(bf16[1024,512]{1,0:T(8,128)(2,1)S(1)} %get-tuple-element.52.l_own), channel_id=1, source_target_pairs={{0,1},{1,0},{2,3},{3,2},{4,5},{5,4},{6,7},{7,6},{8,9},{9,8},{10,11... | collective-permute-start | bytes 3145736 | tf_op jit(solution)/shard_map/ppermute | solution.py:248
  61.6 1.3 %collective-permute-done.8.__1_ = bf16[1024,512]{1,0:T(8,128)(2,1)S(1)} collective-permute-done((bf16[1024,512]{1,0:T(8,128)(2,1)S(1)}, bf16[1024,512]{1,0:T(8,128)(2,1)S(1)}, u32[]{:S(2)}, u32[]{:S(2)}) %collective-permute-start.8) | collective-permute-done | bytes 1048608 | tf_op jit(solution)/shard_map/ppermute | solution.py:248
  62.9 8.3 %all-to-all-done.__0_ = bf16[64,16,512]{2,1,0:T(8,128)(2,1)S(1)} async-done(((bf16[64,16,512]{2,1,0:T(8,128)(2,1)}), bf16[64,16,512]{2,1,0:T(8,128)(2,1)S(1)}, u32[]{:S(2)}, u32[]{:S(2)}) %all-to-all-start) | async-done | bytes 1048608 | tf_op jit(solution)/shard_map/all_to_all | solution.py:290
  71.2 1.4 %collective-permute-start.9 = (bf16[1024,512]{1,0:T(8,128)(2,1)S(1)}, bf16[1024,512]{1,0:T(8,128)(2,1)S(1)}, u32[]{:S(2)}, u32[]{:S(2)}) collective-permute-start(bf16[1024,512]{1,0:T(8,128)(2,1)S(1)} %bitcast.5), channel_id=1, source_target_pairs={{0,1},{1,0},{2,3},{3,2},{4,5},{5,4},{6,7},{7,6},{8,9},{9,8},{10,11... | collective-permute-start | bytes 3145736 | tf_op jit(solution)/shard_map/ppermute | solution.py:248
  72.6 2.3 %collective-permute-done.9.s_far = bf16[1024,512]{1,0:T(8,128)(2,1)S(1)} collective-permute-done((bf16[1024,512]{1,0:T(8,128)(2,1)S(1)}, bf16[1024,512]{1,0:T(8,128)(2,1)S(1)}, u32[]{:S(2)}, u32[]{:S(2)}) %collective-permute-start.9) | collective-permute-done | bytes 1048608 | tf_op jit(solution)/shard_map/ppermute | solution.py:248
  74.9 3.0 %gram.1 = (bf16[2,256,512]{2,1,0:T(8,128)(2,1)S(1)}, bf16[2,256,512]{2,1,0:T(8,128)(2,1)S(1)}, bf16[2,256,512]{2,1,0:T(8,128)(2,1)}, bf16[2,256,512]{2,1,0:T(8,128)(2,1)S(1)}) custom-call(bf16[1024,512]{1,0:T(8,128)(2,1)S(1)} %bitcast.6, bf16[1024,512]{1,0:T(8,128)(2,1)S(1)} %collective-permute-done.9.s_far), custom_call_target="tpu_custom_call" | custom-call | flops 2147483648 | bytes 4194304 | tf_op jit(solution)/shard_map/gram/pallas_call | solution.py:305
  79.4 2.5 %collective-permute-start.10 = (bf16[2,256,512]{2,1,0:T(8,128)(2,1)}, bf16[2,256,512]{2,1,0:T(8,128)(2,1)S(1)}, u32[]{:S(2)}, u32[]{:S(2)}) collective-permute-start(bf16[2,256,512]{2,1,0:T(8,128)(2,1)} %get-tuple-element.54), channel_id=1, source_target_pairs={{0,128},{64,192},{128,0},{192,64},{1,129},{65,193},{129,1},{193,65... | collective-permute-start | bytes 1572872 | tf_op jit(solution)/shard_map/ppermute | solution.py:245
  81.9 3.5 %update_block.1 = bf16[4,64,16,128]{3,2,1,0:T(8,128)(2,1)} custom-call(bf16[1024,512]{1,0:T(8,128)(2,1)S(1)} %bitcast.7, bf16[1024,512]{1,0:T(8,128)(2,1)S(1)} %collective-permute-done.9.s_far, bf16[1024,512]{1,0:T(8,128)(2,1)S(1)} %copy-done.6, bf16[1024,512]{1,0:T(8,128)(2,1)S(1)} %get-tuple-element.63.l_far, bf16[1024,512]{1,0:T(8,128)(2,1)S(1)} %copy-done.8), custom_call_target="tpu_custom_call" | custom-call | flops 2147483648 | bytes 6291456 | tf_op jit(solution)/shard_map/update_block/pallas_call | solution.py:315
  85.3 7.1 %all-to-all-start.1 = ((bf16[256,16,128]{2,1,0:T(8,128)(2,1)}), bf16[256,16,128]{2,1,0:T(8,128)(2,1)S(1)}, u32[]{:S(2)}, u32[]{:S(2)}) async-start(bf16[256,16,128]{2,1,0:T(8,128)(2,1)} %bitcast.2), calls=%async_computation.1 | async-start | bytes 2097152 | tf_op jit(solution)/shard_map/all_to_all | solution.py:326
  92.5 1.5 %collective-permute-start.11 = (bf16[2,256,512]{2,1,0:T(8,128)(2,1)S(1)}, bf16[2,256,512]{2,1,0:T(8,128)(2,1)S(1)}, u32[]{:S(2)}, u32[]{:S(2)}) collective-permute-start(bf16[2,256,512]{2,1,0:T(8,128)(2,1)S(1)} %copy-done.12), channel_id=1, source_target_pairs={{0,64},{64,128},{128,192},{192,0},{1,65},{65,129},{129,193},{193,1... | collective-permute-start | bytes 1572872 | tf_op jit(solution)/shard_map/ppermute | solution.py:245
  94.0 1.4 %collective-permute-start.12 = (bf16[2,256,512]{2,1,0:T(8,128)(2,1)S(1)}, bf16[2,256,512]{2,1,0:T(8,128)(2,1)S(1)}, u32[]{:S(2)}, u32[]{:S(2)}) collective-permute-start(bf16[2,256,512]{2,1,0:T(8,128)(2,1)S(1)} %copy-done.10), channel_id=1, source_target_pairs={{0,192},{64,0},{128,64},{192,128},{1,193},{65,1},{129,65},{193,129... | collective-permute-start | bytes 1572872 | tf_op jit(solution)/shard_map/ppermute | solution.py:245
  95.3 2.6 %collective-permute-start.13 = (bf16[2,256,512]{2,1,0:T(8,128)(2,1)S(1)}, bf16[2,256,512]{2,1,0:T(8,128)(2,1)S(1)}, u32[]{:S(2)}, u32[]{:S(2)}) collective-permute-start(bf16[2,256,512]{2,1,0:T(8,128)(2,1)S(1)} %get-tuple-element.57.rest_0_), channel_id=1, source_target_pairs={{0,1},{1,0},{2,3},{3,2},{4,5},{5,4},{6,7},{7,6},{8,9},{9,8},{10,11... | collective-permute-start | bytes 1572872 | tf_op jit(solution)/shard_map/ppermute | solution.py:248
  98.1 15.9 %collective-permute-done.11.rest_1_ = bf16[2,256,512]{2,1,0:T(8,128)(2,1)S(1)} collective-permute-done((bf16[2,256,512]{2,1,0:T(8,128)(2,1)S(1)}, bf16[2,256,512]{2,1,0:T(8,128)(2,1)S(1)}, u32[]{:S(2)}, u32[]{:S(2)}) %collective-permute-start.11) | collective-permute-done | bytes 524320 | tf_op jit(solution)/shard_map/ppermute | solution.py:245
  114.0 2.7 %collective-permute-start.14 = (bf16[2,256,512]{2,1,0:T(8,128)(2,1)S(1)}, bf16[2,256,512]{2,1,0:T(8,128)(2,1)S(1)}, u32[]{:S(2)}, u32[]{:S(2)}) collective-permute-start(bf16[2,256,512]{2,1,0:T(8,128)(2,1)S(1)} %collective-permute-done.11.rest_1_), channel_id=1, source_target_pairs={{0,1},{1,0},{2,3},{3,2},{4,5},{5,4},{6,7},{7,6},{8,9},{9,8},{10,11... | collective-permute-start | bytes 1572872 | tf_op jit(solution)/shard_map/ppermute | solution.py:248
  119.0 3.1 %statistics.1 = (f32[2,256,1024]{2,1,0:T(8,128)}, f32[2,256,1024]{2,1,0:T(8,128)}) custom-call(s32[8]{0:T(128)S(1)} %get-tuple-element.35.table, f32[2,256,1024]{2,1,0:T(8,128)S(1)} %get-tuple-element.55.left, f32[2,256,1024]{2,1,0:T(8,128)S(1)} %get-tuple-element.56.right, bf16[2,256,512]{2,1,0:T(8,128)(2,1)S(1)} %get-tuple-element.57.rest_0_, ...), custom_call_target="tpu_custom_call" | custom-call | bytes 8388608 | tf_op jit(solution)/shard_map/statistics/pallas_call | solution.py:348
  122.0 1.6 %all-to-all-done.1 = bf16[256,16,128]{2,1,0:T(8,128)(2,1)S(1)} async-done(((bf16[256,16,128]{2,1,0:T(8,128)(2,1)}), bf16[256,16,128]{2,1,0:T(8,128)(2,1)S(1)}, u32[]{:S(2)}, u32[]{:S(2)}) %all-to-all-start.1) | async-done | bytes 1048608 | tf_op jit(solution)/shard_map/all_to_all | solution.py:326
  123.6 1.6 %pick.1 = bf16[48,16,256]{2,1,0:T(8,128)(2,1)} custom-call(s32[48]{0:T(128)S(1)} %get-tuple-element.62.order, s32[48]{0:T(128)S(1)} %get-tuple-element.34.sorted_target, bf16[4,32,2,16,128]{4,3,2,1,0:T(8,128)(2,1)S(1)} %bitcast.4), custom_call_target="tpu_custom_call" | custom-call | bytes 2097152 | tf_op jit(solution)/shard_map/pick/pallas_call | solution.py:327
  (50 shorter events, 8.6 us)
Async XLA Ops:
  1.5 1.4 %copy-start.2 = (bf16[1,48,16,1024]{3,2,1,0:T(8,128)(2,1)S(1)}, bf16[1,48,16,1024]{3,2,1,0:T(8,128)(2,1)}, u32[]{:S(2)}) copy-start(bf16[1,48,16,1024]{3,2,1,0:T(8,128)(2,1)} %param.7) | copy-start | bytes 4718596
  2.9 6.7 %copy-start.3 = (bf16[2,256,1024]{2,1,0:T(8,128)(2,1)S(1)}, bf16[2,256,1024]{2,1,0:T(8,128)(2,1)}, u32[]{:S(2)}) copy-start(bf16[2,256,1024]{2,1,0:T(8,128)(2,1)} %left.1) | copy-start | bytes 3145732
  4.3 10.5 %collective-permute-start.2 = (bf16[12,16,1024]{2,1,0:T(8,128)(2,1)S(1)}, bf16[12,16,1024]{2,1,0:T(8,128)(2,1)S(1)}, u32[]{:S(2)}, u32[]{:S(2)}) collective-permute-start(bf16[12,16,1024]{2,1,0:T(8,128)(2,1)S(1)} %get-tuple-element.42), channel_id=1, source_target_pairs={{0,64},{64,128},{128,192},{192,0},{1,65},{65,129},{129,193},{193,1... | collective-permute-start | bytes 1179656 | tf_op jit(solution)/shard_map/ppermute | solution.py:245
  6.5 9.4 %collective-permute-start.3 = (bf16[12,16,1024]{2,1,0:T(8,128)(2,1)S(1)}, bf16[12,16,1024]{2,1,0:T(8,128)(2,1)S(1)}, u32[]{:S(2)}, u32[]{:S(2)}) collective-permute-start(bf16[12,16,1024]{2,1,0:T(8,128)(2,1)S(1)} %get-tuple-element.43), channel_id=1, source_target_pairs={{0,192},{64,0},{128,64},{192,128},{1,193},{65,1},{129,65},{193,129... | collective-permute-start | bytes 1179656 | tf_op jit(solution)/shard_map/ppermute | solution.py:245
  8.0 18.0 %collective-permute-start.4 = (bf16[12,16,1024]{2,1,0:T(8,128)(2,1)S(1)}, bf16[12,16,1024]{2,1,0:T(8,128)(2,1)S(1)}, u32[]{:S(2)}, u32[]{:S(2)}) collective-permute-start(bf16[12,16,1024]{2,1,0:T(8,128)(2,1)S(1)} %get-tuple-element.44), channel_id=1, source_target_pairs={{0,128},{64,192},{128,0},{192,64},{1,129},{65,193},{129,1},{193,65... | collective-permute-start | bytes 1179656 | tf_op jit(solution)/shard_map/ppermute | solution.py:245
  9.6 1.2 copy-start.4
  13.1 13.0 %collective-permute-start = (bf16[8,256,128]{2,1,0:T(8,128)(2,1)S(1)}, bf16[8,256,128]{2,1,0:T(8,128)(2,1)S(1)}, u32[]{:S(2)}, u32[]{:S(2)}) collective-permute-start(bf16[8,256,128]{2,1,0:T(8,128)(2,1)S(1)} %get-tuple-element.38), channel_id=1, source_target_pairs={{0,1},{1,0},{2,3},{3,2},{4,5},{5,4},{6,7},{7,6},{8,9},{9,8},{10,11... | collective-permute-start | bytes 1572872 | tf_op jit(solution)/shard_map/ppermute | solution.py:248
  14.7 11.4 %collective-permute-start.1 = (bf16[8,256,128]{2,1,0:T(8,128)(2,1)S(1)}, bf16[8,256,128]{2,1,0:T(8,128)(2,1)S(1)}, u32[]{:S(2)}, u32[]{:S(2)}) collective-permute-start(bf16[8,256,128]{2,1,0:T(8,128)(2,1)S(1)} %get-tuple-element.39), channel_id=1, source_target_pairs={{0,1},{1,0},{2,3},{3,2},{4,5},{5,4},{6,7},{7,6},{8,9},{9,8},{10,11... | collective-permute-start | bytes 1572872 | tf_op jit(solution)/shard_map/ppermute | solution.py:248
  29.4 16.7 %collective-permute-start.6 = (bf16[8,256,128]{2,1,0:T(8,128)(2,1)}, bf16[8,256,128]{2,1,0:T(8,128)(2,1)S(1)}, u32[]{:S(2)}, u32[]{:S(2)}) collective-permute-start(bf16[8,256,128]{2,1,0:T(8,128)(2,1)} %get-tuple-element.50), channel_id=1, source_target_pairs={{0,128},{64,192},{128,0},{192,64},{1,129},{65,193},{129,1},{193,65... | collective-permute-start | bytes 1572872 | tf_op jit(solution)/shard_map/ppermute | solution.py:245
  29.6 41.6 %all-to-all-start = ((bf16[64,16,512]{2,1,0:T(8,128)(2,1)}), bf16[64,16,512]{2,1,0:T(8,128)(2,1)S(1)}, u32[]{:S(2)}, u32[]{:S(2)}) async-start(bf16[64,16,512]{2,1,0:T(8,128)(2,1)} %sum_and_place.1), calls=%async_computation | async-start | bytes 2097152 | tf_op jit(solution)/shard_map/all_to_all | solution.py:290
  43.2 14.5 %collective-permute-start.5 = (bf16[8,256,128]{2,1,0:T(8,128)(2,1)S(1)}, bf16[8,256,128]{2,1,0:T(8,128)(2,1)S(1)}, u32[]{:S(2)}, u32[]{:S(2)}) collective-permute-start(bf16[8,256,128]{2,1,0:T(8,128)(2,1)S(1)} %get-tuple-element.49), channel_id=1, source_target_pairs={{0,64},{64,128},{128,192},{192,0},{1,65},{65,129},{129,193},{193,1... | collective-permute-start | bytes 1572872 | tf_op jit(solution)/shard_map/ppermute | solution.py:245
  45.0 12.8 %collective-permute-start.7 = (bf16[8,256,128]{2,1,0:T(8,128)(2,1)S(1)}, bf16[8,256,128]{2,1,0:T(8,128)(2,1)S(1)}, u32[]{:S(2)}, u32[]{:S(2)}) collective-permute-start(bf16[8,256,128]{2,1,0:T(8,128)(2,1)S(1)} %get-tuple-element.51), channel_id=1, source_target_pairs={{0,192},{64,0},{128,64},{192,128},{1,193},{65,1},{129,65},{193,129... | collective-permute-start | bytes 1572872 | tf_op jit(solution)/shard_map/ppermute | solution.py:245
  58.1 1.0 copy-start.7
  59.1 3.9 %collective-permute-start.8 = (bf16[1024,512]{1,0:T(8,128)(2,1)S(1)}, bf16[1024,512]{1,0:T(8,128)(2,1)S(1)}, u32[]{:S(2)}, u32[]{:S(2)}) collective-permute-start(bf16[1024,512]{1,0:T(8,128)(2,1)S(1)} %get-tuple-element.52.l_own), channel_id=1, source_target_pairs={{0,1},{1,0},{2,3},{3,2},{4,5},{5,4},{6,7},{7,6},{8,9},{9,8},{10,11... | collective-permute-start | bytes 3145736 | tf_op jit(solution)/shard_map/ppermute | solution.py:248
  60.7 1.0 copy-start.5
  71.2 10.7 %copy-start.6 = (bf16[1024,512]{1,0:T(8,128)(2,1)S(1)}, bf16[1024,512]{1,0:T(8,128)(2,1)}, u32[]{:S(2)}) copy-start(bf16[1024,512]{1,0:T(8,128)(2,1)} %copy-done.5) | copy-start | bytes 3145732
  71.2 10.7 %copy-start.8 = (bf16[1024,512]{1,0:T(8,128)(2,1)S(1)}, bf16[1024,512]{1,0:T(8,128)(2,1)}, u32[]{:S(2)}) copy-start(bf16[1024,512]{1,0:T(8,128)(2,1)} %copy-done.7) | copy-start | bytes 3145732
  71.2 3.6 %collective-permute-start.9 = (bf16[1024,512]{1,0:T(8,128)(2,1)S(1)}, bf16[1024,512]{1,0:T(8,128)(2,1)S(1)}, u32[]{:S(2)}, u32[]{:S(2)}) collective-permute-start(bf16[1024,512]{1,0:T(8,128)(2,1)S(1)} %bitcast.5), channel_id=1, source_target_pairs={{0,1},{1,0},{2,3},{3,2},{4,5},{5,4},{6,7},{7,6},{8,9},{9,8},{10,11... | collective-permute-start | bytes 3145736 | tf_op jit(solution)/shard_map/ppermute | solution.py:248
  77.8 0.8 copy-start.9
  78.6 0.8 copy-start.11
  79.4 18.6 %collective-permute-start.10 = (bf16[2,256,512]{2,1,0:T(8,128)(2,1)}, bf16[2,256,512]{2,1,0:T(8,128)(2,1)S(1)}, u32[]{:S(2)}, u32[]{:S(2)}) collective-permute-start(bf16[2,256,512]{2,1,0:T(8,128)(2,1)} %get-tuple-element.54), channel_id=1, source_target_pairs={{0,128},{64,192},{128,0},{192,64},{1,129},{65,193},{129,1},{193,65... | collective-permute-start | bytes 1572872 | tf_op jit(solution)/shard_map/ppermute | solution.py:245
  85.3 7.2 %copy-start.12 = (bf16[2,256,512]{2,1,0:T(8,128)(2,1)S(1)}, bf16[2,256,512]{2,1,0:T(8,128)(2,1)}, u32[]{:S(2)}) copy-start(bf16[2,256,512]{2,1,0:T(8,128)(2,1)} %copy-done.11) | copy-start | bytes 1572868
  85.3 8.6 %copy-start.10 = (bf16[2,256,512]{2,1,0:T(8,128)(2,1)S(1)}, bf16[2,256,512]{2,1,0:T(8,128)(2,1)}, u32[]{:S(2)}) copy-start(bf16[2,256,512]{2,1,0:T(8,128)(2,1)} %copy-done.9) | copy-start | bytes 1572868
  85.3 38.2 %all-to-all-start.1 = ((bf16[256,16,128]{2,1,0:T(8,128)(2,1)}), bf16[256,16,128]{2,1,0:T(8,128)(2,1)S(1)}, u32[]{:S(2)}, u32[]{:S(2)}) async-start(bf16[256,16,128]{2,1,0:T(8,128)(2,1)} %bitcast.2), calls=%async_computation.1 | async-start | bytes 2097152 | tf_op jit(solution)/shard_map/all_to_all | solution.py:326
  92.5 21.5 %collective-permute-start.11 = (bf16[2,256,512]{2,1,0:T(8,128)(2,1)S(1)}, bf16[2,256,512]{2,1,0:T(8,128)(2,1)S(1)}, u32[]{:S(2)}, u32[]{:S(2)}) collective-permute-start(bf16[2,256,512]{2,1,0:T(8,128)(2,1)S(1)} %copy-done.12), channel_id=1, source_target_pairs={{0,64},{64,128},{128,192},{192,0},{1,65},{65,129},{129,193},{193,1... | collective-permute-start | bytes 1572872 | tf_op jit(solution)/shard_map/ppermute | solution.py:245
  94.0 22.7 %collective-permute-start.12 = (bf16[2,256,512]{2,1,0:T(8,128)(2,1)S(1)}, bf16[2,256,512]{2,1,0:T(8,128)(2,1)S(1)}, u32[]{:S(2)}, u32[]{:S(2)}) collective-permute-start(bf16[2,256,512]{2,1,0:T(8,128)(2,1)S(1)} %copy-done.10), channel_id=1, source_target_pairs={{0,192},{64,0},{128,64},{192,128},{1,193},{65,1},{129,65},{193,129... | collective-permute-start | bytes 1572872 | tf_op jit(solution)/shard_map/ppermute | solution.py:245
  95.3 21.6 %copy-start = (f32[2,256,1024]{2,1,0:T(8,128)S(1)}, f32[2,256,1024]{2,1,0:T(8,128)}, u32[]{:S(2)}) copy-start(f32[2,256,1024]{2,1,0:T(8,128)} %stat_left.1) | copy-start | bytes 6291460
  95.3 21.6 %copy-start.1 = (f32[2,256,1024]{2,1,0:T(8,128)S(1)}, f32[2,256,1024]{2,1,0:T(8,128)}, u32[]{:S(2)}) copy-start(f32[2,256,1024]{2,1,0:T(8,128)} %stat_right.1) | copy-start | bytes 6291460
  95.3 21.9 %collective-permute-start.13 = (bf16[2,256,512]{2,1,0:T(8,128)(2,1)S(1)}, bf16[2,256,512]{2,1,0:T(8,128)(2,1)S(1)}, u32[]{:S(2)}, u32[]{:S(2)}) collective-permute-start(bf16[2,256,512]{2,1,0:T(8,128)(2,1)S(1)} %get-tuple-element.57.rest_0_), channel_id=1, source_target_pairs={{0,1},{1,0},{2,3},{3,2},{4,5},{5,4},{6,7},{7,6},{8,9},{9,8},{10,11... | collective-permute-start | bytes 1572872 | tf_op jit(solution)/shard_map/ppermute | solution.py:248
  98.0 19.3 %collective-permute-start.15 = (bf16[2,256,512]{2,1,0:T(8,128)(2,1)S(1)}, bf16[2,256,512]{2,1,0:T(8,128)(2,1)S(1)}, u32[]{:S(2)}, u32[]{:S(2)}) collective-permute-start(bf16[2,256,512]{2,1,0:T(8,128)(2,1)S(1)} %settle.9._.rest_2_), channel_id=1, source_target_pairs={{0,1},{1,0},{2,3},{3,2},{4,5},{5,4},{6,7},{7,6},{8,9},{9,8},{10,11... | collective-permute-start | bytes 1572872 | tf_op jit(solution)/shard_map/ppermute | solution.py:248
  114.0 4.2 %collective-permute-start.14 = (bf16[2,256,512]{2,1,0:T(8,128)(2,1)S(1)}, bf16[2,256,512]{2,1,0:T(8,128)(2,1)S(1)}, u32[]{:S(2)}, u32[]{:S(2)}) collective-permute-start(bf16[2,256,512]{2,1,0:T(8,128)(2,1)S(1)} %collective-permute-done.11.rest_1_), channel_id=1, source_target_pairs={{0,1},{1,0},{2,3},{3,2},{4,5},{5,4},{6,7},{7,6},{8,9},{9,8},{10,11... | collective-permute-start | bytes 1572872 | tf_op jit(solution)/shard_map/ppermute | solution.py:248
  116.7 2.3 %collective-permute-start.16 = (bf16[2,256,512]{2,1,0:T(8,128)(2,1)S(1)}, bf16[2,256,512]{2,1,0:T(8,128)(2,1)S(1)}, u32[]{:S(2)}, u32[]{:S(2)}) collective-permute-start(bf16[2,256,512]{2,1,0:T(8,128)(2,1)S(1)} %collective-permute-done.12.rest_3_), channel_id=1, source_target_pairs={{0,1},{1,0},{2,3},{3,2},{4,5},{5,4},{6,7},{7,6},{8,9},{9,8},{10,11... | collective-permute-start | bytes 1572872 | tf_op jit(solution)/shard_map/ppermute | solution.py:248

commit v4 on v3

--- a/solution.py
+++ b/solution.py
@@ -61,14 +61,11 @@
 
 def sum_and_place(sorted_target, _, own, one, two, three, out):
     r, _, _ = my_place()
-    half = out.shape[2]
     out[...] = jnp.zeros_like(out)
     for j in range(own.shape[0]):
         chip = sorted_target[PLANES * j + r] // (CORES * SLOTS)
         total = own[j].astype(F32) + one[j].astype(F32) + two[j].astype(F32) + three[j].astype(F32)
-        total = total.astype(BF16)
-        for h in range(CORES):
-            out[CORES * chip + h] = total[:, h * half : (h + 1) * half]
+        out[chip] = total.astype(BF16)
 
 
 def root_halves(sorted_target, left, right, *outs):
@@ -148,14 +145,31 @@
     )(x, y)
 
 
-def update_block(s_own, s_far, l_own, l_far, r_cols, out, half):
+def gram(s_own, s_far, *outs):
+    grams, block = outs[:PLANES], outs[PLANES]
+    r, _, c = my_place()
+    for i in range(s_own.shape[0]):
+        block[pl.ds(pl.multiple_of(32 * i + 16 * c, 16), 16), :] = s_own[i]
+        block[pl.ds(pl.multiple_of(32 * i + 16 * (1 - c), 16), 16), :] = s_far[i]
+    near = pl.ds(pl.multiple_of(c * 512, 512), 512)
+    across_rows = (((1,), (1,)), ((), ()))
+    across_columns = (((0,), (0,)), ((), ()))
+    for k in range(PLANES):
+        plane = (r + k) % PLANES
+        strip = pl.ds(pl.multiple_of(plane * 256, 256), 256)
+        left = lax.dot_general(block[strip, :], block[near, :], across_rows, preferred_element_type=F32)
+        grams[k][0] = (left / 1024).astype(BF16)
+        right = lax.dot_general(block[:, strip], block[:, near], across_columns, preferred_element_type=F32)
+        grams[k][1] = (right / 1024).astype(BF16)
+
+
+def update_block(block, l_own, l_far, r_cols, out, half):
     r, _, c = my_place()
     near = pl.ds(pl.multiple_of(c * 512, 512), 512)
     far = pl.ds(pl.multiple_of((1 - c) * 512, 512), 512)
     for m in range(4):
         rows = slice(256 * m, 256 * (m + 1))
-        total = jnp.dot(s_own[rows, :], r_cols[near, :], preferred_element_type=F32)
-        total += jnp.dot(s_far[rows, :], r_cols[far, :], preferred_element_type=F32)
+        total = jnp.dot(block[rows, :], r_cols[...], preferred_element_type=F32)
         half[rows, :] = total.astype(BF16)
     for k in range(PLANES):
         rows = slice(256 * k, 256 * (k + 1))
@@ -163,30 +177,10 @@
         total = jnp.dot(l_own[rows, :], half[near, :], preferred_element_type=F32)
         total += jnp.dot(l_far[rows, :], half[far, :], preferred_element_type=F32)
         total = total.astype(BF16)
-        if len(out.shape) == 3:
-            out[pl.ds(16 * source, 16)] = total.reshape(16, 16, 512)
-        else:
-            for kk in range(PLANES):
-                plane = (r - kk + PLANES) % PLANES
-                part = total[:, 128 * kk : 128 * (kk + 1)].reshape(16, 16, 128)
-                out[plane, pl.ds(16 * source, 16)] = part
-
-
-def gram(s_own, s_far, *grams):
-    r, _, c = my_place()
-    near = pl.ds(pl.multiple_of(c * 512, 512), 512)
-    across_rows = (((1,), (1,)), ((), ()))
-    across_columns = (((0,), (0,)), ((), ()))
-    for k in range(PLANES):
-        plane = (r + k) % PLANES
-        rows = pl.ds(pl.multiple_of(plane * 256, 256), 256)
-        left = lax.dot_general(s_own[rows, :], s_own[near, :], across_rows, preferred_element_type=F32)
-        left += lax.dot_general(s_far[rows, :], s_far[near, :], across_rows, preferred_element_type=F32)
-        grams[k][0] = (left / 1024).astype(BF16)
-        columns = pl.ds(pl.multiple_of((plane % 2) * 256, 256), 256)
-        strip = jnp.where(plane // 2 == c, s_own[:, columns], s_far[:, columns])
-        right = lax.dot_general(strip, s_own[...], across_columns, preferred_element_type=F32)
-        grams[k][1] = (right / 1024).astype(BF16)
+        for kk in range(PLANES):
+            plane = (r - kk + PLANES) % PLANES
+            part = total[:, 128 * kk : 128 * (kk + 1)].reshape(16, 16, 128)
+            out[plane, pl.ds(16 * source, 16)] = part
 
 
 def preload(_, stat_left, stat_right, left, right, sems):
@@ -279,7 +273,7 @@
     outgoing = call(
         sum_and_place,
         "sum_and_place",
-        like((fsdp_count, rows, width // CORES)),
+        like((fsdp_count // CORES, rows, width)),
         [SMEM, ANY] + [VMEM] * PLANES,
         VMEM,
         [],
@@ -287,7 +281,10 @@
     )(sorted_target, roots[0], *summands)
     roots, _ = lax.optimization_barrier((roots, outgoing))
     first = settle(along(roots[2], 2), ROOT_HINT)
-    arrived = lax.all_to_all(outgoing, "fsdp", split_axis=0, concat_axis=0, tiled=True)
+    same_core = [list(range(c, fsdp_count, CORES)) for c in range(CORES)]
+    arrived = lax.all_to_all(
+        outgoing, "fsdp", split_axis=0, concat_axis=0, tiled=True, axis_index_groups=same_core
+    )
 
     roots = [roots[0], along(roots[1], 1), first, along(roots[3], 3)]
     l_own, r_cols = call(
@@ -300,14 +297,14 @@
     )(*roots)
 
     arrived, l_far = together(arrived, across(l_own))
-    s_own = arrived.reshape(width, width // CORES)
+    s_own = arrived
     s_far = across(s_own)
-    grams = call(
+    *grams, block = call(
         gram,
         "gram",
-        [like((2, 256, 512))] * PLANES,
+        [like((2, 256, 512))] * PLANES + [like((width, width))],
         [VMEM] * 2,
-        [VMEM] * PLANES,
+        [VMEM] * (PLANES + 1),
         [],
         flops=4 * 1024 * 1024 * 512,
         nbytes=4 << 20,
@@ -316,12 +313,12 @@
         update_block,
         "update_block",
         like((PLANES, fsdp_count, rows, 128)),
-        [VMEM] * 5,
+        [VMEM] * 4,
         VMEM,
         [pltpu.VMEM((width, 512), BF16)],
         flops=4 * 1024 * 1024 * 512,
         nbytes=6 << 20,
-    )(s_own, s_far, l_own, l_far, r_cols)
+    )(block, l_own, l_far, r_cols)
     update = update.reshape(PLANES * fsdp_count, rows, 128)
     returned = lax.all_to_all(update, ("replica", "fsdp"), split_axis=0, concat_axis=0, tiled=True)
     new = call(

time: 125 us -> 121 us (0.968)
  waiting for transfers between devices: 53.9 us -> 49.6 us
  starting transfers between devices: 44.8 us -> 46.5 us
  local copies, waits for them, and re-layouts: 6.19 us -> 4.59 us
    ppermute x8, starting transfers between devices: 10.4 us -> 14.5 us  [across(): return lax.ppermute(x, 'fsdp', [(i, i ^ 1) for i in range(fsdp_count)])]
    all_to_all x1, waiting for transfers between devices: 8.26 us -> 5.34 us  [per_device(): lax.all_to_all(outgoing, 'fsdp', split_axis=0, concat_axis=0, tiled=True,...]
    all_to_all x1, starting transfers between devices: 13.6 us -> 11.2 us  [per_device(): lax.all_to_all(outgoing, 'fsdp', split_axis=0, concat_axis=0, tiled=True,...]
    unnamed x26 -> x22, local copies, waits for them, and re-layouts: 6.19 us -> 4.59 us
    ppermute x9, waiting for transfers between devices: 38.8 us -> 37.4 us  [along(): lax.ppermute(x, 'replica', [(i, (i + step) % PLANES) for i in range(PLANE...]
where the time goes in v4:
time: 121 us
  waiting for transfers between devices  49.6 us (41%)
  starting transfers between devices  46.5 us (38%)
  Pallas kernels  18.6 us (15%)
  local copies, waits for them, and re-layouts  4.59 us (4%)
    ppermute x9, waiting for transfers between devices, along(): lax.ppermute(x, 'replica', [(i, (i + step) % PLANES) for i in range(PLANE...  37.4 us
    ppermute x8, starting transfers between devices, across(): return lax.ppermute(x, 'fsdp', [(i, i ^ 1) for i in range(fsdp_count)])  14.5 us
    ppermute x9, starting transfers between devices, along(): lax.ppermute(x, 'replica', [(i, (i + step) % PLANES) for i in range(PLANE...  13.7 us
    all_to_all x1, starting transfers between devices, per_device(): lax.all_to_all(outgoing, 'fsdp', split_axis=0, concat_axis=0, tiled=True,...  11.2 us
    all_to_all x1, starting transfers between devices, per_device(): lax.all_to_all(update, ('replica', 'fsdp'), split_axis=0, concat_axis=0,...  7.12 us
    all_to_all x1, waiting for transfers between devices, per_device(): lax.all_to_all(outgoing, 'fsdp', split_axis=0, concat_axis=0, tiled=True,...  5.34 us
    ppermute x8, waiting for transfers between devices, across(): return lax.ppermute(x, 'fsdp', [(i, i ^ 1) for i in range(fsdp_count)])  5.27 us
    unnamed x22, local copies, waits for them, and re-layouts  4.59 us
  transfers between devices with their start and end apart: 19, of which 10 were waited for; matrix products, arithmetic and copies ran while one was open for 0% of the time, Pallas kernels for 8%

profile of v4, /device:TPU:1, one launch (start us, length us, event | category | flops | bytes accessed | tf_op | source)
XLA Modules:
  0.0 120.8 jit_solution(10276427430465308798)
XLA Ops:
  1.5 1.4 %copy-done.2 = bf16[1,48,16,1024]{3,2,1,0:T(8,128)(2,1)S(1)} copy-done((bf16[1,48,16,1024]{3,2,1,0:T(8,128)(2,1)S(1)}, bf16[1,48,16,1024]{3,2,1,0:T(8,128)(2,1)}, u32[]{:S(2)}) %copy-start.2) | copy-done | bytes 1572888
  2.9 1.4 %by_plane.1 = (s32[48]{0:T(128)S(1)}, s32[48]{0:T(128)S(1)}, bf16[12,16,1024]{2,1,0:T(8,128)(2,1)S(1)}, bf16[12,16,1024]{2,1,0:T(8,128)(2,1)S(1)}, bf16[12,16,10...) custom-call(s32[48]{0:T(128)S(1)} %convert_reduce_fusion.rank, s32[48]{0:T(128)S(1)} %multiply_add_fusion.target, ...), custom_call_target="tpu_custom_call" | custom-call | bytes 3145728 | tf_op jit(solution)/shard_map/by_plane/pallas_call | solution.py:244
  4.3 2.2 %collective-permute-start.2 = (bf16[12,16,1024]{2,1,0:T(8,128)(2,1)S(1)}, bf16[12,16,1024]{2,1,0:T(8,128)(2,1)S(1)}, u32[]{:S(2)}, u32[]{:S(2)}) collective-permute-start(bf16[12,16,1024]{2,1,0:T(8,128)(2,1)S(1)} %get-tuple-element.43), channel_id=1, source_target_pairs={{0,64},{64,128},{128,192},{192,0},{1,65},{65,129},{129,193},{193,1... | collective-permute-start | bytes 1179656 | tf_op jit(solution)/shard_map/ppermute | solution.py:239
  6.5 1.5 %collective-permute-start.3 = (bf16[12,16,1024]{2,1,0:T(8,128)(2,1)S(1)}, bf16[12,16,1024]{2,1,0:T(8,128)(2,1)S(1)}, u32[]{:S(2)}, u32[]{:S(2)}) collective-permute-start(bf16[12,16,1024]{2,1,0:T(8,128)(2,1)S(1)} %get-tuple-element.44), channel_id=1, source_target_pairs={{0,192},{64,0},{128,64},{192,128},{1,193},{65,1},{129,65},{193,129... | collective-permute-start | bytes 1179656 | tf_op jit(solution)/shard_map/ppermute | solution.py:239
  8.0 1.6 %collective-permute-start.4 = (bf16[12,16,1024]{2,1,0:T(8,128)(2,1)S(1)}, bf16[12,16,1024]{2,1,0:T(8,128)(2,1)S(1)}, u32[]{:S(2)}, u32[]{:S(2)}) collective-permute-start(bf16[12,16,1024]{2,1,0:T(8,128)(2,1)S(1)} %get-tuple-element.45), channel_id=1, source_target_pairs={{0,128},{64,192},{128,0},{192,64},{1,129},{65,193},{129,1},{193,65... | collective-permute-start | bytes 1179656 | tf_op jit(solution)/shard_map/ppermute | solution.py:239
  9.6 1.2 %copy-done.4 = bf16[2,1024,256]{2,1,0:T(8,128)(2,1)S(1)} copy-done((bf16[2,1024,256]{2,1,0:T(8,128)(2,1)S(1)}, bf16[2,1024,256]{2,1,0:T(8,128)(2,1)}, u32[]{:S(2)}) %copy-start.4) | copy-done | bytes 1048600
  10.8 2.2 %root_halves.1 = (bf16[8,256,128]{2,1,0:T(8,128)(2,1)S(1)}, bf16[8,256,128]{2,1,0:T(8,128)(2,1)S(1)}, bf16[8,256,128]{2,1,0:T(8,128)(2,1)S(1)}, bf16[8,256,128]{2,1,0:T(8,128)(2,1)S(1)}, s32[8]{0:T(128)S(1)}) custom-call(s32[48]{0:T(128)S(1)} %get-tuple-element.35.sorted_target, bf16[2,256,1024]{2,1,0:T(8,128)(2,1)S(1)} %copy-done.3, ...), custom_call_target="tpu_custom_call" | custom-call | tf_op jit(solution)/shard_map/root_halves/pallas_call | solution.py:255
  13.1 1.6 %collective-permute-start = (bf16[8,256,128]{2,1,0:T(8,128)(2,1)S(1)}, bf16[8,256,128]{2,1,0:T(8,128)(2,1)S(1)}, u32[]{:S(2)}, u32[]{:S(2)}) collective-permute-start(bf16[8,256,128]{2,1,0:T(8,128)(2,1)S(1)} %get-tuple-element.39), channel_id=1, source_target_pairs={{0,1},{1,0},{2,3},{3,2},{4,5},{5,4},{6,7},{7,6},{8,9},{9,8},{10,11... | collective-permute-start | bytes 1572872 | tf_op jit(solution)/shard_map/ppermute | solution.py:242
  15.9 10.2 %collective-permute-done.4.__0_ = bf16[12,16,1024]{2,1,0:T(8,128)(2,1)S(1)} collective-permute-done((bf16[12,16,1024]{2,1,0:T(8,128)(2,1)S(1)}, bf16[12,16,1024]{2,1,0:T(8,128)(2,1)S(1)}, u32[]{:S(2)}, u32[]{:S(2)}) %collective-permute-start.4) | collective-permute-done | bytes 393248 | tf_op jit(solution)/shard_map/ppermute | solution.py:239
  26.1 1.6 %roots_by_plane.1 = (bf16[8,256,128]{2,1,0:T(8,128)(2,1)S(1)}, bf16[8,256,128]{2,1,0:T(8,128)(2,1)S(1)}, bf16[8,256,128]{2,1,0:T(8,128)(2,1)}, bf16[8,256,128]{2,1,0:T(8,128)(2,1)S(1)}) custom-call(s32[8]{0:T(128)S(1)} %get-tuple-element.36.table, bf16[8,256,128]{2,1,0:T(8,128)(2,1)S(1)} %get-tuple-element.37.refs_0_, ...), custom_call_target="tpu_custom_call" | custom-call | tf_op jit(solution)/shard_map/roots_by_plane/pallas_call | solution.py:264
  27.6 1.8 %sum_and_place.1 = bf16[32,16,1024]{2,1,0:T(8,128)(2,1)} custom-call(s32[48]{0:T(128)S(1)} %get-tuple-element.35.sorted_target, bf16[8,256,128]{2,1,0:T(8,128)(2,1)S(1)} %get-tuple-element.49._.refs_0_, bf16[12,16,1024]{2,1,0:T(8,128)(2,1)S(1)} %get-tuple-element.42.own, bf16[12,16,1024]{2,1,0:T(8,128)(2,1)S(1)} %settle.5.one, ...), custom_call_target="tpu_custom_call" | custom-call | bytes 3145728 | tf_op jit(solution)/shard_map/sum_and_place/pallas_call | solution.py:273
  29.6 11.2 %all-to-all-start = ((bf16[32,16,1024]{2,1,0:T(8,128)(2,1)}), bf16[32,16,1024]{2,1,0:T(8,128)(2,1)S(1)}, u32[]{:S(2)}, u32[]{:S(2)}) async-start(bf16[32,16,1024]{2,1,0:T(8,128)(2,1)} %sum_and_place.1), calls=%async_computation | async-start | bytes 2097152 | tf_op jit(solution)/shard_map/all_to_all | solution.py:285
  40.8 1.2 %collective-permute-start.5 = (bf16[8,256,128]{2,1,0:T(8,128)(2,1)S(1)}, bf16[8,256,128]{2,1,0:T(8,128)(2,1)S(1)}, u32[]{:S(2)}, u32[]{:S(2)}) collective-permute-start(bf16[8,256,128]{2,1,0:T(8,128)(2,1)S(1)} %get-tuple-element.50), channel_id=1, source_target_pairs={{0,64},{64,128},{128,192},{192,0},{1,65},{65,129},{129,193},{193,1... | collective-permute-start | bytes 1572872 | tf_op jit(solution)/shard_map/ppermute | solution.py:239
  42.1 1.5 %collective-permute-start.7 = (bf16[8,256,128]{2,1,0:T(8,128)(2,1)S(1)}, bf16[8,256,128]{2,1,0:T(8,128)(2,1)S(1)}, u32[]{:S(2)}, u32[]{:S(2)}) collective-permute-start(bf16[8,256,128]{2,1,0:T(8,128)(2,1)S(1)} %get-tuple-element.52), channel_id=1, source_target_pairs={{0,192},{64,0},{128,64},{192,128},{1,193},{65,1},{129,65},{193,129... | collective-permute-start | bytes 1572872 | tf_op jit(solution)/shard_map/ppermute | solution.py:239
  43.6 10.2 %collective-permute-done.5.refs_1_ = bf16[8,256,128]{2,1,0:T(8,128)(2,1)S(1)} collective-permute-done((bf16[8,256,128]{2,1,0:T(8,128)(2,1)S(1)}, bf16[8,256,128]{2,1,0:T(8,128)(2,1)S(1)}, u32[]{:S(2)}, u32[]{:S(2)}) %collective-permute-start.5) | collective-permute-done | bytes 524320 | tf_op jit(solution)/shard_map/ppermute | solution.py:239
  55.1 2.9 %collective-permute-start.8 = (bf16[1024,512]{1,0:T(8,128)(2,1)S(1)}, bf16[1024,512]{1,0:T(8,128)(2,1)S(1)}, u32[]{:S(2)}, u32[]{:S(2)}) collective-permute-start(bf16[1024,512]{1,0:T(8,128)(2,1)S(1)} %get-tuple-element.53.l_own), channel_id=1, source_target_pairs={{0,1},{1,0},{2,3},{3,2},{4,5},{5,4},{6,7},{7,6},{8,9},{9,8},{10,11... | collective-permute-start | bytes 3145736 | tf_op jit(solution)/shard_map/ppermute | solution.py:242
  59.0 1.3 %collective-permute-done.8.__1_ = bf16[1024,512]{1,0:T(8,128)(2,1)S(1)} collective-permute-done((bf16[1024,512]{1,0:T(8,128)(2,1)S(1)}, bf16[1024,512]{1,0:T(8,128)(2,1)S(1)}, u32[]{:S(2)}, u32[]{:S(2)}) %collective-permute-start.8) | collective-permute-done | bytes 1048608 | tf_op jit(solution)/shard_map/ppermute | solution.py:242
  60.3 5.3 %all-to-all-done.__0_ = bf16[32,16,1024]{2,1,0:T(8,128)(2,1)S(1)} async-done(((bf16[32,16,1024]{2,1,0:T(8,128)(2,1)}), bf16[32,16,1024]{2,1,0:T(8,128)(2,1)S(1)}, u32[]{:S(2)}, u32[]{:S(2)}) %all-to-all-start) | async-done | bytes 1048608 | tf_op jit(solution)/shard_map/all_to_all | solution.py:285
  65.7 4.2 %collective-permute-start.9 = (bf16[32,16,1024]{2,1,0:T(8,128)(2,1)S(1)}, bf16[32,16,1024]{2,1,0:T(8,128)(2,1)S(1)}, u32[]{:S(2)}, u32[]{:S(2)}) collective-permute-start(bf16[32,16,1024]{2,1,0:T(8,128)(2,1)S(1)} %get-tuple-element.54.s_own), channel_id=1, source_target_pairs={{0,1},{1,0},{2,3},{3,2},{4,5},{5,4},{6,7},{7,6},{8,9},{9,8},{10,11... | collective-permute-start | bytes 3145736 | tf_op jit(solution)/shard_map/ppermute | solution.py:242
  69.8 2.3 %collective-permute-done.9.s_far = bf16[32,16,1024]{2,1,0:T(8,128)(2,1)S(1)} collective-permute-done((bf16[32,16,1024]{2,1,0:T(8,128)(2,1)S(1)}, bf16[32,16,1024]{2,1,0:T(8,128)(2,1)S(1)}, u32[]{:S(2)}, u32[]{:S(2)}) %collective-permute-start.9) | collective-permute-done | bytes 1048608 | tf_op jit(solution)/shard_map/ppermute | solution.py:242
  72.1 2.8 %gram.1 = (bf16[2,256,512]{2,1,0:T(8,128)(2,1)S(1)}, bf16[2,256,512]{2,1,0:T(8,128)(2,1)S(1)}, bf16[2,256,512]{2,1,0:T(8,128)(2,1)}, bf16[2,256,512]{2,1,0:T(8,128)(2,1)S(1)}, bf16[1024,1024]{1,0:T(8,128)(2,1)S(1)}) custom-call(bf16[32,16,1024]{2,1,0:T(8,128)(2,1)S(1)} %get-tuple-element.54.s_own, bf16[32,16,1024]{2,1,0:T(8,128)(2,1)S(1)} %collective-permute-done.9.s_far), custom_call_target="tpu_custom_call" | custom-call | flops 2147483648 | bytes 4194304 | tf_op jit(solution)/shard_map/gram/pallas_call | solution.py:302
  75.0 2.6 %collective-permute-start.10 = (bf16[2,256,512]{2,1,0:T(8,128)(2,1)}, bf16[2,256,512]{2,1,0:T(8,128)(2,1)S(1)}, u32[]{:S(2)}, u32[]{:S(2)}) collective-permute-start(bf16[2,256,512]{2,1,0:T(8,128)(2,1)} %get-tuple-element.55), channel_id=1, source_target_pairs={{0,128},{64,192},{128,0},{192,64},{1,129},{65,193},{129,1},{193,65... | collective-permute-start | bytes 1572872 | tf_op jit(solution)/shard_map/ppermute | solution.py:239
  77.6 3.4 %update_block.1 = bf16[4,64,16,128]{3,2,1,0:T(8,128)(2,1)} custom-call(bf16[1024,1024]{1,0:T(8,128)(2,1)S(1)} %get-tuple-element.64.block, bf16[1024,512]{1,0:T(8,128)(2,1)S(1)} %copy-done.6, bf16[1024,512]{1,0:T(8,128)(2,1)S(1)} %get-tuple-element.65.l_far, bf16[1024,512]{1,0:T(8,128)(2,1)S(1)} %copy-done.8), custom_call_target="tpu_custom_call" | custom-call | flops 2147483648 | bytes 6291456 | tf_op jit(solution)/shard_map/update_block/pallas_call | solution.py:312
  81.0 7.1 %all-to-all-start.1 = ((bf16[256,16,128]{2,1,0:T(8,128)(2,1)}), bf16[256,16,128]{2,1,0:T(8,128)(2,1)S(1)}, u32[]{:S(2)}, u32[]{:S(2)}) async-start(bf16[256,16,128]{2,1,0:T(8,128)(2,1)} %bitcast.1), calls=%async_computation.1 | async-start | bytes 2097152 | tf_op jit(solution)/shard_map/all_to_all | solution.py:323
  88.2 1.5 %collective-permute-start.11 = (bf16[2,256,512]{2,1,0:T(8,128)(2,1)S(1)}, bf16[2,256,512]{2,1,0:T(8,128)(2,1)S(1)}, u32[]{:S(2)}, u32[]{:S(2)}) collective-permute-start(bf16[2,256,512]{2,1,0:T(8,128)(2,1)S(1)} %copy-done.10), channel_id=1, source_target_pairs={{0,64},{64,128},{128,192},{192,0},{1,65},{65,129},{129,193},{193,1... | collective-permute-start | bytes 1572872 | tf_op jit(solution)/shard_map/ppermute | solution.py:239
  89.7 1.4 %collective-permute-start.12 = (bf16[2,256,512]{2,1,0:T(8,128)(2,1)S(1)}, bf16[2,256,512]{2,1,0:T(8,128)(2,1)S(1)}, u32[]{:S(2)}, u32[]{:S(2)}) collective-permute-start(bf16[2,256,512]{2,1,0:T(8,128)(2,1)S(1)} %get-tuple-element.60), channel_id=1, source_target_pairs={{0,192},{64,0},{128,64},{192,128},{1,193},{65,1},{129,65},{193,129... | collective-permute-start | bytes 1572872 | tf_op jit(solution)/shard_map/ppermute | solution.py:239
  91.0 2.6 %collective-permute-start.13 = (bf16[2,256,512]{2,1,0:T(8,128)(2,1)S(1)}, bf16[2,256,512]{2,1,0:T(8,128)(2,1)S(1)}, u32[]{:S(2)}, u32[]{:S(2)}) collective-permute-start(bf16[2,256,512]{2,1,0:T(8,128)(2,1)S(1)} %get-tuple-element.58.rest_0_), channel_id=1, source_target_pairs={{0,1},{1,0},{2,3},{3,2},{4,5},{5,4},{6,7},{7,6},{8,9},{9,8},{10,11... | collective-permute-start | bytes 1572872 | tf_op jit(solution)/shard_map/ppermute | solution.py:242
  93.8 15.9 %collective-permute-done.11.rest_1_ = bf16[2,256,512]{2,1,0:T(8,128)(2,1)S(1)} collective-permute-done((bf16[2,256,512]{2,1,0:T(8,128)(2,1)S(1)}, bf16[2,256,512]{2,1,0:T(8,128)(2,1)S(1)}, u32[]{:S(2)}, u32[]{:S(2)}) %collective-permute-start.11) | collective-permute-done | bytes 524320 | tf_op jit(solution)/shard_map/ppermute | solution.py:239
  109.7 2.7 %collective-permute-start.14 = (bf16[2,256,512]{2,1,0:T(8,128)(2,1)S(1)}, bf16[2,256,512]{2,1,0:T(8,128)(2,1)S(1)}, u32[]{:S(2)}, u32[]{:S(2)}) collective-permute-start(bf16[2,256,512]{2,1,0:T(8,128)(2,1)S(1)} %collective-permute-done.11.rest_1_), channel_id=1, source_target_pairs={{0,1},{1,0},{2,3},{3,2},{4,5},{5,4},{6,7},{7,6},{8,9},{9,8},{10,11... | collective-permute-start | bytes 1572872 | tf_op jit(solution)/shard_map/ppermute | solution.py:242
  114.6 3.1 %statistics.1 = (f32[2,256,1024]{2,1,0:T(8,128)}, f32[2,256,1024]{2,1,0:T(8,128)}) custom-call(s32[8]{0:T(128)S(1)} %get-tuple-element.36.table, f32[2,256,1024]{2,1,0:T(8,128)S(1)} %get-tuple-element.56.left, f32[2,256,1024]{2,1,0:T(8,128)S(1)} %get-tuple-element.57.right, bf16[2,256,512]{2,1,0:T(8,128)(2,1)S(1)} %get-tuple-element.58.rest_0_, ...), custom_call_target="tpu_custom_call" | custom-call | bytes 8388608 | tf_op jit(solution)/shard_map/statistics/pallas_call | solution.py:345
  117.7 1.6 %all-to-all-done.1 = bf16[256,16,128]{2,1,0:T(8,128)(2,1)S(1)} async-done(((bf16[256,16,128]{2,1,0:T(8,128)(2,1)}), bf16[256,16,128]{2,1,0:T(8,128)(2,1)S(1)}, u32[]{:S(2)}, u32[]{:S(2)}) %all-to-all-start.1) | async-done | bytes 1048608 | tf_op jit(solution)/shard_map/all_to_all | solution.py:323
  119.3 1.6 %pick.1 = bf16[48,16,256]{2,1,0:T(8,128)(2,1)} custom-call(s32[48]{0:T(128)S(1)} %get-tuple-element.63.order, s32[48]{0:T(128)S(1)} %get-tuple-element.35.sorted_target, bf16[4,32,2,16,128]{4,3,2,1,0:T(8,128)(2,1)S(1)} %bitcast.3), custom_call_target="tpu_custom_call" | custom-call | bytes 2097152 | tf_op jit(solution)/shard_map/pick/pallas_call | solution.py:324
  (46 shorter events, 7.0 us)
Async XLA Ops:
  1.5 1.4 %copy-start.2 = (bf16[1,48,16,1024]{3,2,1,0:T(8,128)(2,1)S(1)}, bf16[1,48,16,1024]{3,2,1,0:T(8,128)(2,1)}, u32[]{:S(2)}) copy-start(bf16[1,48,16,1024]{3,2,1,0:T(8,128)(2,1)} %param.7) | copy-start | bytes 4718596
  2.9 6.7 %copy-start.3 = (bf16[2,256,1024]{2,1,0:T(8,128)(2,1)S(1)}, bf16[2,256,1024]{2,1,0:T(8,128)(2,1)}, u32[]{:S(2)}) copy-start(bf16[2,256,1024]{2,1,0:T(8,128)(2,1)} %left.1) | copy-start | bytes 3145732
  4.3 10.5 %collective-permute-start.2 = (bf16[12,16,1024]{2,1,0:T(8,128)(2,1)S(1)}, bf16[12,16,1024]{2,1,0:T(8,128)(2,1)S(1)}, u32[]{:S(2)}, u32[]{:S(2)}) collective-permute-start(bf16[12,16,1024]{2,1,0:T(8,128)(2,1)S(1)} %get-tuple-element.43), channel_id=1, source_target_pairs={{0,64},{64,128},{128,192},{192,0},{1,65},{65,129},{129,193},{193,1... | collective-permute-start | bytes 1179656 | tf_op jit(solution)/shard_map/ppermute | solution.py:239
  6.5 9.4 %collective-permute-start.3 = (bf16[12,16,1024]{2,1,0:T(8,128)(2,1)S(1)}, bf16[12,16,1024]{2,1,0:T(8,128)(2,1)S(1)}, u32[]{:S(2)}, u32[]{:S(2)}) collective-permute-start(bf16[12,16,1024]{2,1,0:T(8,128)(2,1)S(1)} %get-tuple-element.44), channel_id=1, source_target_pairs={{0,192},{64,0},{128,64},{192,128},{1,193},{65,1},{129,65},{193,129... | collective-permute-start | bytes 1179656 | tf_op jit(solution)/shard_map/ppermute | solution.py:239
  8.0 18.0 %collective-permute-start.4 = (bf16[12,16,1024]{2,1,0:T(8,128)(2,1)S(1)}, bf16[12,16,1024]{2,1,0:T(8,128)(2,1)S(1)}, u32[]{:S(2)}, u32[]{:S(2)}) collective-permute-start(bf16[12,16,1024]{2,1,0:T(8,128)(2,1)S(1)} %get-tuple-element.45), channel_id=1, source_target_pairs={{0,128},{64,192},{128,0},{192,64},{1,129},{65,193},{129,1},{193,65... | collective-permute-start | bytes 1179656 | tf_op jit(solution)/shard_map/ppermute | solution.py:239
  9.6 1.2 %copy-start.4 = (bf16[2,1024,256]{2,1,0:T(8,128)(2,1)S(1)}, bf16[2,1024,256]{2,1,0:T(8,128)(2,1)}, u32[]{:S(2)}) copy-start(bf16[2,1024,256]{2,1,0:T(8,128)(2,1)} %right.1) | copy-start | bytes 3145732
  13.1 13.0 %collective-permute-start = (bf16[8,256,128]{2,1,0:T(8,128)(2,1)S(1)}, bf16[8,256,128]{2,1,0:T(8,128)(2,1)S(1)}, u32[]{:S(2)}, u32[]{:S(2)}) collective-permute-start(bf16[8,256,128]{2,1,0:T(8,128)(2,1)S(1)} %get-tuple-element.39), channel_id=1, source_target_pairs={{0,1},{1,0},{2,3},{3,2},{4,5},{5,4},{6,7},{7,6},{8,9},{9,8},{10,11... | collective-permute-start | bytes 1572872 | tf_op jit(solution)/shard_map/ppermute | solution.py:242
  14.7 11.4 %collective-permute-start.1 = (bf16[8,256,128]{2,1,0:T(8,128)(2,1)S(1)}, bf16[8,256,128]{2,1,0:T(8,128)(2,1)S(1)}, u32[]{:S(2)}, u32[]{:S(2)}) collective-permute-start(bf16[8,256,128]{2,1,0:T(8,128)(2,1)S(1)} %get-tuple-element.40), channel_id=1, source_target_pairs={{0,1},{1,0},{2,3},{3,2},{4,5},{5,4},{6,7},{7,6},{8,9},{9,8},{10,11... | collective-permute-start | bytes 1572872 | tf_op jit(solution)/shard_map/ppermute | solution.py:242
  29.4 14.2 %collective-permute-start.6 = (bf16[8,256,128]{2,1,0:T(8,128)(2,1)}, bf16[8,256,128]{2,1,0:T(8,128)(2,1)S(1)}, u32[]{:S(2)}, u32[]{:S(2)}) collective-permute-start(bf16[8,256,128]{2,1,0:T(8,128)(2,1)} %get-tuple-element.51), channel_id=1, source_target_pairs={{0,128},{64,192},{128,0},{192,64},{1,129},{65,193},{129,1},{193,65... | collective-permute-start | bytes 1572872 | tf_op jit(solution)/shard_map/ppermute | solution.py:239
  29.6 36.1 %all-to-all-start = ((bf16[32,16,1024]{2,1,0:T(8,128)(2,1)}), bf16[32,16,1024]{2,1,0:T(8,128)(2,1)S(1)}, u32[]{:S(2)}, u32[]{:S(2)}) async-start(bf16[32,16,1024]{2,1,0:T(8,128)(2,1)} %sum_and_place.1), calls=%async_computation | async-start | bytes 2097152 | tf_op jit(solution)/shard_map/all_to_all | solution.py:285
  40.8 12.9 %collective-permute-start.5 = (bf16[8,256,128]{2,1,0:T(8,128)(2,1)S(1)}, bf16[8,256,128]{2,1,0:T(8,128)(2,1)S(1)}, u32[]{:S(2)}, u32[]{:S(2)}) collective-permute-start(bf16[8,256,128]{2,1,0:T(8,128)(2,1)S(1)} %get-tuple-element.50), channel_id=1, source_target_pairs={{0,64},{64,128},{128,192},{192,0},{1,65},{65,129},{129,193},{193,1... | collective-permute-start | bytes 1572872 | tf_op jit(solution)/shard_map/ppermute | solution.py:239
  42.1 11.7 %collective-permute-start.7 = (bf16[8,256,128]{2,1,0:T(8,128)(2,1)S(1)}, bf16[8,256,128]{2,1,0:T(8,128)(2,1)S(1)}, u32[]{:S(2)}, u32[]{:S(2)}) collective-permute-start(bf16[8,256,128]{2,1,0:T(8,128)(2,1)S(1)} %get-tuple-element.52), channel_id=1, source_target_pairs={{0,192},{64,0},{128,64},{192,128},{1,193},{65,1},{129,65},{193,129... | collective-permute-start | bytes 1572872 | tf_op jit(solution)/shard_map/ppermute | solution.py:239
  54.2 1.0 copy-start.7
  55.1 5.2 %collective-permute-start.8 = (bf16[1024,512]{1,0:T(8,128)(2,1)S(1)}, bf16[1024,512]{1,0:T(8,128)(2,1)S(1)}, u32[]{:S(2)}, u32[]{:S(2)}) collective-permute-start(bf16[1024,512]{1,0:T(8,128)(2,1)S(1)} %get-tuple-element.53.l_own), channel_id=1, source_target_pairs={{0,1},{1,0},{2,3},{3,2},{4,5},{5,4},{6,7},{7,6},{8,9},{9,8},{10,11... | collective-permute-start | bytes 3145736 | tf_op jit(solution)/shard_map/ppermute | solution.py:242
  58.0 1.0 copy-start.5
  65.7 11.9 %copy-start.6 = (bf16[1024,512]{1,0:T(8,128)(2,1)S(1)}, bf16[1024,512]{1,0:T(8,128)(2,1)}, u32[]{:S(2)}) copy-start(bf16[1024,512]{1,0:T(8,128)(2,1)} %copy-done.5) | copy-start | bytes 3145732
  65.7 11.9 %copy-start.8 = (bf16[1024,512]{1,0:T(8,128)(2,1)S(1)}, bf16[1024,512]{1,0:T(8,128)(2,1)}, u32[]{:S(2)}) copy-start(bf16[1024,512]{1,0:T(8,128)(2,1)} %copy-done.7) | copy-start | bytes 3145732
  65.7 6.5 %collective-permute-start.9 = (bf16[32,16,1024]{2,1,0:T(8,128)(2,1)S(1)}, bf16[32,16,1024]{2,1,0:T(8,128)(2,1)S(1)}, u32[]{:S(2)}, u32[]{:S(2)}) collective-permute-start(bf16[32,16,1024]{2,1,0:T(8,128)(2,1)S(1)} %get-tuple-element.54.s_own), channel_id=1, source_target_pairs={{0,1},{1,0},{2,3},{3,2},{4,5},{5,4},{6,7},{7,6},{8,9},{9,8},{10,11... | collective-permute-start | bytes 3145736 | tf_op jit(solution)/shard_map/ppermute | solution.py:242
  75.0 6.1 %copy-start.9 = (bf16[2,256,512]{2,1,0:T(8,128)(2,1)}, bf16[2,256,512]{2,1,0:T(8,128)(2,1)S(1)}, u32[]{:S(2)}) copy-start(bf16[2,256,512]{2,1,0:T(8,128)(2,1)S(1)} %get-tuple-element.59) | copy-start | bytes 1572868
  75.0 18.7 %collective-permute-start.10 = (bf16[2,256,512]{2,1,0:T(8,128)(2,1)}, bf16[2,256,512]{2,1,0:T(8,128)(2,1)S(1)}, u32[]{:S(2)}, u32[]{:S(2)}) collective-permute-start(bf16[2,256,512]{2,1,0:T(8,128)(2,1)} %get-tuple-element.55), channel_id=1, source_target_pairs={{0,128},{64,192},{128,0},{192,64},{1,129},{65,193},{129,1},{193,65... | collective-permute-start | bytes 1572872 | tf_op jit(solution)/shard_map/ppermute | solution.py:239
  81.0 7.1 %copy-start.10 = (bf16[2,256,512]{2,1,0:T(8,128)(2,1)S(1)}, bf16[2,256,512]{2,1,0:T(8,128)(2,1)}, u32[]{:S(2)}) copy-start(bf16[2,256,512]{2,1,0:T(8,128)(2,1)} %copy-done.9) | copy-start | bytes 1572868
  81.0 38.2 %all-to-all-start.1 = ((bf16[256,16,128]{2,1,0:T(8,128)(2,1)}), bf16[256,16,128]{2,1,0:T(8,128)(2,1)S(1)}, u32[]{:S(2)}, u32[]{:S(2)}) async-start(bf16[256,16,128]{2,1,0:T(8,128)(2,1)} %bitcast.1), calls=%async_computation.1 | async-start | bytes 2097152 | tf_op jit(solution)/shard_map/all_to_all | solution.py:323
  88.2 21.5 %collective-permute-start.11 = (bf16[2,256,512]{2,1,0:T(8,128)(2,1)S(1)}, bf16[2,256,512]{2,1,0:T(8,128)(2,1)S(1)}, u32[]{:S(2)}, u32[]{:S(2)}) collective-permute-start(bf16[2,256,512]{2,1,0:T(8,128)(2,1)S(1)} %copy-done.10), channel_id=1, source_target_pairs={{0,64},{64,128},{128,192},{192,0},{1,65},{65,129},{129,193},{193,1... | collective-permute-start | bytes 1572872 | tf_op jit(solution)/shard_map/ppermute | solution.py:239
  89.7 22.7 %collective-permute-start.12 = (bf16[2,256,512]{2,1,0:T(8,128)(2,1)S(1)}, bf16[2,256,512]{2,1,0:T(8,128)(2,1)S(1)}, u32[]{:S(2)}, u32[]{:S(2)}) collective-permute-start(bf16[2,256,512]{2,1,0:T(8,128)(2,1)S(1)} %get-tuple-element.60), channel_id=1, source_target_pairs={{0,192},{64,0},{128,64},{192,128},{1,193},{65,1},{129,65},{193,129... | collective-permute-start | bytes 1572872 | tf_op jit(solution)/shard_map/ppermute | solution.py:239
  91.0 21.6 %copy-start = (f32[2,256,1024]{2,1,0:T(8,128)S(1)}, f32[2,256,1024]{2,1,0:T(8,128)}, u32[]{:S(2)}) copy-start(f32[2,256,1024]{2,1,0:T(8,128)} %stat_left.1) | copy-start | bytes 6291460
  91.0 21.6 %copy-start.1 = (f32[2,256,1024]{2,1,0:T(8,128)S(1)}, f32[2,256,1024]{2,1,0:T(8,128)}, u32[]{:S(2)}) copy-start(f32[2,256,1024]{2,1,0:T(8,128)} %stat_right.1) | copy-start | bytes 6291460
  91.0 21.9 %collective-permute-start.13 = (bf16[2,256,512]{2,1,0:T(8,128)(2,1)S(1)}, bf16[2,256,512]{2,1,0:T(8,128)(2,1)S(1)}, u32[]{:S(2)}, u32[]{:S(2)}) collective-permute-start(bf16[2,256,512]{2,1,0:T(8,128)(2,1)S(1)} %get-tuple-element.58.rest_0_), channel_id=1, source_target_pairs={{0,1},{1,0},{2,3},{3,2},{4,5},{5,4},{6,7},{7,6},{8,9},{9,8},{10,11... | collective-permute-start | bytes 1572872 | tf_op jit(solution)/shard_map/ppermute | solution.py:242
  93.7 19.3 %collective-permute-start.15 = (bf16[2,256,512]{2,1,0:T(8,128)(2,1)S(1)}, bf16[2,256,512]{2,1,0:T(8,128)(2,1)S(1)}, u32[]{:S(2)}, u32[]{:S(2)}) collective-permute-start(bf16[2,256,512]{2,1,0:T(8,128)(2,1)S(1)} %settle.9._.rest_2_), channel_id=1, source_target_pairs={{0,1},{1,0},{2,3},{3,2},{4,5},{5,4},{6,7},{7,6},{8,9},{9,8},{10,11... | collective-permute-start | bytes 1572872 | tf_op jit(solution)/shard_map/ppermute | solution.py:242
  109.7 4.2 %collective-permute-start.14 = (bf16[2,256,512]{2,1,0:T(8,128)(2,1)S(1)}, bf16[2,256,512]{2,1,0:T(8,128)(2,1)S(1)}, u32[]{:S(2)}, u32[]{:S(2)}) collective-permute-start(bf16[2,256,512]{2,1,0:T(8,128)(2,1)S(1)} %collective-permute-done.11.rest_1_), channel_id=1, source_target_pairs={{0,1},{1,0},{2,3},{3,2},{4,5},{5,4},{6,7},{7,6},{8,9},{9,8},{10,11... | collective-permute-start | bytes 1572872 | tf_op jit(solution)/shard_map/ppermute | solution.py:242
  112.3 2.3 %collective-permute-start.16 = (bf16[2,256,512]{2,1,0:T(8,128)(2,1)S(1)}, bf16[2,256,512]{2,1,0:T(8,128)(2,1)S(1)}, u32[]{:S(2)}, u32[]{:S(2)}) collective-permute-start(bf16[2,256,512]{2,1,0:T(8,128)(2,1)S(1)} %collective-permute-done.12.rest_3_), channel_id=1, source_target_pairs={{0,1},{1,0},{2,3},{3,2},{4,5},{5,4},{6,7},{7,6},{8,9},{9,8},{10,11... | collective-permute-start | bytes 1572872 | tf_op jit(solution)/shard_map/ppermute | solution.py:242

commit v5 on v4

--- a/solution.py
+++ b/solution.py
@@ -44,6 +44,10 @@
     return lax.axis_index("replica"), f // CORES, f % CORES
 
 
+def slots_of(owner, slot, target):
+    target[...] = owner[...] * SLOTS + slot[...]
+
+
 def by_plane(rank, target, g, sorted_target, order, *outs):
     count = g.shape[0]
     r, _, _ = my_place()
@@ -232,7 +236,15 @@
     blocks, rows, width = gradients.shape[1:]
     each = blocks // PLANES
     fsdp_count = lax.axis_size("fsdp")
-    target = block_owner * SLOTS + block_slot
+    target = call(
+        slots_of,
+        "slots_of",
+        like(block_owner.shape, jnp.int32),
+        [VMEM] * 2,
+        VMEM,
+        [],
+        flops=SUM_HINT,
+    )(block_owner, block_slot)
     rank = jnp.sum((target[None, :] < target[:, None]).astype(jnp.int32), axis=1)
 
     def along(x, step):

time: 121 us -> 120 us (level)
    ppermute x9, waiting for transfers between devices: 37.4 us -> 38.6 us  [along(): lax.ppermute(x, 'replica', [(i, (i + step) % PLANES) for i in range(PLANE...]
    unnamed x22 -> x26, local copies, waits for them, and re-layouts: 4.59 us -> 3.4 us
  transfers between devices with their start and end apart: 19 -> 19, of which waited for: 10 -> 11; matrix products, arithmetic and copies ran while one was open for 0% -> 0% of each run, Pallas kernels for 8% -> 8%
where the time goes in v5:
time: 120 us
  waiting for transfers between devices  50.8 us (42%)
  starting transfers between devices  46.5 us (39%)
  Pallas kernels  18.6 us (16%)
  local copies, waits for them, and re-layouts  3.4 us (3%)
    ppermute x9, waiting for transfers between devices, along(): lax.ppermute(x, 'replica', [(i, (i + step) % PLANES) for i in range(PLANE...  38.6 us
    ppermute x8, starting transfers between devices, across(): return lax.ppermute(x, 'fsdp', [(i, i ^ 1) for i in range(fsdp_count)])  14.5 us
    ppermute x9, starting transfers between devices, along(): lax.ppermute(x, 'replica', [(i, (i + step) % PLANES) for i in range(PLANE...  13.7 us
    all_to_all x1, starting transfers between devices, per_device(): lax.all_to_all(outgoing, 'fsdp', split_axis=0, concat_axis=0, tiled=True,...  11.2 us
    all_to_all x1, starting transfers between devices, per_device(): lax.all_to_all(update, ('replica', 'fsdp'), split_axis=0, concat_axis=0,...  7.12 us
    all_to_all x1, waiting for transfers between devices, per_device(): lax.all_to_all(outgoing, 'fsdp', split_axis=0, concat_axis=0, tiled=True,...  5.34 us
    ppermute x8, waiting for transfers between devices, across(): return lax.ppermute(x, 'fsdp', [(i, i ^ 1) for i in range(fsdp_count)])  5.27 us
    pallas_call x1, Pallas kernels, per_device(): call(update_block, 'update_block', like((PLANES, fsdp_count, rows, 128)),...  3.45 us
  transfers between devices with their start and end apart: 19, of which 11 were waited for; matrix products, arithmetic and copies ran while one was open for 0% of the time, Pallas kernels for 8%

profile of v5, /device:TPU:1, one launch (start us, length us, event | category | flops | bytes accessed | tf_op | source)
XLA Modules:
  0.0 120.2 jit_solution(2912650991853362551)
XLA Ops:
  2.3 1.4 %by_plane.1 = (s32[48]{0:T(128)S(1)}, s32[48]{0:T(128)S(1)}, bf16[12,16,1024]{2,1,0:T(8,128)(2,1)S(1)}, bf16[12,16,1024]{2,1,0:T(8,128)(2,1)S(1)}, bf16[12,16,10...) custom-call(s32[48]{0:T(128)S(1)} %convert_reduce_fusion.rank, s32[48]{0:T(128)S(1)} %slots_of.1.target, ...), custom_call_target="tpu_custom_call" | custom-call | bytes 3145728 | tf_op jit(solution)/shard_map/by_plane/pallas_call | solution.py:256
  3.7 2.2 %collective-permute-start.2 = (bf16[12,16,1024]{2,1,0:T(8,128)(2,1)S(1)}, bf16[12,16,1024]{2,1,0:T(8,128)(2,1)S(1)}, u32[]{:S(2)}, u32[]{:S(2)}) collective-permute-start(bf16[12,16,1024]{2,1,0:T(8,128)(2,1)S(1)} %get-tuple-element.43), channel_id=1, source_target_pairs={{0,64},{64,128},{128,192},{192,0},{1,65},{65,129},{129,193},{193,1... | collective-permute-start | bytes 1179656 | tf_op jit(solution)/shard_map/ppermute | solution.py:251
  5.9 1.5 %collective-permute-start.3 = (bf16[12,16,1024]{2,1,0:T(8,128)(2,1)S(1)}, bf16[12,16,1024]{2,1,0:T(8,128)(2,1)S(1)}, u32[]{:S(2)}, u32[]{:S(2)}) collective-permute-start(bf16[12,16,1024]{2,1,0:T(8,128)(2,1)S(1)} %get-tuple-element.44), channel_id=1, source_target_pairs={{0,192},{64,0},{128,64},{192,128},{1,193},{65,1},{129,65},{193,129... | collective-permute-start | bytes 1179656 | tf_op jit(solution)/shard_map/ppermute | solution.py:251
  7.4 1.6 %collective-permute-start.4 = (bf16[12,16,1024]{2,1,0:T(8,128)(2,1)S(1)}, bf16[12,16,1024]{2,1,0:T(8,128)(2,1)S(1)}, u32[]{:S(2)}, u32[]{:S(2)}) collective-permute-start(bf16[12,16,1024]{2,1,0:T(8,128)(2,1)S(1)} %get-tuple-element.45), channel_id=1, source_target_pairs={{0,128},{64,192},{128,0},{192,64},{1,129},{65,193},{129,1},{193,65... | collective-permute-start | bytes 1179656 | tf_op jit(solution)/shard_map/ppermute | solution.py:251
  9.0 2.2 %root_halves.1 = (bf16[8,256,128]{2,1,0:T(8,128)(2,1)S(1)}, bf16[8,256,128]{2,1,0:T(8,128)(2,1)S(1)}, bf16[8,256,128]{2,1,0:T(8,128)(2,1)S(1)}, bf16[8,256,128]{2,1,0:T(8,128)(2,1)S(1)}, s32[8]{0:T(128)S(1)}) custom-call(s32[48]{0:T(128)S(1)} %get-tuple-element.35.sorted_target, bf16[2,256,1024]{2,1,0:T(8,128)(2,1)S(1)} %copy-done.3, ...), custom_call_target="tpu_custom_call" | custom-call | tf_op jit(solution)/shard_map/root_halves/pallas_call | solution.py:267
  11.2 1.6 %collective-permute-start = (bf16[8,256,128]{2,1,0:T(8,128)(2,1)S(1)}, bf16[8,256,128]{2,1,0:T(8,128)(2,1)S(1)}, u32[]{:S(2)}, u32[]{:S(2)}) collective-permute-start(bf16[8,256,128]{2,1,0:T(8,128)(2,1)S(1)} %get-tuple-element.39), channel_id=1, source_target_pairs={{0,1},{1,0},{2,3},{3,2},{4,5},{5,4},{6,7},{7,6},{8,9},{9,8},{10,11... | collective-permute-start | bytes 1572872 | tf_op jit(solution)/shard_map/ppermute | solution.py:254
  12.9 1.2 collective-permute-done.2.__0_
  14.1 1.2 collective-permute-done.3.__0_
  15.3 10.2 %collective-permute-done.4.__0_ = bf16[12,16,1024]{2,1,0:T(8,128)(2,1)S(1)} collective-permute-done((bf16[12,16,1024]{2,1,0:T(8,128)(2,1)S(1)}, bf16[12,16,1024]{2,1,0:T(8,128)(2,1)S(1)}, u32[]{:S(2)}, u32[]{:S(2)}) %collective-permute-start.4) | collective-permute-done | bytes 393248 | tf_op jit(solution)/shard_map/ppermute | solution.py:251
  25.4 1.6 %roots_by_plane.1 = (bf16[8,256,128]{2,1,0:T(8,128)(2,1)S(1)}, bf16[8,256,128]{2,1,0:T(8,128)(2,1)S(1)}, bf16[8,256,128]{2,1,0:T(8,128)(2,1)}, bf16[8,256,128]{2,1,0:T(8,128)(2,1)S(1)}) custom-call(s32[8]{0:T(128)S(1)} %get-tuple-element.36.table, bf16[8,256,128]{2,1,0:T(8,128)(2,1)S(1)} %get-tuple-element.37.refs_0_, ...), custom_call_target="tpu_custom_call" | custom-call | tf_op jit(solution)/shard_map/roots_by_plane/pallas_call | solution.py:276
  27.0 1.8 %sum_and_place.1 = bf16[32,16,1024]{2,1,0:T(8,128)(2,1)} custom-call(s32[48]{0:T(128)S(1)} %get-tuple-element.35.sorted_target, bf16[8,256,128]{2,1,0:T(8,128)(2,1)S(1)} %get-tuple-element.49._.refs_0_, bf16[12,16,1024]{2,1,0:T(8,128)(2,1)S(1)} %get-tuple-element.42.own, bf16[12,16,1024]{2,1,0:T(8,128)(2,1)S(1)} %settle.5.one, ...), custom_call_target="tpu_custom_call" | custom-call | bytes 3145728 | tf_op jit(solution)/shard_map/sum_and_place/pallas_call | solution.py:285
  29.0 11.2 %all-to-all-start = ((bf16[32,16,1024]{2,1,0:T(8,128)(2,1)}), bf16[32,16,1024]{2,1,0:T(8,128)(2,1)S(1)}, u32[]{:S(2)}, u32[]{:S(2)}) async-start(bf16[32,16,1024]{2,1,0:T(8,128)(2,1)} %sum_and_place.1), calls=%async_computation | async-start | bytes 2097152 | tf_op jit(solution)/shard_map/all_to_all | solution.py:297
  40.2 1.2 %collective-permute-start.5 = (bf16[8,256,128]{2,1,0:T(8,128)(2,1)S(1)}, bf16[8,256,128]{2,1,0:T(8,128)(2,1)S(1)}, u32[]{:S(2)}, u32[]{:S(2)}) collective-permute-start(bf16[8,256,128]{2,1,0:T(8,128)(2,1)S(1)} %get-tuple-element.50), channel_id=1, source_target_pairs={{0,64},{64,128},{128,192},{192,0},{1,65},{65,129},{129,193},{193,1... | collective-permute-start | bytes 1572872 | tf_op jit(solution)/shard_map/ppermute | solution.py:251
  41.4 1.5 %collective-permute-start.7 = (bf16[8,256,128]{2,1,0:T(8,128)(2,1)S(1)}, bf16[8,256,128]{2,1,0:T(8,128)(2,1)S(1)}, u32[]{:S(2)}, u32[]{:S(2)}) collective-permute-start(bf16[8,256,128]{2,1,0:T(8,128)(2,1)S(1)} %get-tuple-element.52), channel_id=1, source_target_pairs={{0,192},{64,0},{128,64},{192,128},{1,193},{65,1},{129,65},{193,129... | collective-permute-start | bytes 1572872 | tf_op jit(solution)/shard_map/ppermute | solution.py:251
  43.0 10.2 %collective-permute-done.5.refs_1_ = bf16[8,256,128]{2,1,0:T(8,128)(2,1)S(1)} collective-permute-done((bf16[8,256,128]{2,1,0:T(8,128)(2,1)S(1)}, bf16[8,256,128]{2,1,0:T(8,128)(2,1)S(1)}, u32[]{:S(2)}, u32[]{:S(2)}) %collective-permute-start.5) | collective-permute-done | bytes 524320 | tf_op jit(solution)/shard_map/ppermute | solution.py:251
  54.5 2.9 %collective-permute-start.8 = (bf16[1024,512]{1,0:T(8,128)(2,1)S(1)}, bf16[1024,512]{1,0:T(8,128)(2,1)S(1)}, u32[]{:S(2)}, u32[]{:S(2)}) collective-permute-start(bf16[1024,512]{1,0:T(8,128)(2,1)S(1)} %get-tuple-element.53.l_own), channel_id=1, source_target_pairs={{0,1},{1,0},{2,3},{3,2},{4,5},{5,4},{6,7},{7,6},{8,9},{9,8},{10,11... | collective-permute-start | bytes 3145736 | tf_op jit(solution)/shard_map/ppermute | solution.py:254
  58.4 1.3 %collective-permute-done.8.__1_ = bf16[1024,512]{1,0:T(8,128)(2,1)S(1)} collective-permute-done((bf16[1024,512]{1,0:T(8,128)(2,1)S(1)}, bf16[1024,512]{1,0:T(8,128)(2,1)S(1)}, u32[]{:S(2)}, u32[]{:S(2)}) %collective-permute-start.8) | collective-permute-done | bytes 1048608 | tf_op jit(solution)/shard_map/ppermute | solution.py:254
  59.7 5.3 %all-to-all-done.__0_ = bf16[32,16,1024]{2,1,0:T(8,128)(2,1)S(1)} async-done(((bf16[32,16,1024]{2,1,0:T(8,128)(2,1)}), bf16[32,16,1024]{2,1,0:T(8,128)(2,1)S(1)}, u32[]{:S(2)}, u32[]{:S(2)}) %all-to-all-start) | async-done | bytes 1048608 | tf_op jit(solution)/shard_map/all_to_all | solution.py:297
  65.0 4.2 %collective-permute-start.9 = (bf16[32,16,1024]{2,1,0:T(8,128)(2,1)S(1)}, bf16[32,16,1024]{2,1,0:T(8,128)(2,1)S(1)}, u32[]{:S(2)}, u32[]{:S(2)}) collective-permute-start(bf16[32,16,1024]{2,1,0:T(8,128)(2,1)S(1)} %get-tuple-element.54.s_own), channel_id=1, source_target_pairs={{0,1},{1,0},{2,3},{3,2},{4,5},{5,4},{6,7},{7,6},{8,9},{9,8},{10,11... | collective-permute-start | bytes 3145736 | tf_op jit(solution)/shard_map/ppermute | solution.py:254
  69.2 2.3 %collective-permute-done.9.s_far = bf16[32,16,1024]{2,1,0:T(8,128)(2,1)S(1)} collective-permute-done((bf16[32,16,1024]{2,1,0:T(8,128)(2,1)S(1)}, bf16[32,16,1024]{2,1,0:T(8,128)(2,1)S(1)}, u32[]{:S(2)}, u32[]{:S(2)}) %collective-permute-start.9) | collective-permute-done | bytes 1048608 | tf_op jit(solution)/shard_map/ppermute | solution.py:254
  71.5 2.8 %gram.1 = (bf16[2,256,512]{2,1,0:T(8,128)(2,1)S(1)}, bf16[2,256,512]{2,1,0:T(8,128)(2,1)S(1)}, bf16[2,256,512]{2,1,0:T(8,128)(2,1)}, bf16[2,256,512]{2,1,0:T(8,128)(2,1)S(1)}, bf16[1024,1024]{1,0:T(8,128)(2,1)S(1)}) custom-call(bf16[32,16,1024]{2,1,0:T(8,128)(2,1)S(1)} %get-tuple-element.54.s_own, bf16[32,16,1024]{2,1,0:T(8,128)(2,1)S(1)} %collective-permute-done.9.s_far), custom_call_target="tpu_custom_call" | custom-call | flops 2147483648 | bytes 4194304 | tf_op jit(solution)/shard_map/gram/pallas_call | solution.py:314
  74.3 2.6 %collective-permute-start.10 = (bf16[2,256,512]{2,1,0:T(8,128)(2,1)}, bf16[2,256,512]{2,1,0:T(8,128)(2,1)S(1)}, u32[]{:S(2)}, u32[]{:S(2)}) collective-permute-start(bf16[2,256,512]{2,1,0:T(8,128)(2,1)} %get-tuple-element.55), channel_id=1, source_target_pairs={{0,128},{64,192},{128,0},{192,64},{1,129},{65,193},{129,1},{193,65... | collective-permute-start | bytes 1572872 | tf_op jit(solution)/shard_map/ppermute | solution.py:251
  77.0 3.5 %update_block.1 = bf16[4,64,16,128]{3,2,1,0:T(8,128)(2,1)} custom-call(bf16[1024,1024]{1,0:T(8,128)(2,1)S(1)} %get-tuple-element.64.block, bf16[1024,512]{1,0:T(8,128)(2,1)S(1)} %copy-done.6, bf16[1024,512]{1,0:T(8,128)(2,1)S(1)} %get-tuple-element.65.l_far, bf16[1024,512]{1,0:T(8,128)(2,1)S(1)} %copy-done.8), custom_call_target="tpu_custom_call" | custom-call | flops 2147483648 | bytes 6291456 | tf_op jit(solution)/shard_map/update_block/pallas_call | solution.py:324
  80.4 7.1 %all-to-all-start.1 = ((bf16[256,16,128]{2,1,0:T(8,128)(2,1)}), bf16[256,16,128]{2,1,0:T(8,128)(2,1)S(1)}, u32[]{:S(2)}, u32[]{:S(2)}) async-start(bf16[256,16,128]{2,1,0:T(8,128)(2,1)} %bitcast.1), calls=%async_computation.1 | async-start | bytes 2097152 | tf_op jit(solution)/shard_map/all_to_all | solution.py:335
  87.6 1.5 %collective-permute-start.11 = (bf16[2,256,512]{2,1,0:T(8,128)(2,1)S(1)}, bf16[2,256,512]{2,1,0:T(8,128)(2,1)S(1)}, u32[]{:S(2)}, u32[]{:S(2)}) collective-permute-start(bf16[2,256,512]{2,1,0:T(8,128)(2,1)S(1)} %copy-done.10), channel_id=1, source_target_pairs={{0,64},{64,128},{128,192},{192,0},{1,65},{65,129},{129,193},{193,1... | collective-permute-start | bytes 1572872 | tf_op jit(solution)/shard_map/ppermute | solution.py:251
  89.0 1.4 %collective-permute-start.12 = (bf16[2,256,512]{2,1,0:T(8,128)(2,1)S(1)}, bf16[2,256,512]{2,1,0:T(8,128)(2,1)S(1)}, u32[]{:S(2)}, u32[]{:S(2)}) collective-permute-start(bf16[2,256,512]{2,1,0:T(8,128)(2,1)S(1)} %get-tuple-element.60), channel_id=1, source_target_pairs={{0,192},{64,0},{128,64},{192,128},{1,193},{65,1},{129,65},{193,129... | collective-permute-start | bytes 1572872 | tf_op jit(solution)/shard_map/ppermute | solution.py:251
  90.4 2.6 %collective-permute-start.13 = (bf16[2,256,512]{2,1,0:T(8,128)(2,1)S(1)}, bf16[2,256,512]{2,1,0:T(8,128)(2,1)S(1)}, u32[]{:S(2)}, u32[]{:S(2)}) collective-permute-start(bf16[2,256,512]{2,1,0:T(8,128)(2,1)S(1)} %get-tuple-element.58.rest_0_), channel_id=1, source_target_pairs={{0,1},{1,0},{2,3},{3,2},{4,5},{5,4},{6,7},{7,6},{8,9},{9,8},{10,11... | collective-permute-start | bytes 1572872 | tf_op jit(solution)/shard_map/ppermute | solution.py:254
  93.1 15.9 %collective-permute-done.11.rest_1_ = bf16[2,256,512]{2,1,0:T(8,128)(2,1)S(1)} collective-permute-done((bf16[2,256,512]{2,1,0:T(8,128)(2,1)S(1)}, bf16[2,256,512]{2,1,0:T(8,128)(2,1)S(1)}, u32[]{:S(2)}, u32[]{:S(2)}) %collective-permute-start.11) | collective-permute-done | bytes 524320 | tf_op jit(solution)/shard_map/ppermute | solution.py:251
  109.0 2.7 %collective-permute-start.14 = (bf16[2,256,512]{2,1,0:T(8,128)(2,1)S(1)}, bf16[2,256,512]{2,1,0:T(8,128)(2,1)S(1)}, u32[]{:S(2)}, u32[]{:S(2)}) collective-permute-start(bf16[2,256,512]{2,1,0:T(8,128)(2,1)S(1)} %collective-permute-done.11.rest_1_), channel_id=1, source_target_pairs={{0,1},{1,0},{2,3},{3,2},{4,5},{5,4},{6,7},{7,6},{8,9},{9,8},{10,11... | collective-permute-start | bytes 1572872 | tf_op jit(solution)/shard_map/ppermute | solution.py:254
  114.0 3.1 %statistics.1 = (f32[2,256,1024]{2,1,0:T(8,128)}, f32[2,256,1024]{2,1,0:T(8,128)}) custom-call(s32[8]{0:T(128)S(1)} %get-tuple-element.36.table, f32[2,256,1024]{2,1,0:T(8,128)S(1)} %get-tuple-element.56.left, f32[2,256,1024]{2,1,0:T(8,128)S(1)} %get-tuple-element.57.right, bf16[2,256,512]{2,1,0:T(8,128)(2,1)S(1)} %get-tuple-element.58.rest_0_, ...), custom_call_target="tpu_custom_call" | custom-call | bytes 8388608 | tf_op jit(solution)/shard_map/statistics/pallas_call | solution.py:357
  117.1 1.6 %all-to-all-done.1 = bf16[256,16,128]{2,1,0:T(8,128)(2,1)S(1)} async-done(((bf16[256,16,128]{2,1,0:T(8,128)(2,1)}), bf16[256,16,128]{2,1,0:T(8,128)(2,1)S(1)}, u32[]{:S(2)}, u32[]{:S(2)}) %all-to-all-start.1) | async-done | bytes 1048608 | tf_op jit(solution)/shard_map/all_to_all | solution.py:335
  118.6 1.6 %pick.1 = bf16[48,16,256]{2,1,0:T(8,128)(2,1)} custom-call(s32[48]{0:T(128)S(1)} %get-tuple-element.63.order, s32[48]{0:T(128)S(1)} %get-tuple-element.35.sorted_target, bf16[4,32,2,16,128]{4,3,2,1,0:T(8,128)(2,1)S(1)} %bitcast.3), custom_call_target="tpu_custom_call" | custom-call | bytes 2097152 | tf_op jit(solution)/shard_map/pick/pallas_call | solution.py:336
  (50 shorter events, 6.6 us)
Async XLA Ops:
  0.6 1.6 %copy-start.2 = (bf16[1,48,16,1024]{3,2,1,0:T(8,128)(2,1)S(1)}, bf16[1,48,16,1024]{3,2,1,0:T(8,128)(2,1)}, u32[]{:S(2)}) copy-start(bf16[1,48,16,1024]{3,2,1,0:T(8,128)(2,1)} %param.7) | copy-start | bytes 4718596
  0.6 0.8 copy-start.11
  1.4 0.7 copy-start.12
  2.1 6.9 %copy-start.4 = (bf16[2,1024,256]{2,1,0:T(8,128)(2,1)S(1)}, bf16[2,1024,256]{2,1,0:T(8,128)(2,1)}, u32[]{:S(2)}) copy-start(bf16[2,1024,256]{2,1,0:T(8,128)(2,1)} %right.1) | copy-start | bytes 3145732
  2.1 6.9 %copy-start.3 = (bf16[2,256,1024]{2,1,0:T(8,128)(2,1)S(1)}, bf16[2,256,1024]{2,1,0:T(8,128)(2,1)}, u32[]{:S(2)}) copy-start(bf16[2,256,1024]{2,1,0:T(8,128)(2,1)} %left.1) | copy-start | bytes 3145732
  3.7 10.4 %collective-permute-start.2 = (bf16[12,16,1024]{2,1,0:T(8,128)(2,1)S(1)}, bf16[12,16,1024]{2,1,0:T(8,128)(2,1)S(1)}, u32[]{:S(2)}, u32[]{:S(2)}) collective-permute-start(bf16[12,16,1024]{2,1,0:T(8,128)(2,1)S(1)} %get-tuple-element.43), channel_id=1, source_target_pairs={{0,64},{64,128},{128,192},{192,0},{1,65},{65,129},{129,193},{193,1... | collective-permute-start | bytes 1179656 | tf_op jit(solution)/shard_map/ppermute | solution.py:251
  5.9 9.4 %collective-permute-start.3 = (bf16[12,16,1024]{2,1,0:T(8,128)(2,1)S(1)}, bf16[12,16,1024]{2,1,0:T(8,128)(2,1)S(1)}, u32[]{:S(2)}, u32[]{:S(2)}) collective-permute-start(bf16[12,16,1024]{2,1,0:T(8,128)(2,1)S(1)} %get-tuple-element.44), channel_id=1, source_target_pairs={{0,192},{64,0},{128,64},{192,128},{1,193},{65,1},{129,65},{193,129... | collective-permute-start | bytes 1179656 | tf_op jit(solution)/shard_map/ppermute | solution.py:251
  7.4 18.0 %collective-permute-start.4 = (bf16[12,16,1024]{2,1,0:T(8,128)(2,1)S(1)}, bf16[12,16,1024]{2,1,0:T(8,128)(2,1)S(1)}, u32[]{:S(2)}, u32[]{:S(2)}) collective-permute-start(bf16[12,16,1024]{2,1,0:T(8,128)(2,1)S(1)} %get-tuple-element.45), channel_id=1, source_target_pairs={{0,128},{64,192},{128,0},{192,64},{1,129},{65,193},{129,1},{193,65... | collective-permute-start | bytes 1179656 | tf_op jit(solution)/shard_map/ppermute | solution.py:251
  11.2 14.2 %collective-permute-start = (bf16[8,256,128]{2,1,0:T(8,128)(2,1)S(1)}, bf16[8,256,128]{2,1,0:T(8,128)(2,1)S(1)}, u32[]{:S(2)}, u32[]{:S(2)}) collective-permute-start(bf16[8,256,128]{2,1,0:T(8,128)(2,1)S(1)} %get-tuple-element.39), channel_id=1, source_target_pairs={{0,1},{1,0},{2,3},{3,2},{4,5},{5,4},{6,7},{7,6},{8,9},{9,8},{10,11... | collective-permute-start | bytes 1572872 | tf_op jit(solution)/shard_map/ppermute | solution.py:254
  12.8 12.6 %collective-permute-start.1 = (bf16[8,256,128]{2,1,0:T(8,128)(2,1)S(1)}, bf16[8,256,128]{2,1,0:T(8,128)(2,1)S(1)}, u32[]{:S(2)}, u32[]{:S(2)}) collective-permute-start(bf16[8,256,128]{2,1,0:T(8,128)(2,1)S(1)} %get-tuple-element.40), channel_id=1, source_target_pairs={{0,1},{1,0},{2,3},{3,2},{4,5},{5,4},{6,7},{7,6},{8,9},{9,8},{10,11... | collective-permute-start | bytes 1572872 | tf_op jit(solution)/shard_map/ppermute | solution.py:254
  28.8 14.2 %collective-permute-start.6 = (bf16[8,256,128]{2,1,0:T(8,128)(2,1)}, bf16[8,256,128]{2,1,0:T(8,128)(2,1)S(1)}, u32[]{:S(2)}, u32[]{:S(2)}) collective-permute-start(bf16[8,256,128]{2,1,0:T(8,128)(2,1)} %get-tuple-element.51), channel_id=1, source_target_pairs={{0,128},{64,192},{128,0},{192,64},{1,129},{65,193},{129,1},{193,65... | collective-permute-start | bytes 1572872 | tf_op jit(solution)/shard_map/ppermute | solution.py:251
  29.0 36.1 %all-to-all-start = ((bf16[32,16,1024]{2,1,0:T(8,128)(2,1)}), bf16[32,16,1024]{2,1,0:T(8,128)(2,1)S(1)}, u32[]{:S(2)}, u32[]{:S(2)}) async-start(bf16[32,16,1024]{2,1,0:T(8,128)(2,1)} %sum_and_place.1), calls=%async_computation | async-start | bytes 2097152 | tf_op jit(solution)/shard_map/all_to_all | solution.py:297
  40.2 12.9 %collective-permute-start.5 = (bf16[8,256,128]{2,1,0:T(8,128)(2,1)S(1)}, bf16[8,256,128]{2,1,0:T(8,128)(2,1)S(1)}, u32[]{:S(2)}, u32[]{:S(2)}) collective-permute-start(bf16[8,256,128]{2,1,0:T(8,128)(2,1)S(1)} %get-tuple-element.50), channel_id=1, source_target_pairs={{0,64},{64,128},{128,192},{192,0},{1,65},{65,129},{129,193},{193,1... | collective-permute-start | bytes 1572872 | tf_op jit(solution)/shard_map/ppermute | solution.py:251
  41.4 11.7 %collective-permute-start.7 = (bf16[8,256,128]{2,1,0:T(8,128)(2,1)S(1)}, bf16[8,256,128]{2,1,0:T(8,128)(2,1)S(1)}, u32[]{:S(2)}, u32[]{:S(2)}) collective-permute-start(bf16[8,256,128]{2,1,0:T(8,128)(2,1)S(1)} %get-tuple-element.52), channel_id=1, source_target_pairs={{0,192},{64,0},{128,64},{192,128},{1,193},{65,1},{129,65},{193,129... | collective-permute-start | bytes 1572872 | tf_op jit(solution)/shard_map/ppermute | solution.py:251
  53.5 1.0 copy-start.7
  54.5 5.2 %collective-permute-start.8 = (bf16[1024,512]{1,0:T(8,128)(2,1)S(1)}, bf16[1024,512]{1,0:T(8,128)(2,1)S(1)}, u32[]{:S(2)}, u32[]{:S(2)}) collective-permute-start(bf16[1024,512]{1,0:T(8,128)(2,1)S(1)} %get-tuple-element.53.l_own), channel_id=1, source_target_pairs={{0,1},{1,0},{2,3},{3,2},{4,5},{5,4},{6,7},{7,6},{8,9},{9,8},{10,11... | collective-permute-start | bytes 3145736 | tf_op jit(solution)/shard_map/ppermute | solution.py:254
  57.4 1.0 copy-start.5
  65.0 11.9 %copy-start.6 = (bf16[1024,512]{1,0:T(8,128)(2,1)S(1)}, bf16[1024,512]{1,0:T(8,128)(2,1)}, u32[]{:S(2)}) copy-start(bf16[1024,512]{1,0:T(8,128)(2,1)} %copy-done.5) | copy-start | bytes 3145732
  65.0 11.9 %copy-start.8 = (bf16[1024,512]{1,0:T(8,128)(2,1)S(1)}, bf16[1024,512]{1,0:T(8,128)(2,1)}, u32[]{:S(2)}) copy-start(bf16[1024,512]{1,0:T(8,128)(2,1)} %copy-done.7) | copy-start | bytes 3145732
  65.0 6.5 %collective-permute-start.9 = (bf16[32,16,1024]{2,1,0:T(8,128)(2,1)S(1)}, bf16[32,16,1024]{2,1,0:T(8,128)(2,1)S(1)}, u32[]{:S(2)}, u32[]{:S(2)}) collective-permute-start(bf16[32,16,1024]{2,1,0:T(8,128)(2,1)S(1)} %get-tuple-element.54.s_own), channel_id=1, source_target_pairs={{0,1},{1,0},{2,3},{3,2},{4,5},{5,4},{6,7},{7,6},{8,9},{9,8},{10,11... | collective-permute-start | bytes 3145736 | tf_op jit(solution)/shard_map/ppermute | solution.py:254
  74.3 6.1 %copy-start.9 = (bf16[2,256,512]{2,1,0:T(8,128)(2,1)}, bf16[2,256,512]{2,1,0:T(8,128)(2,1)S(1)}, u32[]{:S(2)}) copy-start(bf16[2,256,512]{2,1,0:T(8,128)(2,1)S(1)} %get-tuple-element.59) | copy-start | bytes 1572868
  74.3 18.7 %collective-permute-start.10 = (bf16[2,256,512]{2,1,0:T(8,128)(2,1)}, bf16[2,256,512]{2,1,0:T(8,128)(2,1)S(1)}, u32[]{:S(2)}, u32[]{:S(2)}) collective-permute-start(bf16[2,256,512]{2,1,0:T(8,128)(2,1)} %get-tuple-element.55), channel_id=1, source_target_pairs={{0,128},{64,192},{128,0},{192,64},{1,129},{65,193},{129,1},{193,65... | collective-permute-start | bytes 1572872 | tf_op jit(solution)/shard_map/ppermute | solution.py:251
  80.4 7.1 %copy-start.10 = (bf16[2,256,512]{2,1,0:T(8,128)(2,1)S(1)}, bf16[2,256,512]{2,1,0:T(8,128)(2,1)}, u32[]{:S(2)}) copy-start(bf16[2,256,512]{2,1,0:T(8,128)(2,1)} %copy-done.9) | copy-start | bytes 1572868
  80.4 38.2 %all-to-all-start.1 = ((bf16[256,16,128]{2,1,0:T(8,128)(2,1)}), bf16[256,16,128]{2,1,0:T(8,128)(2,1)S(1)}, u32[]{:S(2)}, u32[]{:S(2)}) async-start(bf16[256,16,128]{2,1,0:T(8,128)(2,1)} %bitcast.1), calls=%async_computation.1 | async-start | bytes 2097152 | tf_op jit(solution)/shard_map/all_to_all | solution.py:335
  87.6 21.5 %collective-permute-start.11 = (bf16[2,256,512]{2,1,0:T(8,128)(2,1)S(1)}, bf16[2,256,512]{2,1,0:T(8,128)(2,1)S(1)}, u32[]{:S(2)}, u32[]{:S(2)}) collective-permute-start(bf16[2,256,512]{2,1,0:T(8,128)(2,1)S(1)} %copy-done.10), channel_id=1, source_target_pairs={{0,64},{64,128},{128,192},{192,0},{1,65},{65,129},{129,193},{193,1... | collective-permute-start | bytes 1572872 | tf_op jit(solution)/shard_map/ppermute | solution.py:251
  89.0 22.7 %collective-permute-start.12 = (bf16[2,256,512]{2,1,0:T(8,128)(2,1)S(1)}, bf16[2,256,512]{2,1,0:T(8,128)(2,1)S(1)}, u32[]{:S(2)}, u32[]{:S(2)}) collective-permute-start(bf16[2,256,512]{2,1,0:T(8,128)(2,1)S(1)} %get-tuple-element.60), channel_id=1, source_target_pairs={{0,192},{64,0},{128,64},{192,128},{1,193},{65,1},{129,65},{193,129... | collective-permute-start | bytes 1572872 | tf_op jit(solution)/shard_map/ppermute | solution.py:251
  90.4 21.6 %copy-start = (f32[2,256,1024]{2,1,0:T(8,128)S(1)}, f32[2,256,1024]{2,1,0:T(8,128)}, u32[]{:S(2)}) copy-start(f32[2,256,1024]{2,1,0:T(8,128)} %stat_left.1) | copy-start | bytes 6291460
  90.4 21.6 %copy-start.1 = (f32[2,256,1024]{2,1,0:T(8,128)S(1)}, f32[2,256,1024]{2,1,0:T(8,128)}, u32[]{:S(2)}) copy-start(f32[2,256,1024]{2,1,0:T(8,128)} %stat_right.1) | copy-start | bytes 6291460
  90.4 21.9 %collective-permute-start.13 = (bf16[2,256,512]{2,1,0:T(8,128)(2,1)S(1)}, bf16[2,256,512]{2,1,0:T(8,128)(2,1)S(1)}, u32[]{:S(2)}, u32[]{:S(2)}) collective-permute-start(bf16[2,256,512]{2,1,0:T(8,128)(2,1)S(1)} %get-tuple-element.58.rest_0_), channel_id=1, source_target_pairs={{0,1},{1,0},{2,3},{3,2},{4,5},{5,4},{6,7},{7,6},{8,9},{9,8},{10,11... | collective-permute-start | bytes 1572872 | tf_op jit(solution)/shard_map/ppermute | solution.py:254
  93.0 19.3 %collective-permute-start.15 = (bf16[2,256,512]{2,1,0:T(8,128)(2,1)S(1)}, bf16[2,256,512]{2,1,0:T(8,128)(2,1)S(1)}, u32[]{:S(2)}, u32[]{:S(2)}) collective-permute-start(bf16[2,256,512]{2,1,0:T(8,128)(2,1)S(1)} %settle.9._.rest_2_), channel_id=1, source_target_pairs={{0,1},{1,0},{2,3},{3,2},{4,5},{5,4},{6,7},{7,6},{8,9},{9,8},{10,11... | collective-permute-start | bytes 1572872 | tf_op jit(solution)/shard_map/ppermute | solution.py:254
  109.0 4.2 %collective-permute-start.14 = (bf16[2,256,512]{2,1,0:T(8,128)(2,1)S(1)}, bf16[2,256,512]{2,1,0:T(8,128)(2,1)S(1)}, u32[]{:S(2)}, u32[]{:S(2)}) collective-permute-start(bf16[2,256,512]{2,1,0:T(8,128)(2,1)S(1)} %collective-permute-done.11.rest_1_), channel_id=1, source_target_pairs={{0,1},{1,0},{2,3},{3,2},{4,5},{5,4},{6,7},{7,6},{8,9},{9,8},{10,11... | collective-permute-start | bytes 1572872 | tf_op jit(solution)/shard_map/ppermute | solution.py:254
  111.7 2.3 %collective-permute-start.16 = (bf16[2,256,512]{2,1,0:T(8,128)(2,1)S(1)}, bf16[2,256,512]{2,1,0:T(8,128)(2,1)S(1)}, u32[]{:S(2)}, u32[]{:S(2)}) collective-permute-start(bf16[2,256,512]{2,1,0:T(8,128)(2,1)S(1)} %collective-permute-done.12.rest_3_), channel_id=1, source_target_pairs={{0,1},{1,0},{2,3},{3,2},{4,5},{5,4},{6,7},{7,6},{8,9},{9,8},{10,11... | collective-permute-start | bytes 1572872 | tf_op jit(solution)/shard_map/ppermute | solution.py:254
